TPU v7x, 32 devices: a whole 2x2x4 slice. The times are simulated.
32 devices in a mesh: atom: 8 (over z, x), energy: 4 (over y, core).
Axes of the slice: x: 2, y: 2, z: 4, core: 2. Of those that a mesh axis runs over, the one named last changes fastest.
Arguments:
- bare_green: bfloat16 [2, 12, 12, 32, 512], P(None, None, None, 'atom', 'energy'), may hold values from -6 to 6
- coupling_grad: bfloat16 [8, 12, 12, 32], P(None, None, None, 'atom'), may hold values from -1.75 to 1.75
- neighbours: int32 [32, 8], P('atom'), may hold values from 0 to 31, as said below
- shifts: int32 [32], replicated, may hold values from 1 to 4
- strength: float32 [32], replicated, may hold values from 5e-05 to 0.0005
- occupation: float32 [32], replicated, may hold values from 0.1 to 4
Outputs:
- green: bfloat16 [2, 12, 12, 32, 512], P(None, None, None, 'atom', 'energy')
Inputs may be any that keep to these rules, and one draw needn't show every extreme that they name: Each atom's 8 neighbours differ from it by 1 to 4 in index (not necessarily distinct); in every row one lies exactly 4 away.
All inputs are finite; a program needn't handle non-finite values.
Results may differ from a plain program's by a relative error of at most 0.0071.
Values may be sent and summed in bfloat16 or wider, within the bound.
No kernel may reach another device: no remote copies, remote signals or barrier semaphores. Data moves between devices by JAX's collectives and lax.ppermute only.
A program may use at most 64 MiB of HBM per device.

v0:
```python
import jax
import jax.numpy as jnp
from jax import lax
from jax.sharding import PartitionSpec as P

WIDTH = 4


def padded(block, sides, width):
    for axis, dim in sides:
        count = lax.axis_size(axis)
        forward = [(i, i + 1) for i in range(count - 1)]
        backward = [(target, source) for source, target in forward]
        low = lax.ppermute(
            lax.slice_in_dim(block, block.shape[dim] - width, None, axis=dim), axis, forward
        )
        high = lax.ppermute(lax.slice_in_dim(block, 0, width, axis=dim), axis, backward)
        block = jnp.concatenate([low, block, high], axis=dim)
    return block


def coefficients(shifts, strength, occupation):
    offsets = jnp.arange(2 * WIDTH + 1, dtype=jnp.int32) - WIDTH
    lower_hit = offsets[:, None] == -shifts[None, :]
    upper_hit = offsets[:, None] == shifts[None, :]
    weights = jnp.where(lower_hit, (strength * occupation)[None, :], jnp.zeros((), jnp.float32))
    weights = weights + jnp.where(
        upper_hit, (strength * (occupation + 1.0))[None, :], jnp.zeros((), jnp.float32)
    )
    return jnp.sum(weights, axis=1).astype(jnp.bfloat16)


def band_matrix(offset_weights, energy_count):
    row_index = jnp.arange(energy_count + 2 * WIDTH, dtype=jnp.int32)[:, None]
    col_index = jnp.arange(energy_count, dtype=jnp.int32)[None, :]
    gap_index = row_index - col_index - WIDTH
    offsets = jnp.arange(2 * WIDTH + 1, dtype=jnp.int32) - WIDTH
    pick_mask = gap_index[None, :, :] == offsets[:, None, None]
    table = jnp.where(
        pick_mask, offset_weights.astype(jnp.float32)[:, None, None], jnp.zeros((), jnp.float32)
    )
    return jnp.sum(table, axis=0).astype(jnp.bfloat16)


def complex_product(factor_left, factor_right):
    real_part = jnp.einsum(
        "ikae,kjae->ijae", factor_left[0], factor_right[0], preferred_element_type=jnp.float32
    )
    real_part = real_part - jnp.einsum(
        "ikae,kjae->ijae", factor_left[1], factor_right[1], preferred_element_type=jnp.float32
    )
    imag_part = jnp.einsum(
        "ikae,kjae->ijae", factor_left[0], factor_right[1], preferred_element_type=jnp.float32
    )
    imag_part = imag_part + jnp.einsum(
        "ikae,kjae->ijae", factor_left[1], factor_right[0], preferred_element_type=jnp.float32
    )
    return jnp.stack([real_part, imag_part])


def convolve(extended, band_table):
    energy_count = band_table.shape[1]
    flat_rows = extended.reshape(-1, extended.shape[4])
    summed = jnp.dot(flat_rows, band_table, preferred_element_type=jnp.float32).astype(jnp.bfloat16)
    return summed.reshape(
        extended.shape[0], extended.shape[1], extended.shape[2], extended.shape[3], energy_count
    )


def sandwich(phonon_sum, index_row, grad_atom):
    picked = jnp.take(phonon_sum, index_row, axis=3)
    half_product = jnp.einsum(
        "nik,rklne->rilne", grad_atom, picked, preferred_element_type=jnp.float32
    ).astype(jnp.bfloat16)
    return jnp.einsum(
        "rilne,njl->rije", half_product, grad_atom, preferred_element_type=jnp.float32
    )


def per_device(bare_green, coupling_grad, neighbours, shifts, strength, occupation):
    atoms_here = bare_green.shape[3]
    energies_here = bare_green.shape[4]
    offset_weights = coefficients(shifts, strength, occupation)
    band_table = band_matrix(offset_weights, energies_here)
    local_index = neighbours - lax.axis_index("atom") * atoms_here + WIDTH
    bond_grads = jnp.moveaxis(coupling_grad, 3, 0)
    green_now = bare_green
    tall_block = padded(green_now, (("energy", 4),), WIDTH)
    narrow = convolve(tall_block, band_table)
    phonon_sum = padded(narrow, (("atom", 3),), WIDTH)

    def per_atom(atom_item):
        return sandwich(phonon_sum, atom_item[0], atom_item[1])

    self_energy = lax.map(per_atom, (local_index, bond_grads))
    self_energy = jnp.moveaxis(self_energy, 0, 3).astype(jnp.bfloat16)
    left_product = complex_product(bare_green, self_energy).astype(jnp.bfloat16)
    green_now = (bare_green.astype(jnp.float32) + complex_product(left_product, bare_green)).astype(
        jnp.bfloat16
    )
    return green_now


def solution(mesh):
    placed = (
        P(None, None, None, "atom", "energy"),
        P(None, None, None, "atom"),
        P("atom", None),
        P(),
        P(),
        P(),
    )
    return jax.shard_map(
        per_device,
        mesh=mesh,
        in_specs=placed,
        out_specs=P(None, None, None, "atom", "energy"),
        check_vma=False,
    )
```

profile of v0, /device:TPU:0, one launch (start us, length us, event | category | flops | bytes accessed | tf_op | source)
XLA Modules:
  0.0 84.9 jit_solution(9908697919064452499)
XLA Ops:
  0.0 1.3 %fusion.31 = (bf16[2,12,12,4,4]{4,3,2,1,0:T(4,128)(2,1)S(1)}, bf16[2,12,12,4,4]{4,3,2,1,0:T(4,128)(2,1)S(1)}) fusion(bf16[2,12,12,4,128]{4,3,2,1,0:T(4,128)(2,1)} %param.8), kind=kLoop, calls=%fused_computation.58 | loop fusion | bytes 36864 | tf_op jit(solution)/shard_map/slice | solution.py:15
  1.3 2.4 %collective-permute-start = (bf16[2,12,12,4,4]{4,3,2,1,0:T(4,128)(2,1)S(1)}, bf16[2,12,12,4,4]{4,3,2,1,0:T(4,128)(2,1)S(1)}, u32[]{:S(2)}, u32[]{:S(2)}) collective-permute-start(bf16[2,12,12,4,4]{4,3,2,1,0:T(4,128)(2,1)S(1)} %get-tuple-element.45), channel_id=1, source_target_pairs={{0,1},{1,2},{2,3},{4,5},{5,6},{6,7},{8,9},{9,10},{10,11},{12,13},{... | collective-permute-start | bytes 27656 | tf_op jit(solution)/shard_map/ppermute | solution.py:14
  3.7 1.3 %collective-permute-start.1 = (bf16[2,12,12,4,4]{4,3,2,1,0:T(4,128)(2,1)S(1)}, bf16[2,12,12,4,4]{4,3,2,1,0:T(4,128)(2,1)S(1)}, u32[]{:S(2)}, u32[]{:S(2)}) collective-permute-start(bf16[2,12,12,4,4]{4,3,2,1,0:T(4,128)(2,1)S(1)} %get-tuple-element.46), channel_id=1, source_target_pairs={{1,0},{2,1},{3,2},{5,4},{6,5},{7,6},{9,8},{10,9},{11,10},{13,12},{... | collective-permute-start | bytes 27656 | tf_op jit(solution)/shard_map/ppermute | solution.py:17
  6.4 0.8 add_reduce_fusion
  7.4 1.9 %collective-permute-done.1 = bf16[2,12,12,4,4]{4,3,2,1,0:T(4,128)(2,1)S(1)} collective-permute-done((bf16[2,12,12,4,4]{4,3,2,1,0:T(4,128)(2,1)S(1)}, bf16[2,12,12,4,4]{4,3,2,1,0:T(4,128)(2,1)S(1)}, u32[]{:S(2)}, u32[]{:S(2)}) %collective-permute-start.1) | collective-permute-done | bytes 9248 | tf_op jit(solution)/shard_map/ppermute | solution.py:17
  9.3 1.8 %pad_maximum_fusion.1 = bf16[2,12,12,4,136]{4,3,2,1,0:T(4,128)(2,1)S(1)} fusion(bf16[2,12,12,4,4]{4,3,2,1,0:T(4,128)(2,1)S(1)} %collective-permute-done.1, bf16[2,12,12,4,128]{4,3,2,1,0:T(4,128)(2,1)} %param.8, bf16[2,12,12,4,4]{4,3,2,1,0:T(4,128)(2,1)S(1)} %collective-permute-done), kind=kLoop, calls=%fused_computation.46 | loop fusion | flops 940032 | bytes 626688 | tf_op jit(solution)/shard_map/concatenate | solution.py:18
  12.2 1.3 %collective-permute-start.3 = (bf16[2,12,12,4,128]{4,0,3,2,1:T(2,128)(2,1)S(1)}, bf16[2,12,12,4,128]{4,0,3,2,1:T(2,128)(2,1)}, u32[]{:S(2)}, u32[]{:S(2)}) collective-permute-start(bf16[2,12,12,4,128]{4,0,3,2,1:T(2,128)(2,1)S(1)} %copy.48), channel_id=1, source_target_pairs={{4,0},{8,4},{12,8},{16,12},{20,16},{24,20},{28,24},{5,1},{9,5},{13... | collective-permute-start | bytes 884744 | tf_op jit(solution)/shard_map/ppermute | solution.py:17
  13.5 5.3 %collective-permute-start.2 = (bf16[2,12,12,4,128]{4,0,3,2,1:T(2,128)(2,1)S(1)}, bf16[2,12,12,4,128]{4,0,3,2,1:T(2,128)(2,1)}, u32[]{:S(2)}, u32[]{:S(2)}) collective-permute-start(bf16[2,12,12,4,128]{4,0,3,2,1:T(2,128)(2,1)S(1)} %copy.48), channel_id=1, source_target_pairs={{0,4},{4,8},{8,12},{12,16},{16,20},{20,24},{24,28},{1,5},{5,9},{9,... | collective-permute-start | bytes 884744 | tf_op jit(solution)/shard_map/ppermute | solution.py:14
  18.9 1.9 %copy.68 = bf16[1,12,12,4,128]{2,1,4,3,0:T(8,128)(2,1)S(1)} copy(bf16[1,12,12,4,128]{4,3,2,1,0:T(4,128)(2,1)S(1)} %get-tuple-element.43) | data formatting | bytes 294912
  20.9 2.6 %copy.67 = bf16[1,12,12,4,128]{2,1,4,3,0:T(8,128)(2,1)} copy(bf16[1,12,12,4,128]{4,3,2,1,0:T(4,128)(2,1)S(1)} %get-tuple-element.44) | data formatting | bytes 294912
  23.4 5.6 %collective-permute-done.2 = bf16[2,12,12,4,128]{4,0,3,2,1:T(2,128)(2,1)} collective-permute-done((bf16[2,12,12,4,128]{4,0,3,2,1:T(2,128)(2,1)S(1)}, bf16[2,12,12,4,128]{4,0,3,2,1:T(2,128)(2,1)}, u32[]{:S(2)}, u32[]{:S(2)}) %collective-permute-start.2) | collective-permute-done | bytes 294944 | tf_op jit(solution)/shard_map/ppermute | solution.py:14
  29.1 3.0 %pad_maximum_fusion = bf16[2,12,12,12,128]{4,0,3,2,1:T(2,128)(2,1)} fusion(bf16[2,12,12,4,128]{4,0,3,2,1:T(2,128)(2,1)} %collective-permute-done.3, bf16[2,12,12,4,128]{4,0,3,2,1:T(2,128)(2,1)S(1)} %copy.48, bf16[2,12,12,4,128]{4,0,3,2,1:T(2,128)(2,1)} %collective-permute-done.2), kind=kLoop, calls=%fused_computation.44 | loop fusion | flops 884736 | bytes 1769472 | tf_op jit(solution)/shard_map/concatenate | solution.py:18
  32.1 20.1 %while.10 = (s32[]{:T(128)}, bf16[4,2,12,12,128]{4,3,2,1,0:T(8,128)(2,1)S(1)}, bf16[4,8,12,12]{3,2,1,0:T(8,128)(2,1)S(1)}, s32[4,8]{1,0:T(4,128)S(1)}, bf16[2,12,12,12,128]{4,0,3,2,1:T(2,128)(2,1)}, /*index=5*/s32[]{:T(128)}) while((s32[]{:T(128)}, bf16[4,2,12,12,128]{4,3,2,1,0:T(8,128)(2,1)S(1)}, bf16[4,8,12,12]{3,2,1,0:T(8,128)(2,1)S(1)}, ...), condition=%wide.region_3.4_spmd, body=%wide.region_2.3_spmd.sunk | while | flops 14746698 | bytes 4592905 | solution.py:95
  32.1 3.3 %gather_fusion = bf16[8,2,12,12,128]{4,1,3,2,0:T(2,128)(2,1)S(1)} fusion(bf16[2,12,12,12,128]{4,0,3,2,1:T(2,128)(2,1)} %get-tuple-element.96, s32[1024]{0:T(1024)S(1)} %pad_clamp_fusion.2), kind=kCustom, calls=%fused_computation.clone.1 | custom fusion | bytes 1179680 | tf_op jit(solution)/shard_map/while/body/eval_jaxpr/jit(_take)/gather | solution.py:71
  36.4 0.7 fusion.50
  37.2 3.3 %gather_fusion = bf16[8,2,12,12,128]{4,1,3,2,0:T(2,128)(2,1)S(1)} fusion(bf16[2,12,12,12,128]{4,0,3,2,1:T(2,128)(2,1)} %get-tuple-element.96, s32[1024]{0:T(1024)S(1)} %pad_clamp_fusion.2), kind=kCustom, calls=%fused_computation.clone.1 | custom fusion | bytes 1179680 | tf_op jit(solution)/shard_map/while/body/eval_jaxpr/jit(_take)/gather | solution.py:71
  42.2 3.3 %gather_fusion = bf16[8,2,12,12,128]{4,1,3,2,0:T(2,128)(2,1)S(1)} fusion(bf16[2,12,12,12,128]{4,0,3,2,1:T(2,128)(2,1)} %get-tuple-element.96, s32[1024]{0:T(1024)S(1)} %pad_clamp_fusion.2), kind=kCustom, calls=%fused_computation.clone.1 | custom fusion | bytes 1179680 | tf_op jit(solution)/shard_map/while/body/eval_jaxpr/jit(_take)/gather | solution.py:71
  46.4 0.7 fusion.50
  47.2 3.3 %gather_fusion = bf16[8,2,12,12,128]{4,1,3,2,0:T(2,128)(2,1)S(1)} fusion(bf16[2,12,12,12,128]{4,0,3,2,1:T(2,128)(2,1)} %get-tuple-element.96, s32[1024]{0:T(1024)S(1)} %pad_clamp_fusion.2), kind=kCustom, calls=%fused_computation.clone.1 | custom fusion | bytes 1179680 | tf_op jit(solution)/shard_map/while/body/eval_jaxpr/jit(_take)/gather | solution.py:71
  52.2 4.4 %copy.51 = bf16[4,2,12,12,128]{2,3,4,0,1:T(8,128)(2,1)} copy(bf16[4,2,12,12,128]{4,3,2,1,0:T(8,128)(2,1)S(1)} %get-tuple-element.32) | data formatting | bytes 589824 | tf_op jit(solution)/shard_map/convert_element_type | solution.py:96
  56.6 3.6 %fusion.23 = f32[4,128,12,12]{3,2,1,0:T(8,128)S(1)} fusion(bf16[1,12,12,4,128]{2,1,4,3,0:T(8,128)(2,1)} %copy.67, bf16[2,12,12,4,128]{1,2,4,3,0:T(8,128)(2,1)} %bitcast.97), kind=kOutput, calls=%fused_computation.39 | convolution fusion | flops 1769472 | bytes 4489216 | tf_op jit(solution)/shard_map/ikae,kjae->ijae/dot_general | solution.py:52
  60.7 1.2 %fusion.26 = f32[4,128,12,12]{3,2,1,0:T(8,128)S(1)} fusion(bf16[1,12,12,4,128]{2,1,4,3,0:T(8,128)(2,1)S(1)} %copy-done, bf16[2,12,12,4,128]{1,2,4,3,0:T(8,128)(2,1)S(1)} %bitcast.98), kind=kOutput, calls=%fused_computation.42 | convolution fusion | flops 1769472 | bytes 4489216 | tf_op jit(solution)/shard_map/ikae,kjae->ijae/dot_general | solution.py:46
  61.9 1.3 %subtract_convert_fusion = bf16[4,128,12,12]{3,2,1,0:T(8,128)(2,1)S(1)} fusion(f32[4,128,12,12]{3,2,1,0:T(8,128)S(1)} %fusion.26, bf16[1,12,12,4,128]{2,1,4,3,0:T(8,128)(2,1)S(1)} %copy.68, bf16[2,12,12,4,128]{1,2,4,3,0:T(8,128)(2,1)S(1)} %bitcast.99), kind=kOutput, calls=%fused_computation.24 | convolution fusion | flops 1916928 | bytes 8536064 | tf_op jit(solution)/shard_map/ikae,kjae->ijae/dot_general | solution.py:49
  63.1 1.0 %fusion.14 = f32[4,128,12,12]{3,2,1,0:T(8,128)S(1)} fusion(bf16[4,128,12,12]{3,2,1,0:T(8,128)(2,1)S(1)} %subtract_convert_fusion, bf16[1,12,12,4,128]{2,1,4,3,0:T(8,128)(2,1)S(1)} %copy.68), kind=kOutput, calls=%fused_computation.30 | convolution fusion | flops 1769472 | bytes 589824 | tf_op jit(solution)/shard_map/ikae,kjae->ijae/dot_general | solution.py:52
  64.1 2.5 %fusion.16 = f32[4,128,12,12]{3,2,1,0:T(8,128)} fusion(bf16[4,128,12,12]{3,2,1,0:T(8,128)(2,1)S(1)} %subtract_convert_fusion, bf16[1,12,12,4,128]{2,1,4,3,0:T(8,128)(2,1)S(1)} %copy-done), kind=kOutput, calls=%fused_computation.32 | convolution fusion | flops 1769472 | bytes 589824 | tf_op jit(solution)/shard_map/ikae,kjae->ijae/dot_general | solution.py:46
  66.6 1.3 %add_convert_fusion = bf16[4,128,12,12]{3,2,1,0:T(8,128)(2,1)S(1)} fusion(f32[4,128,12,12]{3,2,1,0:T(8,128)S(1)} %fusion.23, bf16[1,12,12,4,128]{2,1,4,3,0:T(8,128)(2,1)S(1)} %copy.68, bf16[2,12,12,4,128]{1,2,4,3,0:T(8,128)(2,1)S(1)} %bitcast.100), kind=kOutput, calls=%fused_computation.23 | convolution fusion | flops 1916928 | bytes 8536064 | tf_op jit(solution)/shard_map/ikae,kjae->ijae/dot_general | solution.py:55
  67.8 1.4 %copy-done.2 = bf16[4,128,12,12]{3,2,1,0:T(8,128)(2,1)} copy-done((bf16[4,128,12,12]{3,2,1,0:T(8,128)(2,1)}, bf16[4,128,12,12]{3,2,1,0:T(8,128)(2,1)S(1)}, u32[]{:S(2)}) %copy-start.2) | copy-done | bytes 147480
  69.2 2.5 %add_bitcast_fusion = f32[1,12,12,4,128]{2,1,4,3,0:T(8,128)} fusion(f32[4,128,12,12]{3,2,1,0:T(8,128)S(1)} %fusion.14, bf16[4,128,12,12]{3,2,1,0:T(8,128)(2,1)S(1)} %add_convert_fusion, bf16[1,12,12,4,128]{2,1,4,3,0:T(8,128)(2,1)S(1)} %copy-done), kind=kOutput, calls=%fused_computation.21 | convolution fusion | flops 1843200 | bytes 884736 | tf_op jit(solution)/shard_map/ikae,kjae->ijae/dot_general | solution.py:55
  71.7 3.3 %copy.59 = f32[1,12,12,4,128]{4,3,2,1,0:T(4,128)S(1)} copy(f32[1,12,12,4,128]{2,1,4,3,0:T(8,128)} %add_bitcast_fusion) | data formatting | bytes 589824 | tf_op jit(solution)/shard_map/stack | solution.py:58
  75.1 5.6 %subtract_bitcast_fusion = f32[1,12,12,4,128]{2,1,4,3,0:T(8,128)} fusion(f32[4,128,12,12]{3,2,1,0:T(8,128)} %fusion.16, bf16[4,128,12,12]{3,2,1,0:T(8,128)(2,1)} %copy-done.2, bf16[1,12,12,4,128]{2,1,4,3,0:T(8,128)(2,1)S(1)} %copy.68), kind=kOutput, calls=%fused_computation.22 | convolution fusion | flops 1843200 | bytes 884736 | tf_op jit(solution)/shard_map/ikae,kjae->ijae/dot_general | solution.py:49
  80.7 3.3 %copy.58 = f32[1,12,12,4,128]{4,3,2,1,0:T(4,128)S(1)} copy(f32[1,12,12,4,128]{2,1,4,3,0:T(8,128)} %subtract_bitcast_fusion) | data formatting | bytes 589824 | tf_op jit(solution)/shard_map/stack | solution.py:58
  84.0 0.9 %fusion.28 = bf16[2,12,12,4,128]{4,3,2,1,0:T(4,128)(2,1)} fusion(f32[1,12,12,4,128]{4,3,2,1,0:T(4,128)S(1)} %copy.59, f32[1,12,12,4,128]{4,3,2,1,0:T(4,128)S(1)} %copy.58, bf16[2,12,12,4,128]{4,3,2,1,0:T(4,128)(2,1)S(1)} %copy-done.3), kind=kLoop, calls=%fused_computation.48 | loop fusion | flops 589824 | bytes 1179648 | tf_op jit(solution)/shard_map/convert_element_type | solution.py:98
  (48 shorter events, 8.6 us)
Async XLA Ops:
  1.3 6.0 %collective-permute-start = (bf16[2,12,12,4,4]{4,3,2,1,0:T(4,128)(2,1)S(1)}, bf16[2,12,12,4,4]{4,3,2,1,0:T(4,128)(2,1)S(1)}, u32[]{:S(2)}, u32[]{:S(2)}) collective-permute-start(bf16[2,12,12,4,4]{4,3,2,1,0:T(4,128)(2,1)S(1)} %get-tuple-element.45), channel_id=1, source_target_pairs={{0,1},{1,2},{2,3},{4,5},{5,6},{6,7},{8,9},{9,10},{10,11},{12,13},{... | collective-permute-start | bytes 27656 | tf_op jit(solution)/shard_map/ppermute | solution.py:14
  3.7 5.6 %collective-permute-start.1 = (bf16[2,12,12,4,4]{4,3,2,1,0:T(4,128)(2,1)S(1)}, bf16[2,12,12,4,4]{4,3,2,1,0:T(4,128)(2,1)S(1)}, u32[]{:S(2)}, u32[]{:S(2)}) collective-permute-start(bf16[2,12,12,4,4]{4,3,2,1,0:T(4,128)(2,1)S(1)} %get-tuple-element.46), channel_id=1, source_target_pairs={{1,0},{2,1},{3,2},{5,4},{6,5},{7,6},{9,8},{10,9},{11,10},{13,12},{... | collective-permute-start | bytes 27656 | tf_op jit(solution)/shard_map/ppermute | solution.py:17
  7.4 11.4 %copy-start.3 = (bf16[2,12,12,4,128]{4,3,2,1,0:T(4,128)(2,1)S(1)}, bf16[2,12,12,4,128]{4,3,2,1,0:T(4,128)(2,1)}, u32[]{:S(2)}) copy-start(bf16[2,12,12,4,128]{4,3,2,1,0:T(4,128)(2,1)} %param.8) | copy-start | bytes 884740
  7.4 11.5 %copy-start.4 = (bf16[8,12,12,4]{2,3,1,0:T(4,128)(2,1)S(1)}, bf16[8,12,12,4]{2,3,1,0:T(4,128)(2,1)}, u32[]{:S(2)}) copy-start(bf16[8,12,12,4]{2,3,1,0:T(4,128)(2,1)} %param.9) | copy-start | bytes 27652
  12.2 11.3 %collective-permute-start.3 = (bf16[2,12,12,4,128]{4,0,3,2,1:T(2,128)(2,1)S(1)}, bf16[2,12,12,4,128]{4,0,3,2,1:T(2,128)(2,1)}, u32[]{:S(2)}, u32[]{:S(2)}) collective-permute-start(bf16[2,12,12,4,128]{4,0,3,2,1:T(2,128)(2,1)S(1)} %copy.48), channel_id=1, source_target_pairs={{4,0},{8,4},{12,8},{16,12},{20,16},{24,20},{28,24},{5,1},{9,5},{13... | collective-permute-start | bytes 884744 | tf_op jit(solution)/shard_map/ppermute | solution.py:17
  13.5 15.6 %collective-permute-start.2 = (bf16[2,12,12,4,128]{4,0,3,2,1:T(2,128)(2,1)S(1)}, bf16[2,12,12,4,128]{4,0,3,2,1:T(2,128)(2,1)}, u32[]{:S(2)}, u32[]{:S(2)}) collective-permute-start(bf16[2,12,12,4,128]{4,0,3,2,1:T(2,128)(2,1)S(1)} %copy.48), channel_id=1, source_target_pairs={{0,4},{4,8},{8,12},{12,16},{16,20},{20,24},{24,28},{1,5},{5,9},{9,... | collective-permute-start | bytes 884744 | tf_op jit(solution)/shard_map/ppermute | solution.py:14
  18.9 4.5 %copy-start.5 = (s32[4,8]{1,0:T(4,128)S(1)}, s32[4,8]{1,0:T(4,128)}, u32[]{:S(2)}) copy-start(s32[4,8]{1,0:T(4,128)} %param.10) | copy-start | bytes 388
  56.6 3.6 %copy-start = (bf16[1,12,12,4,128]{2,1,4,3,0:T(8,128)(2,1)S(1)}, bf16[1,12,12,4,128]{2,1,4,3,0:T(8,128)(2,1)}, u32[]{:S(2)}) copy-start(bf16[1,12,12,4,128]{2,1,4,3,0:T(8,128)(2,1)} %copy.67) | copy-start | bytes 442372
  56.6 4.1 %copy-start.1 = (bf16[4,2,12,12,128]{2,3,4,0,1:T(8,128)(2,1)S(1)}, bf16[4,2,12,12,128]{2,3,4,0,1:T(8,128)(2,1)}, u32[]{:S(2)}) copy-start(bf16[4,2,12,12,128]{2,3,4,0,1:T(8,128)(2,1)} %copy.51) | copy-start | bytes 884740
  67.8 1.4 %copy-start.2 = (bf16[4,128,12,12]{3,2,1,0:T(8,128)(2,1)}, bf16[4,128,12,12]{3,2,1,0:T(8,128)(2,1)S(1)}, u32[]{:S(2)}) copy-start(bf16[4,128,12,12]{3,2,1,0:T(8,128)(2,1)S(1)} %add_convert_fusion) | copy-start | bytes 442372
where the time goes:
time: 86.1 us; the launch traced here: 84.9 us
  local copies, waits for them, and re-layouts  32.7 us (38%)
  matrix products  23.5 us (27%)
  other arithmetic  10.4 us (12%)
  starting transfers between devices  10.2 us (12%)
  waiting for transfers between devices  7.55 us (9%)
    gather x4, local copies, waits for them, and re-layouts, sandwich(): picked = jnp.take(phonon_sum, index_row, axis=3)  13.1 us
    ppermute x2, starting transfers between devices, padded(): lax.ppermute(lax.slice_in_dim(block, block.shape[dim] - width, None, axis...  7.66 us
    dot_general x2, matrix products, complex_product(): jnp.einsum('ikae,kjae->ijae', factor_left[1], factor_right[1], preferred_...  6.89 us
    another operation x2, local copies, waits for them, and re-layouts, complex_product(): return jnp.stack([real_part, imag_part])  6.62 us
    unnamed x15, local copies, waits for them, and re-layouts  6.4 us
    ppermute x2, waiting for transfers between devices, padded(): lax.ppermute(lax.slice_in_dim(block, block.shape[dim] - width, None, axis...  5.64 us
    concatenate x2, other arithmetic, padded(): block = jnp.concatenate([low, block, high], axis=dim)  4.75 us
    dot_general x2, matrix products, complex_product(): jnp.einsum('ikae,kjae->ijae', factor_left[0], factor_right[1], preferred_...  4.52 us
  transfers between devices with their start and end apart: 4, of which 2 were waited for; matrix products, arithmetic and copies ran while one was open for 8% of the time, Pallas kernels for 0%

commit v1 on v0

v1 whole, which is shorter than its diff:
```python
import functools
import math
import jax
import jax.numpy as jnp
from jax import lax
from jax.experimental import pallas as pl
from jax.experimental.pallas import tpu as pltpu
from jax.sharding import PartitionSpec as P

WIDTH = 4
EDGE = 2 * WIDTH
LANES = 128
F32 = jnp.float32
BF16 = jnp.bfloat16


def iota(shape, axis):
    return lax.broadcasted_iota(jnp.int32, shape, axis)


def dot(a, b, dims=((1,), (0,))):
    return lax.dot_general(a, b, (dims, ((), ())), preferred_element_type=F32)


def steps_below(x, step, most):
    return sum((x >= step * m).astype(jnp.int32) for m in range(1, most))


def pack_kernel(g_ref, edge_ref):
    energies = g_ref.shape[2]
    row = iota((EDGE, energies), 0)
    lane = iota((EDGE, energies), 1)
    want = jnp.where(row < WIDTH, row, row + energies - EDGE)
    pick = (lane == want).astype(F32).astype(BF16)
    parts = [dot(pick, g_ref[r], ((1,), (1,))) for r in range(2)]
    edge_ref[...] = jnp.concatenate(parts, axis=0).astype(BF16)


def band_weights(sh_ref, st_ref, oc_ref):
    shifts = sh_ref[...]
    emit = st_ref[...] * oc_ref[...]
    absorb = st_ref[...] * (oc_ref[...] + 1.0)
    zero = jnp.zeros_like(emit)
    weights = []
    for o in range(-WIDTH, WIDTH + 1):
        both = jnp.where(shifts == -o, emit, zero) + jnp.where(shifts == o, absorb, zero)
        weights.append(jnp.sum(both, axis=1, keepdims=True))
    return weights


def banded(weights, gap, keep=None):
    table = jnp.zeros(gap.shape, F32)
    for o in range(-WIDTH, WIDTH + 1):
        hit = gap == o
        if keep is not None:
            hit = hit & keep
        table = jnp.where(hit, weights[o + WIDTH], table)
    return table.astype(BF16)


def weights_kernel(orb, c_ref, nbr_ref, g_ref, sh_ref, st_ref, oc_ref,
                   wl_ref, wo_ref, wh_ref, s_ref, band_ref, rim_ref, t1_ref, t2_ref):
    atoms, bonds = nbr_ref.shape
    energies = g_ref.shape[2]
    span = orb * atoms
    cols = t1_ref.shape[3]
    tiles = cols // LANES
    period = t2_ref.shape[4]
    here = lax.axis_index("atom")
    place = lax.axis_index("energy")
    last = lax.axis_size("energy") - 1

    weights = band_weights(sh_ref, st_ref, oc_ref)
    band_ref[...] = banded(weights, iota((energies, energies), 0) - iota((energies, energies), 1))
    rim = (2 * EDGE, energies)
    row = iota(rim, 0)
    spot = row & (EDGE - 1)
    lane = iota(rim, 1)
    low_part = spot < WIDTH
    keep = jnp.where(low_part, jnp.where(place < last, 1, 0), jnp.where(place > 0, 1, 0)) > 0
    gap = jnp.where(low_part, energies + spot, spot - EDGE) - lane
    for r in range(2):
        rim_ref[r] = banded(weights, gap, keep & ((row >= EDGE) == (r == 1)))

    c = c_ref[...]
    krow, klane = iota((orb, cols), 0), iota((orb, cols), 1)
    spread = ((klane >= krow * span) & (klane < (krow + 1) * span)).astype(F32).astype(BF16)
    left = dot(c, spread).reshape(bonds * orb * atoms // 8, 8, cols)
    turned = pltpu.roll(left, atoms, 1)
    upper = iota(left.shape, 1) < atoms
    first = jnp.where(upper, left, turned)
    second = jnp.where(upper, turned, left)
    both = jnp.stack([first, second], axis=1).reshape(bonds, orb, 8, cols)
    t1_ref[...] = jnp.concatenate([both, both], axis=2).astype(BF16)

    lrow, llane = iota((orb, period), 0), iota((orb, period), 1)
    inner = llane - span * steps_below(llane, span, period // span)
    spread = ((inner >= lrow * atoms) & (inner < (lrow + 1) * atoms)).astype(F32).astype(BF16)
    right = dot(c, spread).reshape(bonds, span // 16, 16, period)
    own = iota((16, period), 0) & (atoms - 1)
    other = iota((16, period), 1) & (atoms - 1)
    for n in range(bonds):
        near = jnp.zeros((16, period), jnp.int32)
        for a in range(atoms):
            near = jnp.where(own == a, nbr_ref[a, n], near)
        for s in range(3):
            mask = near == other + (here + (s - 1)) * atoms
            t2_ref[s, n] = jnp.where(mask[None], right[n], 0.0).astype(BF16)

    for t in range(tiles):
        at = slice(t * LANES, (t + 1) * LANES)
        start = (t * LANES) % period
        cut = slice(start, start + LANES)

        def body(i, carry):
            x = t1_ref[:, i, :, at]
            for s, out in enumerate((wl_ref, wo_ref, wh_ref)):
                for q in range(span // 16):
                    total = x[0] * t2_ref[s, 0, q, :, cut]
                    for n in range(1, bonds):
                        total = total + x[n] * t2_ref[s, n, q, :, cut]
                    out[i, q * 16:(q + 1) * 16, at] = total
            return carry

        lax.fori_loop(0, orb, body, 0)

    s_ref[...] = slab_product(wo_ref, g_ref)


def slab_product(w_ref, g_ref):
    rows = g_ref.shape[1]
    w = w_ref[...].reshape(rows, w_ref.shape[2])[:, :rows]
    return dot(w, jnp.concatenate([g_ref[0], g_ref[1]], axis=1))


def rim_product(w_ref, f_ref):
    rows = f_ref.shape[1]
    w = w_ref[...].reshape(rows, w_ref.shape[2])[:, :rows]
    return dot(w, f_ref[...], ((1,), (1,)))


def doubled(x, orb, atoms):
    pairs = x.reshape(orb * orb * atoms // 8, 8, x.shape[1])
    turned = pltpu.roll(pairs, atoms, 1)
    upper = iota(pairs.shape, 1) < atoms
    first = jnp.where(upper, pairs, turned)
    second = jnp.where(upper, turned, pairs)
    return jnp.stack([first, second], axis=1).reshape(orb, orb, 8, x.shape[1])


def final_kernel(orb, atoms, g_ref, gl_ref, gh_ref, f_ref, fl_ref, fh_ref, wl_ref, wo_ref, wh_ref,
                 s_ref, band_ref, rim_ref, out_ref, gn_ref, gd_ref, sn_ref, ld_ref):
    rows = g_ref.shape[1]
    energies = g_ref.shape[2]
    groups = orb * atoms // 8

    def put(ref, c, x):
        ref[c] = x.reshape(orb, groups, 8, energies)

    gr = g_ref[0].astype(F32)
    gi = g_ref[1].astype(F32)
    for c, x in enumerate((gr, gi, gr + gi)):
        put(gn_ref, c, x)
        gd_ref[c] = doubled(x, orb, atoms)

    total = s_ref[...] + slab_product(wl_ref, gl_ref) + slab_product(wh_ref, gh_ref)
    rim = rim_product(wo_ref, f_ref) + rim_product(wl_ref, fl_ref) + rim_product(wh_ref, fh_ref)
    rim = rim.astype(BF16)
    parts = []
    for r in range(2):
        body = total[:, r * energies:(r + 1) * energies].astype(BF16)
        parts.append(dot(body, band_ref[...]) + dot(rim, rim_ref[r]))
    for c, x in enumerate((parts[0], parts[1], parts[0] + parts[1])):
        put(sn_ref, c, x)

    def product(left, right_ref, acc):
        for k in range(orb):
            for c in range(3):
                right = right_ref[c, k]
                for d in range(2):
                    term = left(c, d, k)[None] * right
                    acc[c][d] = term if acc[c][d] is None else acc[c][d] + term
        return acc

    def pair(p, carry):
        m = product(lambda c, d, k: gd_ref[c, 2 * p + d, k], sn_ref, [[None, None] for _ in range(3)])
        upper = iota((groups, 8, energies), 1) < atoms
        for d in range(2):
            lr = m[0][d] - m[1][d]
            li = m[2][d] - (m[0][d] + m[1][d])
            for c, x in enumerate((lr, li, lr + li)):
                turned = pltpu.roll(x, atoms, 1)
                first = jnp.where(upper, x, turned)
                second = jnp.where(upper, turned, x)
                ld_ref[c, d] = jnp.stack([first, second], axis=1).reshape(orb, 8, energies)
        m = product(lambda c, d, k: ld_ref[c, d, k], gn_ref, [[None, None] for _ in range(3)])
        for d in range(2):
            i = 2 * p + d
            ur = gn_ref[0, i] + (m[0][d] - m[1][d])
            ui = gn_ref[1, i] + (m[2][d] - (m[0][d] + m[1][d]))
            out_ref[0, i] = ur.reshape(orb * atoms, energies).astype(BF16)
            out_ref[1, i] = ui.reshape(orb * atoms, energies).astype(BF16)
        return carry

    lax.fori_loop(0, orb // 2, pair, 0)


def ring(value, axis, step):
    count = lax.axis_size(axis)
    return lax.ppermute(value, axis, [(i, (i + step) % count) for i in range(count)])


def per_device(bare_green, coupling_grad, neighbours, shifts, strength, occupation):
    _, orb, _, atoms, energies = bare_green.shape
    bonds = coupling_grad.shape[0]
    rows = orb * orb * atoms
    span = orb * atoms
    cols = -(-rows // LANES) * LANES
    period = span * LANES // math.gcd(span, LANES)
    vmem = pl.BlockSpec(memory_space=pltpu.VMEM)
    smem = pl.BlockSpec(memory_space=pltpu.SMEM)
    big = pltpu.CompilerParams(vmem_limit_bytes=48 * 1024 * 1024)

    green = bare_green.reshape(2, rows, energies)
    from_low = ring(green, "atom", 1)
    from_high = ring(green, "atom", -1)

    edge = pl.pallas_call(
        pack_kernel,
        out_shape=jax.ShapeDtypeStruct((2 * EDGE, rows), BF16),
        in_specs=[vmem], out_specs=vmem, name="pack_edges",
    )(green)
    edge_low = ring(edge, "energy", 1)
    edge_high = ring(edge, "energy", -1)
    high_side = (jnp.arange(2 * EDGE, dtype=jnp.int32)[:, None] & WIDTH) > 0
    rim = jnp.where(high_side, edge_low, edge_high)
    rim_low = ring(rim, "atom", 1)
    rim_high = ring(rim, "atom", -1)

    grads = jnp.transpose(coupling_grad, (0, 1, 3, 2)).reshape(bonds * orb * atoms, orb)
    w_shape = jax.ShapeDtypeStruct((orb, span, cols), BF16)
    w_low, w_own, w_high, partial_sum, band, rim_band = pl.pallas_call(
        functools.partial(weights_kernel, orb),
        out_shape=[
            w_shape, w_shape, w_shape,
            jax.ShapeDtypeStruct((rows, 2 * energies), F32),
            jax.ShapeDtypeStruct((energies, energies), BF16),
            jax.ShapeDtypeStruct((2, 2 * EDGE, energies), BF16),
        ],
        in_specs=[vmem, smem, vmem, vmem, vmem, vmem], out_specs=[vmem] * 6,
        scratch_shapes=[
            pltpu.VMEM((bonds, orb, 16, cols), BF16),
            pltpu.VMEM((3, bonds, span // 16, 16, period), BF16),
        ],
        compiler_params=big, name="weights",
    )(grads, neighbours, green, shifts[None], strength[None], occupation[None])

    full = (3, orb, span // 8, 8, energies)
    result = pl.pallas_call(
        functools.partial(final_kernel, orb, atoms),
        out_shape=jax.ShapeDtypeStruct((2, orb, span, energies), BF16),
        in_specs=[vmem] * 12, out_specs=vmem,
        scratch_shapes=[
            pltpu.VMEM(full, F32),
            pltpu.VMEM((3, orb, orb, 8, energies), F32),
            pltpu.VMEM(full, F32),
            pltpu.VMEM((3, 2, orb, 8, energies), F32),
        ],
        compiler_params=big, name="green_update",
    )(green, from_low, from_high, rim, rim_low, rim_high, w_low, w_own, w_high, partial_sum, band, rim_band)
    return result.reshape(bare_green.shape)


def solution(mesh):
    placed = (
        P(None, None, None, "atom", "energy"),
        P(None, None, None, "atom"),
        P("atom", None),
        P(),
        P(),
        P(),
    )
    return jax.shard_map(
        per_device,
        mesh=mesh,
        in_specs=placed,
        out_specs=P(None, None, None, "atom", "energy"),
        check_vma=False,
    )
```

time: 86.1 us -> 25.5 us (0.30); the launches traced: 84.9 us -> 25.3 us
  local copies, waits for them, and re-layouts: 32.7 us -> 1.58 us
  matrix products: 23.5 us -> 0 us
  other arithmetic: 10.4 us -> 0.09 us
  Pallas kernels: 0 us -> 10.1 us
  waiting for transfers between devices: 7.55 us -> 1.77 us
  starting transfers between devices: 10.2 us -> 11.7 us
    dot_general x17 -> x0, matrix products: 23.5 us -> none  [the longest x2 6.89 us: complex_product(): jnp.einsum('ikae,kjae->ijae', factor_left[1], factor_right[1], preferred_...]
    gather x4 -> x0, local copies, waits for them, and re-layouts: 13.1 us -> none  [sandwich(): picked = jnp.take(phonon_sum, index_row, axis=3)]
    pallas_call x0 -> x3, Pallas kernels: none -> 10.1 us  [the longest x1 4.28 us: per_device(): pl.pallas_call(functools.partial(weights_kernel, orb), out_shape=[w_shape...]
    another operation x2 -> x0, local copies, waits for them, and re-layouts: 6.62 us -> none  [complex_product(): return jnp.stack([real_part, imag_part])]
    ppermute x4 -> x6, waiting for transfers between devices: 7.55 us -> 1.77 us  [ring(): lax.ppermute(value, axis, [(i, (i + step) % count) for i in range(count)])]
    unnamed x15 -> x12, local copies, waits for them, and re-layouts: 6.4 us -> 1.58 us
    concatenate x2 -> x0, other arithmetic: 4.75 us -> none  [padded(): block = jnp.concatenate([low, block, high], axis=dim)]
    convert_element_type x1 -> x0, local copies, waits for them, and re-layouts: 4.4 us -> none  [per_device(): self_energy = jnp.moveaxis(self_energy, 0, 3).astype(jnp.bfloat16)]
  transfers between devices with their start and end apart: 4 -> 6, of which waited for: 2 -> 1; matrix products, arithmetic and copies ran while one was open for 8% -> 0% of each run, Pallas kernels for 0% -> 17%
where the time goes in v1:
time: 25.5 us; the launch traced here: 25.3 us
  starting transfers between devices  11.7 us (46%)
  Pallas kernels  10.1 us (40%)
  waiting for transfers between devices  1.77 us (7%)
  local copies, waits for them, and re-layouts  1.58 us (6%)
    ppermute x6, starting transfers between devices, ring(): lax.ppermute(value, axis, [(i, (i + step) % count) for i in range(count)])  11.7 us
    pallas_call x1, Pallas kernels, per_device(): pl.pallas_call(functools.partial(weights_kernel, orb), out_shape=[w_shape...  4.28 us
    pallas_call x1, Pallas kernels, per_device(): pl.pallas_call(functools.partial(final_kernel, orb, atoms), out_shape=jax...  4.03 us
    pallas_call x1, Pallas kernels, per_device(): pl.pallas_call(pack_kernel, out_shape=jax.ShapeDtypeStruct((2 * EDGE, row...  1.84 us
    ppermute x6, waiting for transfers between devices, ring(): lax.ppermute(value, axis, [(i, (i + step) % count) for i in range(count)])  1.77 us
    unnamed x12, local copies, waits for them, and re-layouts  1.58 us
  transfers between devices with their start and end apart: 6, of which 1 were waited for; matrix products, arithmetic and copies ran while one was open for 0% of the time, Pallas kernels for 17%

profile of v1, /device:TPU:0, one launch (start us, length us, event | category | flops | bytes accessed | tf_op | source)
XLA Modules:
  0.0 25.3 jit_solution(1206095370593514176)
XLA Ops:
  0.0 0.0 copy-start
  0.0 1.8 %pack_edges.1 = bf16[16,576]{1,0:T(8,128)(2,1)} custom-call(bf16[2,576,128]{2,1,0:T(8,128)(2,1)} %bitcast.8), custom_call_target="tpu_custom_call" | custom-call | tf_op jit(solution)/shard_map/pack_edges/pallas_call | solution.py:228
  1.8 2.4 %collective-permute-start.3 = (bf16[16,576]{1,0:T(8,128)(2,1)}, bf16[16,576]{1,0:T(8,128)(2,1)S(1)}, u32[]{:S(2)}, u32[]{:S(2)}) collective-permute-start(bf16[16,576]{1,0:T(8,128)(2,1)} %pack_edges.1), channel_id=1, source_target_pairs={{0,3},{1,0},{2,1},{3,2},{4,7},{5,4},{6,5},{7,6},{8,11},{9,8},{10,9... | collective-permute-start | bytes 55304 | tf_op jit(solution)/shard_map/ppermute | solution.py:210
  4.2 0.0 collective-permute-start.2
  4.3 0.0 copy-done
  4.3 4.5 %collective-permute-start.1 = (bf16[2,576,128]{2,1,0:T(8,128)(2,1)S(1)}, bf16[2,576,128]{2,1,0:T(8,128)(2,1)S(1)}, u32[]{:S(2)}, u32[]{:S(2)}) collective-permute-start(bf16[2,576,128]{2,1,0:T(8,128)(2,1)S(1)} %bitcast.9), channel_id=1, source_target_pairs={{0,28},{4,0},{8,4},{12,8},{16,12},{20,16},{24,20},{28,24},{1,29},{... | collective-permute-start | bytes 884744 | tf_op jit(solution)/shard_map/ppermute | solution.py:210
  8.8 0.0 collective-permute-start
  8.8 0.0 collective-permute-done.3
  8.8 0.0 collective-permute-done.2
  8.8 0.1 broadcast_select_fusion.f_ref
  8.9 4.7 %collective-permute-start.5 = (bf16[16,576]{1,0:T(8,128)(2,1)S(1)}, bf16[16,576]{1,0:T(8,128)(2,1)S(1)}, u32[]{:S(2)}, u32[]{:S(2)}) collective-permute-start(bf16[16,576]{1,0:T(8,128)(2,1)S(1)} %broadcast_select_fusion.f_ref), channel_id=1, source_target_pairs={{0,28},{4,0},{8,4},{12,8},{16,12},{20,16},{24,20},{28,24},{1,29},{... | collective-permute-start | bytes 55304 | tf_op jit(solution)/shard_map/ppermute | solution.py:210
  13.6 0.0 collective-permute-start.4
  13.6 0.0 copy-start.2
  13.6 0.0 copy-start.3
  13.6 0.0 copy-start.4
  13.6 0.0 copy-start.5
  13.6 0.7 %copy-done.2 = s32[4,8]{1,0:T(4,128)S(1)} copy-done((s32[4,8]{1,0:T(4,128)S(1)}, s32[4,8]{1,0:T(4,128)}, u32[]{:S(2)}) %copy-start.2) | copy-done | bytes 152
  14.3 0.0 copy-done.3
  14.3 0.0 copy-done.4
  14.3 0.0 copy-done.5
  14.3 0.0 copy-start.1
  14.3 0.9 %copy-done.1 = bf16[8,12,12,4]{2,3,1,0:T(4,128)(2,1)S(1)} copy-done((bf16[8,12,12,4]{2,3,1,0:T(4,128)(2,1)S(1)}, bf16[8,12,12,4]{2,3,1,0:T(4,128)(2,1)}, u32[]{:S(2)}) %copy-start.1) | copy-done | bytes 9240
  15.2 4.3 %weights.1 = (bf16[12,48,640]{2,1,0:T(8,128)(2,1)S(1)}, bf16[12,48,640]{2,1,0:T(8,128)(2,1)S(1)}, bf16[12,48,640]{2,1,0:T(8,128)(2,1)S(1)}, f32[576,256]{1,0:T(8...) custom-call(bf16[384,12]{1,0:T(8,128)(2,1)S(1)} %bitcast.13, s32[4,8]{1,0:T(4,128)S(1)} %copy-done.2, ...), custom_call_target="tpu_custom_call" | custom-call | tf_op jit(solution)/shard_map/weights/pallas_call | solution.py:242
  19.5 0.0 collective-permute-done.5.fh_ref
  19.5 1.8 %collective-permute-done.4.fl_ref = bf16[16,576]{1,0:T(8,128)(2,1)S(1)} collective-permute-done((bf16[16,576]{1,0:T(8,128)(2,1)S(1)}, bf16[16,576]{1,0:T(8,128)(2,1)S(1)}, u32[]{:S(2)}, u32[]{:S(2)}) %collective-permute-start.4) | collective-permute-done | bytes 18464 | tf_op jit(solution)/shard_map/ppermute | solution.py:210
  21.3 0.0 collective-permute-done.1.gh_ref
  21.3 0.0 collective-permute-done.gl_ref
  21.3 4.0 %green_update.1 = bf16[2,12,48,128]{3,2,1,0:T(8,128)(2,1)} custom-call(bf16[2,576,128]{2,1,0:T(8,128)(2,1)S(1)} %bitcast.12, bf16[2,576,128]{2,1,0:T(8,128)(2,1)S(1)} %collective-permute-done.gl_ref, bf16[2,576,128]{2,1,0:T(8,128)(2,1)S(1)} %collective-permute-done.1.gh_ref, bf16[16,576]{1,0:T(8,128)(2,1)S(1)} %broadcast_select_fusion.f_ref, ...), custom_call_target="tpu_custom_call" | custom-call | tf_op jit(solution)/shard_map/green_update/pallas_call | solution.py:259
  (1 shorter events, 0.0 us)
Async XLA Ops:
  0.0 4.3 %copy-start = (bf16[2,12,12,4,128]{4,3,2,1,0:T(4,128)(2,1)S(1)}, bf16[2,12,12,4,128]{4,3,2,1,0:T(4,128)(2,1)}, u32[]{:S(2)}) copy-start(bf16[2,12,12,4,128]{4,3,2,1,0:T(4,128)(2,1)} %param.6) | copy-start | bytes 884740
  1.8 7.0 %collective-permute-start.3 = (bf16[16,576]{1,0:T(8,128)(2,1)}, bf16[16,576]{1,0:T(8,128)(2,1)S(1)}, u32[]{:S(2)}, u32[]{:S(2)}) collective-permute-start(bf16[16,576]{1,0:T(8,128)(2,1)} %pack_edges.1), channel_id=1, source_target_pairs={{0,3},{1,0},{2,1},{3,2},{4,7},{5,4},{6,5},{7,6},{8,11},{9,8},{10,9... | collective-permute-start | bytes 55304 | tf_op jit(solution)/shard_map/ppermute | solution.py:210
  4.2 4.6 %collective-permute-start.2 = (bf16[16,576]{1,0:T(8,128)(2,1)}, bf16[16,576]{1,0:T(8,128)(2,1)S(1)}, u32[]{:S(2)}, u32[]{:S(2)}) collective-permute-start(bf16[16,576]{1,0:T(8,128)(2,1)} %pack_edges.1), channel_id=1, source_target_pairs={{0,1},{1,2},{2,3},{3,0},{4,5},{5,6},{6,7},{7,4},{8,9},{9,10},{10,1... | collective-permute-start | bytes 55304 | tf_op jit(solution)/shard_map/ppermute | solution.py:210
  4.3 17.0 %collective-permute-start.1 = (bf16[2,576,128]{2,1,0:T(8,128)(2,1)S(1)}, bf16[2,576,128]{2,1,0:T(8,128)(2,1)S(1)}, u32[]{:S(2)}, u32[]{:S(2)}) collective-permute-start(bf16[2,576,128]{2,1,0:T(8,128)(2,1)S(1)} %bitcast.9), channel_id=1, source_target_pairs={{0,28},{4,0},{8,4},{12,8},{16,12},{20,16},{24,20},{28,24},{1,29},{... | collective-permute-start | bytes 884744 | tf_op jit(solution)/shard_map/ppermute | solution.py:210
  8.8 12.5 %collective-permute-start = (bf16[2,576,128]{2,1,0:T(8,128)(2,1)S(1)}, bf16[2,576,128]{2,1,0:T(8,128)(2,1)S(1)}, u32[]{:S(2)}, u32[]{:S(2)}) collective-permute-start(bf16[2,576,128]{2,1,0:T(8,128)(2,1)S(1)} %bitcast.10), channel_id=1, source_target_pairs={{0,4},{4,8},{8,12},{12,16},{16,20},{20,24},{24,28},{28,0},{1,5},{5... | collective-permute-start | bytes 884744 | tf_op jit(solution)/shard_map/ppermute | solution.py:210
  8.9 10.6 %collective-permute-start.5 = (bf16[16,576]{1,0:T(8,128)(2,1)S(1)}, bf16[16,576]{1,0:T(8,128)(2,1)S(1)}, u32[]{:S(2)}, u32[]{:S(2)}) collective-permute-start(bf16[16,576]{1,0:T(8,128)(2,1)S(1)} %broadcast_select_fusion.f_ref), channel_id=1, source_target_pairs={{0,28},{4,0},{8,4},{12,8},{16,12},{20,16},{24,20},{28,24},{1,29},{... | collective-permute-start | bytes 55304 | tf_op jit(solution)/shard_map/ppermute | solution.py:210
  13.6 7.7 %collective-permute-start.4 = (bf16[16,576]{1,0:T(8,128)(2,1)S(1)}, bf16[16,576]{1,0:T(8,128)(2,1)S(1)}, u32[]{:S(2)}, u32[]{:S(2)}) collective-permute-start(bf16[16,576]{1,0:T(8,128)(2,1)S(1)} %broadcast_select_fusion.f_ref), channel_id=1, source_target_pairs={{0,4},{4,8},{8,12},{12,16},{16,20},{20,24},{24,28},{28,0},{1,5},{5... | collective-permute-start | bytes 55304 | tf_op jit(solution)/shard_map/ppermute | solution.py:210
  13.6 0.7 %copy-start.2 = (s32[4,8]{1,0:T(4,128)S(1)}, s32[4,8]{1,0:T(4,128)}, u32[]{:S(2)}) copy-start(s32[4,8]{1,0:T(4,128)} %nbr_ref.1) | copy-start | bytes 388
  13.6 0.7 %copy-start.3 = (s32[32]{0:T(128)S(1)}, s32[32]{0:T(128)}, u32[]{:S(2)}) copy-start(s32[32]{0:T(128)} %param.9) | copy-start | bytes 388
  13.6 0.7 %copy-start.4 = (f32[32]{0:T(128)S(1)}, f32[32]{0:T(128)}, u32[]{:S(2)}) copy-start(f32[32]{0:T(128)} %param.10) | copy-start | bytes 388
  13.6 0.7 %copy-start.5 = (f32[32]{0:T(128)S(1)}, f32[32]{0:T(128)}, u32[]{:S(2)}) copy-start(f32[32]{0:T(128)} %param.11) | copy-start | bytes 388
  14.3 0.9 %copy-start.1 = (bf16[8,12,12,4]{2,3,1,0:T(4,128)(2,1)S(1)}, bf16[8,12,12,4]{2,3,1,0:T(4,128)(2,1)}, u32[]{:S(2)}) copy-start(bf16[8,12,12,4]{2,3,1,0:T(4,128)(2,1)} %param.7) | copy-start | bytes 27652

commit v2 on v1

--- a/solution.py
+++ b/solution.py
@@ -34,6 +34,12 @@
     pick = (lane == want).astype(F32).astype(BF16)
     parts = [dot(pick, g_ref[r], ((1,), (1,))) for r in range(2)]
     edge_ref[...] = jnp.concatenate(parts, axis=0).astype(BF16)
+
+
+def rim_kernel(low_ref, high_ref, after_ref, rim_ref):
+    below = (iota(rim_ref.shape, 0) & WIDTH) == 0
+    low, high = low_ref[...].astype(F32), high_ref[...].astype(F32)
+    rim_ref[...] = jnp.where(below, high, low).astype(BF16)
 
 
 def band_weights(sh_ref, st_ref, oc_ref):
@@ -97,6 +103,8 @@
     inner = llane - span * steps_below(llane, span, period // span)
     spread = ((inner >= lrow * atoms) & (inner < (lrow + 1) * atoms)).astype(F32).astype(BF16)
     right = dot(c, spread).reshape(bonds, span // 16, 16, period)
+    odd = here & 1
+    base = (here + 1 - 2 * odd, here, here - 1 + 2 * odd)
     own = iota((16, period), 0) & (atoms - 1)
     other = iota((16, period), 1) & (atoms - 1)
     for n in range(bonds):
@@ -104,7 +112,7 @@
         for a in range(atoms):
             near = jnp.where(own == a, nbr_ref[a, n], near)
         for s in range(3):
-            mask = near == other + (here + (s - 1)) * atoms
+            mask = near == other + base[s] * atoms
             t2_ref[s, n] = jnp.where(mask[None], right[n], 0.0).astype(BF16)
 
     for t in range(tiles):
@@ -124,13 +132,13 @@
 
         lax.fori_loop(0, orb, body, 0)
 
-    s_ref[...] = slab_product(wo_ref, g_ref)
-
-
-def slab_product(w_ref, g_ref):
-    rows = g_ref.shape[1]
+    s_ref[...] = slab_product(wo_ref, g_ref.at[0], g_ref.at[1])
+
+
+def slab_product(w_ref, *parts):
+    rows = parts[0].shape[0]
     w = w_ref[...].reshape(rows, w_ref.shape[2])[:, :rows]
-    return dot(w, jnp.concatenate([g_ref[0], g_ref[1]], axis=1))
+    return dot(w, jnp.concatenate([x[...] for x in parts], axis=1))
 
 
 def rim_product(w_ref, f_ref):
@@ -148,7 +156,7 @@
     return jnp.stack([first, second], axis=1).reshape(orb, orb, 8, x.shape[1])
 
 
-def final_kernel(orb, atoms, g_ref, gl_ref, gh_ref, f_ref, fl_ref, fh_ref, wl_ref, wo_ref, wh_ref,
+def final_kernel(orb, atoms, g_ref, b_ref, a_ref, f_ref, fl_ref, fh_ref, wl_ref, wo_ref, wh_ref,
                  s_ref, band_ref, rim_ref, out_ref, gn_ref, gd_ref, sn_ref, ld_ref):
     rows = g_ref.shape[1]
     energies = g_ref.shape[2]
@@ -163,7 +171,7 @@
         put(gn_ref, c, x)
         gd_ref[c] = doubled(x, orb, atoms)
 
-    total = s_ref[...] + slab_product(wl_ref, gl_ref) + slab_product(wh_ref, gh_ref)
+    total = s_ref[...] + slab_product(wl_ref, a_ref.at[0], a_ref.at[1]) + slab_product(wh_ref, b_ref.at[0], b_ref.at[1])
     rim = rim_product(wo_ref, f_ref) + rim_product(wl_ref, fl_ref) + rim_product(wh_ref, fh_ref)
     rim = rim.astype(BF16)
     parts = []
@@ -205,9 +213,34 @@
     lax.fori_loop(0, orb // 2, pair, 0)
 
 
+def move(value, axis, target):
+    count = lax.axis_size(axis)
+    return lax.ppermute(value, axis, [(i, target(i) % count) for i in range(count)])
+
+
 def ring(value, axis, step):
-    count = lax.axis_size(axis)
-    return lax.ppermute(value, axis, [(i, (i + step) % count) for i in range(count)])
+    return move(value, axis, lambda i: i + step)
+
+
+def pair(i):
+    return i ^ 1
+
+
+def relay(i, count):
+    if i & 1:
+        return i - 2 if i > 1 else 0
+    return i + 2 if i + 2 < count else count - 1
+
+
+def move_far(value):
+    atoms, energies = lax.axis_size("atom"), lax.axis_size("energy")
+    moves = []
+    for a in range(atoms):
+        b = a + 1 if a & 1 else a - 1
+        for e in range(energies):
+            target = (b, e) if 0 <= b < atoms else (a, (e ^ 1) % energies)
+            moves.append((a * energies + e, target[0] * energies + target[1]))
+    return lax.ppermute(value, ("atom", "energy"), moves)
 
 
 def per_device(bare_green, coupling_grad, neighbours, shifts, strength, occupation):
@@ -219,24 +252,16 @@
     period = span * LANES // math.gcd(span, LANES)
     vmem = pl.BlockSpec(memory_space=pltpu.VMEM)
     smem = pl.BlockSpec(memory_space=pltpu.SMEM)
-    big = pltpu.CompilerParams(vmem_limit_bytes=48 * 1024 * 1024)
+    big = pltpu.CompilerParams(vmem_limit_bytes=20 * 1024 * 1024)
 
     green = bare_green.reshape(2, rows, energies)
-    from_low = ring(green, "atom", 1)
-    from_high = ring(green, "atom", -1)
-
+    far = move_far(green)
+    near = move(green, "atom", pair)
     edge = pl.pallas_call(
         pack_kernel,
         out_shape=jax.ShapeDtypeStruct((2 * EDGE, rows), BF16),
-        in_specs=[vmem], out_specs=vmem, name="pack_edges",
+        in_specs=[vmem], out_specs=vmem, compiler_params=big, name="pack_edges",
     )(green)
-    edge_low = ring(edge, "energy", 1)
-    edge_high = ring(edge, "energy", -1)
-    high_side = (jnp.arange(2 * EDGE, dtype=jnp.int32)[:, None] & WIDTH) > 0
-    rim = jnp.where(high_side, edge_low, edge_high)
-    rim_low = ring(rim, "atom", 1)
-    rim_high = ring(rim, "atom", -1)
-
     grads = jnp.transpose(coupling_grad, (0, 1, 3, 2)).reshape(bonds * orb * atoms, orb)
     w_shape = jax.ShapeDtypeStruct((orb, span, cols), BF16)
     w_low, w_own, w_high, partial_sum, band, rim_band = pl.pallas_call(
@@ -255,6 +280,13 @@
         compiler_params=big, name="weights",
     )(grads, neighbours, green, shifts[None], strength[None], occupation[None])
 
+    rim = pl.pallas_call(
+        rim_kernel, out_shape=jax.ShapeDtypeStruct((2 * EDGE, rows), BF16),
+        in_specs=[vmem] * 3, out_specs=vmem, compiler_params=big, name="rim",
+    )(ring(edge, "energy", 1), ring(edge, "energy", -1), band)
+    rim_low = move(rim, "atom", pair)
+    rim_high = move_far(rim)
+
     full = (3, orb, span // 8, 8, energies)
     result = pl.pallas_call(
         functools.partial(final_kernel, orb, atoms),
@@ -267,7 +299,7 @@
             pltpu.VMEM((3, 2, orb, 8, energies), F32),
         ],
         compiler_params=big, name="green_update",
-    )(green, from_low, from_high, rim, rim_low, rim_high, w_low, w_own, w_high, partial_sum, band, rim_band)
+    )(green, far, near, rim, rim_low, rim_high, w_low, w_own, w_high, partial_sum, band, rim_band)
     return result.reshape(bare_green.shape)
 
 

time: 25.5 us -> 20.6 us (0.81)
  starting transfers between devices: 11.7 us -> 6.91 us
  waiting for transfers between devices: 1.77 us -> 4.13 us
  Pallas kernels: 10.1 us -> 8.34 us
  local copies, waits for them, and re-layouts: 1.58 us -> 1.01 us
    ppermute x6, starting transfers between devices: 11.7 us -> 6.91 us  [the longest x4 6.24 us: move(): lax.ppermute(value, axis, [(i, target(i) % count) for i in range(count)])]
    ppermute x6, waiting for transfers between devices: 1.77 us -> 4.13 us  [the longest x4 4.13 us: move(): lax.ppermute(value, axis, [(i, target(i) % count) for i in range(count)])]
    pallas_call x1, Pallas kernels: 1.84 us -> 0.18 us  [per_device(): pl.pallas_call(pack_kernel, out_shape=jax.ShapeDtypeStruct((2 * EDGE, row...]
    unnamed x12 -> x14, local copies, waits for them, and re-layouts: 1.58 us -> 1.01 us
  transfers between devices with their start and end apart: 6 -> 6, of which waited for: 1 -> 1; matrix products, arithmetic and copies ran while one was open for 0% -> 0% of each run, Pallas kernels for 17% -> 22%
where the time goes in v2:
time: 20.6 us; the launch traced here: 20.5 us
  Pallas kernels  8.34 us (40%)
  starting transfers between devices  6.91 us (34%)
  waiting for transfers between devices  4.13 us (20%)
  local copies, waits for them, and re-layouts  1.01 us (5%)
    ppermute x4, starting transfers between devices, move(): lax.ppermute(value, axis, [(i, target(i) % count) for i in range(count)])  6.24 us
    pallas_call x1, Pallas kernels, per_device(): pl.pallas_call(functools.partial(weights_kernel, orb), out_shape=[w_shape...  4.29 us
    ppermute x4, waiting for transfers between devices, move(): lax.ppermute(value, axis, [(i, target(i) % count) for i in range(count)])  4.13 us
    pallas_call x1, Pallas kernels, per_device(): pl.pallas_call(functools.partial(final_kernel, orb, atoms), out_shape=jax...  3.86 us
    unnamed x14, local copies, waits for them, and re-layouts  1.01 us
    ppermute x2, starting transfers between devices, move_far(): return lax.ppermute(value, ('atom', 'energy'), moves)  0.67 us
  transfers between devices with their start and end apart: 6, of which 1 were waited for; matrix products, arithmetic and copies ran while one was open for 0% of the time, Pallas kernels for 22%

profile of v2, /device:TPU:0, one launch (start us, length us, event | category | flops | bytes accessed | tf_op | source)
XLA Modules:
  0.0 20.5 jit_solution(7123938534670311655)
XLA Ops:
  0.0 2.9 %collective-permute-start.1 = (bf16[2,576,128]{2,1,0:T(8,128)(2,1)}, bf16[2,576,128]{2,1,0:T(8,128)(2,1)S(1)}, u32[]{:S(2)}, u32[]{:S(2)}) collective-permute-start(bf16[2,576,128]{2,1,0:T(8,128)(2,1)} %bitcast.8), channel_id=1, source_target_pairs={{0,4},{4,0},{8,12},{12,8},{16,20},{20,16},{24,28},{28,24},{1,5},{5... | collective-permute-start | bytes 884744 | tf_op jit(solution)/shard_map/ppermute | solution.py:218
  2.9 0.0 collective-permute-start
  2.9 0.0 copy-start
  2.9 1.0 %copy-done = bf16[2,12,12,4,128]{4,3,2,1,0:T(4,128)(2,1)S(1)} copy-done((bf16[2,12,12,4,128]{4,3,2,1,0:T(4,128)(2,1)S(1)}, bf16[2,12,12,4,128]{4,3,2,1,0:T(4,128)(2,1)}, u32[]{:S(2)}) %copy-start) | copy-done | bytes 294936
  3.9 0.0 copy-start.2
  3.9 0.0 copy-start.3
  3.9 0.0 copy-start.4
  3.9 0.0 copy-start.5
  3.9 0.0 copy-start.6
  4.0 0.2 pack_edges.1
  4.1 0.0 copy-start.1
  4.1 1.6 %collective-permute-start.3 = (bf16[16,576]{1,0:T(8,128)(2,1)S(1)}, bf16[16,576]{1,0:T(8,128)(2,1)S(1)}, u32[]{:S(2)}, u32[]{:S(2)}) collective-permute-start(bf16[16,576]{1,0:T(8,128)(2,1)S(1)} %pack_edges.1), channel_id=1, source_target_pairs={{0,3},{1,0},{2,1},{3,2},{4,7},{5,4},{6,5},{7,6},{8,11},{9,8},{10,9... | collective-permute-start | bytes 55304 | tf_op jit(solution)/shard_map/ppermute | solution.py:218
  5.8 0.0 collective-permute-start.2
  5.8 0.0 copy-done.2
  5.8 0.0 copy-done.3
  5.8 0.0 copy-done.4
  5.8 0.0 copy-done.5
  5.8 0.0 copy-done.6
  5.8 4.3 %weights.1 = (bf16[12,48,640]{2,1,0:T(8,128)(2,1)S(1)}, bf16[12,48,640]{2,1,0:T(8,128)(2,1)S(1)}, bf16[12,48,640]{2,1,0:T(8,128)(2,1)S(1)}, f32[576,256]{1,0:T(8...) custom-call(bf16[384,12]{1,0:T(8,128)(2,1)S(1)} %bitcast.13, s32[4,8]{1,0:T(4,128)S(1)} %copy-done.3, ...), custom_call_target="tpu_custom_call" | custom-call | tf_op jit(solution)/shard_map/weights/pallas_call | solution.py:267
  10.1 0.0 collective-permute-done.3.high_ref
  10.1 0.0 collective-permute-done.2.low_ref
  10.2 0.7 %collective-permute-start.5 = (bf16[16,576]{1,0:T(8,128)(2,1)S(1)}, bf16[16,576]{1,0:T(8,128)(2,1)S(1)}, u32[]{:S(2)}, u32[]{:S(2)}) collective-permute-start(bf16[16,576]{1,0:T(8,128)(2,1)S(1)} %rim.1.f_ref), channel_id=1, source_target_pairs={{0,1},{1,0},{2,3},{3,2},{4,8},{5,9},{6,10},{7,11},{8,4},{9,5},{10,... | collective-permute-start | bytes 55304 | tf_op jit(solution)/shard_map/ppermute | solution.py:243
  10.8 1.7 %collective-permute-start.4 = (bf16[16,576]{1,0:T(8,128)(2,1)S(1)}, bf16[16,576]{1,0:T(8,128)(2,1)S(1)}, u32[]{:S(2)}, u32[]{:S(2)}) collective-permute-start(bf16[16,576]{1,0:T(8,128)(2,1)S(1)} %rim.1.f_ref), channel_id=1, source_target_pairs={{0,4},{4,0},{8,12},{12,8},{16,20},{20,16},{24,28},{28,24},{1,5},{5... | collective-permute-start | bytes 55304 | tf_op jit(solution)/shard_map/ppermute | solution.py:218
  12.5 0.0 collective-permute-done.5.fh_ref
  12.5 4.1 %collective-permute-done.4.fl_ref = bf16[16,576]{1,0:T(8,128)(2,1)S(1)} collective-permute-done((bf16[16,576]{1,0:T(8,128)(2,1)S(1)}, bf16[16,576]{1,0:T(8,128)(2,1)S(1)}, u32[]{:S(2)}, u32[]{:S(2)}) %collective-permute-start.4) | collective-permute-done | bytes 18464 | tf_op jit(solution)/shard_map/ppermute | solution.py:218
  16.6 0.0 collective-permute-done.1.a_ref
  16.6 0.0 collective-permute-done.b_ref
  16.6 0.0 copy-done.1
  16.6 3.9 %green_update.1 = bf16[2,12,48,128]{3,2,1,0:T(8,128)(2,1)} custom-call(bf16[2,576,128]{2,1,0:T(8,128)(2,1)S(1)} %bitcast.12, bf16[2,576,128]{2,1,0:T(8,128)(2,1)S(1)} %collective-permute-done.b_ref, bf16[2,576,128]{2,1,0:T(8,128)(2,1)S(1)} %collective-permute-done.1.a_ref, bf16[16,576]{1,0:T(8,128)(2,1)S(1)} %rim.1.f_ref, ...), custom_call_target="tpu_custom_call" | custom-call | tf_op jit(solution)/shard_map/green_update/pallas_call | solution.py:291
  (1 shorter events, 0.0 us)
Async XLA Ops:
  0.0 16.6 %collective-permute-start.1 = (bf16[2,576,128]{2,1,0:T(8,128)(2,1)}, bf16[2,576,128]{2,1,0:T(8,128)(2,1)S(1)}, u32[]{:S(2)}, u32[]{:S(2)}) collective-permute-start(bf16[2,576,128]{2,1,0:T(8,128)(2,1)} %bitcast.8), channel_id=1, source_target_pairs={{0,4},{4,0},{8,12},{12,8},{16,20},{20,16},{24,28},{28,24},{1,5},{5... | collective-permute-start | bytes 884744 | tf_op jit(solution)/shard_map/ppermute | solution.py:218
  2.9 13.7 %collective-permute-start = (bf16[2,576,128]{2,1,0:T(8,128)(2,1)}, bf16[2,576,128]{2,1,0:T(8,128)(2,1)S(1)}, u32[]{:S(2)}, u32[]{:S(2)}) collective-permute-start(bf16[2,576,128]{2,1,0:T(8,128)(2,1)} %bitcast.9), channel_id=1, source_target_pairs={{0,1},{1,0},{2,3},{3,2},{4,8},{5,9},{6,10},{7,11},{8,4},{9,5},{10,... | collective-permute-start | bytes 884744 | tf_op jit(solution)/shard_map/ppermute | solution.py:243
  2.9 1.0 %copy-start = (bf16[2,12,12,4,128]{4,3,2,1,0:T(4,128)(2,1)S(1)}, bf16[2,12,12,4,128]{4,3,2,1,0:T(4,128)(2,1)}, u32[]{:S(2)}) copy-start(bf16[2,12,12,4,128]{4,3,2,1,0:T(4,128)(2,1)} %param.6) | copy-start | bytes 884740
  3.9 1.9 %copy-start.2 = (bf16[8,12,12,4]{2,3,1,0:T(4,128)(2,1)S(1)}, bf16[8,12,12,4]{2,3,1,0:T(4,128)(2,1)}, u32[]{:S(2)}) copy-start(bf16[8,12,12,4]{2,3,1,0:T(4,128)(2,1)} %param.7) | copy-start | bytes 27652
  3.9 1.9 %copy-start.3 = (s32[4,8]{1,0:T(4,128)S(1)}, s32[4,8]{1,0:T(4,128)}, u32[]{:S(2)}) copy-start(s32[4,8]{1,0:T(4,128)} %nbr_ref.1) | copy-start | bytes 388
  3.9 1.9 %copy-start.4 = (s32[32]{0:T(128)S(1)}, s32[32]{0:T(128)}, u32[]{:S(2)}) copy-start(s32[32]{0:T(128)} %param.9) | copy-start | bytes 388
  3.9 1.9 %copy-start.5 = (f32[32]{0:T(128)S(1)}, f32[32]{0:T(128)}, u32[]{:S(2)}) copy-start(f32[32]{0:T(128)} %param.10) | copy-start | bytes 388
  3.9 1.9 %copy-start.6 = (f32[32]{0:T(128)S(1)}, f32[32]{0:T(128)}, u32[]{:S(2)}) copy-start(f32[32]{0:T(128)} %param.11) | copy-start | bytes 388
  4.1 12.5 %copy-start.1 = (bf16[2,12,12,4,128]{4,3,2,1,0:T(4,128)(2,1)S(1)}, bf16[2,12,12,4,128]{4,3,2,1,0:T(4,128)(2,1)}, u32[]{:S(2)}) copy-start(bf16[2,12,12,4,128]{4,3,2,1,0:T(4,128)(2,1)} %param.6) | copy-start | bytes 884740
  4.1 6.0 %collective-permute-start.3 = (bf16[16,576]{1,0:T(8,128)(2,1)S(1)}, bf16[16,576]{1,0:T(8,128)(2,1)S(1)}, u32[]{:S(2)}, u32[]{:S(2)}) collective-permute-start(bf16[16,576]{1,0:T(8,128)(2,1)S(1)} %pack_edges.1), channel_id=1, source_target_pairs={{0,3},{1,0},{2,1},{3,2},{4,7},{5,4},{6,5},{7,6},{8,11},{9,8},{10,9... | collective-permute-start | bytes 55304 | tf_op jit(solution)/shard_map/ppermute | solution.py:218
  5.8 4.4 %collective-permute-start.2 = (bf16[16,576]{1,0:T(8,128)(2,1)S(1)}, bf16[16,576]{1,0:T(8,128)(2,1)S(1)}, u32[]{:S(2)}, u32[]{:S(2)}) collective-permute-start(bf16[16,576]{1,0:T(8,128)(2,1)S(1)} %pack_edges.1), channel_id=1, source_target_pairs={{0,1},{1,2},{2,3},{3,0},{4,5},{5,6},{6,7},{7,4},{8,9},{9,10},{10,1... | collective-permute-start | bytes 55304 | tf_op jit(solution)/shard_map/ppermute | solution.py:218
  10.2 2.3 %collective-permute-start.5 = (bf16[16,576]{1,0:T(8,128)(2,1)S(1)}, bf16[16,576]{1,0:T(8,128)(2,1)S(1)}, u32[]{:S(2)}, u32[]{:S(2)}) collective-permute-start(bf16[16,576]{1,0:T(8,128)(2,1)S(1)} %rim.1.f_ref), channel_id=1, source_target_pairs={{0,1},{1,0},{2,3},{3,2},{4,8},{5,9},{6,10},{7,11},{8,4},{9,5},{10,... | collective-permute-start | bytes 55304 | tf_op jit(solution)/shard_map/ppermute | solution.py:243
  10.8 5.8 %collective-permute-start.4 = (bf16[16,576]{1,0:T(8,128)(2,1)S(1)}, bf16[16,576]{1,0:T(8,128)(2,1)S(1)}, u32[]{:S(2)}, u32[]{:S(2)}) collective-permute-start(bf16[16,576]{1,0:T(8,128)(2,1)S(1)} %rim.1.f_ref), channel_id=1, source_target_pairs={{0,4},{4,0},{8,12},{12,8},{16,20},{20,16},{24,28},{28,24},{1,5},{5... | collective-permute-start | bytes 55304 | tf_op jit(solution)/shard_map/ppermute | solution.py:218

commit v3 on v2

v3 whole, which is shorter than its diff:
```python
import functools
import math
import jax
import jax.numpy as jnp
from jax import lax
from jax.experimental import pallas as pl
from jax.experimental.pallas import tpu as pltpu
from jax.sharding import PartitionSpec as P

WIDTH = 4
EDGE = 2 * WIDTH
LANES = 128
F32 = jnp.float32
BF16 = jnp.bfloat16


def iota(shape, axis):
    return lax.broadcasted_iota(jnp.int32, shape, axis)


def dot(a, b, dims=((1,), (0,))):
    return lax.dot_general(a, b, (dims, ((), ())), preferred_element_type=F32)


def steps_below(x, step, most):
    return sum((x >= step * m).astype(jnp.int32) for m in range(1, most))


def pack_kernel(orb, g_hbm, c_hbm, nbr_hbm, sh_hbm, st_hbm, oc_hbm,
                edge_ref, g_ref, c_ref, near_ref, sh_ref, st_ref, oc_ref, nbr_ref, sems):
    ends = ((g_hbm, g_ref), (nbr_hbm, nbr_ref), (c_hbm, c_ref), (sh_hbm, sh_ref), (st_hbm, st_ref), (oc_hbm, oc_ref))
    copies = [pltpu.make_async_copy(source, target, sems.at[i]) for i, (source, target) in enumerate(ends)]
    for copy in copies:
        copy.start()
    copies[0].wait()
    span = g_ref.shape[1] // orb
    lane = iota((span, LANES), 1)
    for r in range(2):
        total = jnp.zeros((span, LANES), F32)
        for k in range(orb):
            x = g_ref[r, k * span:(k + 1) * span].astype(F32)
            turned = pltpu.roll(x, EDGE * k + WIDTH, 1)
            total = jnp.where((lane >= EDGE * k) & (lane < EDGE * (k + 1)), turned, total)
        edge_ref[r * span:(r + 1) * span] = total.astype(BF16)
    copies[1].wait()
    atoms, bonds = nbr_ref.shape
    own = iota(near_ref.shape[1:], 0) & (atoms - 1)
    for n in range(bonds):
        near = jnp.zeros(near_ref.shape[1:], jnp.int32)
        for a in range(atoms):
            near = jnp.where(own == a, nbr_ref[a, n], near)
        near_ref[n] = near
    for copy in copies[2:]:
        copy.wait()


def join_kernel(low_ref, high_ref, g_ref, after_ref, out_ref, rim_ref):
    rows = g_ref.shape[1]
    rim = low_ref.shape[0]
    rest = (out_ref.shape[0] - rim) // 2
    for r in range(2):
        out_ref[r * rest:(r + 1) * rest] = g_ref[r, rows - rest:]
    below = (iota(low_ref.shape, 1) & WIDTH) == 0
    low, high = low_ref[...].astype(F32), high_ref[...].astype(F32)
    halo = jnp.where(below, low, high).astype(BF16)
    out_ref[2 * rest:] = halo
    rim_ref[...] = halo


def pass_kernel(x_ref, after_ref, out_ref):
    out_ref[...] = x_ref[:, :out_ref.shape[1]]


def band_weights(sh_ref, st_ref, oc_ref):
    shifts = sh_ref[...]
    emit = st_ref[...] * oc_ref[...]
    absorb = st_ref[...] * (oc_ref[...] + 1.0)
    zero = jnp.zeros_like(emit)
    weights = []
    for o in range(-WIDTH, WIDTH + 1):
        both = jnp.where(shifts == -o, emit, zero) + jnp.where(shifts == o, absorb, zero)
        weights.append(jnp.sum(both, axis=1, keepdims=True))
    return weights


def banded(weights, gap, keep=None):
    table = jnp.zeros(gap.shape, F32)
    for o in range(-WIDTH, WIDTH + 1):
        hit = gap == o
        if keep is not None:
            hit = hit & keep
        table = jnp.where(hit, weights[o + WIDTH], table)
    return table.astype(BF16)


def factors_kernel(orb, atoms, c_ref, near_ref, sh_ref, st_ref, oc_ref, t1_ref, t2_ref, table_ref):
    bonds = near_ref.shape[0]
    energies = table_ref.shape[2]
    span = orb * atoms
    cols = t1_ref.shape[3]
    period = t2_ref.shape[4]
    here = lax.axis_index("atom")
    place = lax.axis_index("energy")
    last = lax.axis_size("energy") - 1

    weights = band_weights(sh_ref, st_ref, oc_ref)
    band = banded(weights, iota((energies, energies), 0) - iota((energies, energies), 1))
    rim = (LANES, energies)
    row = iota(rim, 0)
    spot = row & (EDGE - 1)
    below = spot < WIDTH
    keep = jnp.where(below, jnp.where(place > 0, 1, 0), jnp.where(place < last, 1, 0)) > 0
    edge = banded(weights, jnp.where(below, spot - WIDTH, spot - WIDTH + energies) - iota(rim, 1), keep)
    for k in range(orb):
        table_ref[k, :energies] = band
        table_ref[k, energies:] = jnp.where((row >= EDGE * k) & (row < EDGE * (k + 1)), edge, jnp.zeros_like(edge))

    c = c_ref[...]
    krow, klane = iota((orb, cols), 0), iota((orb, cols), 1)
    spread = ((klane >= krow * span) & (klane < (krow + 1) * span)).astype(F32).astype(BF16)
    left = dot(c, spread).reshape(bonds * orb * atoms // 8, 8, cols)
    turned = pltpu.roll(left, atoms, 1)
    upper = iota(left.shape, 1) < atoms
    first = jnp.where(upper, left, turned)
    second = jnp.where(upper, turned, left)
    both = jnp.stack([first, second], axis=1).reshape(bonds, orb, 8, cols)
    t1_ref[...] = jnp.concatenate([both, both], axis=2).astype(BF16)

    lrow, llane = iota((orb, period), 0), iota((orb, period), 1)
    inner = llane - span * steps_below(llane, span, period // span)
    spread = ((inner >= lrow * atoms) & (inner < (lrow + 1) * atoms)).astype(F32).astype(BF16)
    right = dot(c, spread).reshape(bonds, span // 16, 16, period)
    odd = here & 1
    base = (here + 1 - 2 * odd, here, here - 1 + 2 * odd)
    other = iota((16, period), 1) & (atoms - 1)
    for n in range(bonds):
        near = jnp.concatenate([near_ref[n]] * (period // LANES), axis=1)
        for s in range(3):
            mask = near == other + base[s] * atoms
            t2_ref[s, n] = jnp.where(mask[None], right[n], 0.0).astype(BF16)


def weights_kernel(orb, atoms, t1_ref, t2_ref, table_ref, g_ref, rim_ref, wl_ref, wo_ref, wh_ref, s_ref, gn_ref, gd_ref):
    bonds = t1_ref.shape[0]
    span = orb * atoms
    tiles = t1_ref.shape[3] // LANES
    period = t2_ref.shape[4]
    gr = g_ref[0].astype(F32)
    gi = g_ref[1].astype(F32)
    for c, x in enumerate((gr, gi, gr + gi)):
        gn_ref[c] = x.reshape(gn_ref.shape[1:])
        gd_ref[c] = doubled(x, orb, atoms)

    for t in range(tiles):
        at = slice(t * LANES, (t + 1) * LANES)
        start = (t * LANES) % period
        cut = slice(start, start + LANES)

        def body(i, carry):
            x = t1_ref[:, i, :, at]
            for s, out in enumerate((wl_ref, wo_ref, wh_ref)):
                for q in range(span // 16):
                    total = x[0] * t2_ref[s, 0, q, :, cut]
                    for n in range(1, bonds):
                        total = total + x[n] * t2_ref[s, n, q, :, cut]
                    out[i, q * 16:(q + 1) * 16, at] = total
            return carry

        lax.fori_loop(0, orb, body, 0)

    s_ref[...] = slab_products([wo_ref], [whole(g_ref, orb)], [rim_ref[...]], table_ref)


def rim_of(join_ref, span):
    return join_ref[join_ref.shape[0] - 2 * span:]


def whole(ref, orb):
    return [[(ref.at[0], k), (ref.at[1], k)] for k in range(orb)]


def joined(first_ref, join_ref, orb, span):
    early = first_ref.shape[1] // span
    late = orb - early
    blocks = [[(first_ref.at[0], k), (first_ref.at[1], k)] for k in range(early)]
    return blocks + [[(join_ref, k), (join_ref, late + k)] for k in range(late)]


def slab_products(w_refs, slabs, rims, table_ref):
    orb = len(slabs[0])
    span = rims[0].shape[0] // 2
    rims = jnp.concatenate(rims, axis=0)
    summed = []
    for k in range(orb):
        body = jnp.concatenate([ref[i * span:(i + 1) * span] for slab in slabs for ref, i in slab[k]], axis=0)
        summed.append(dot(jnp.concatenate([body, rims], axis=1), table_ref[k]).astype(BF16))
    total = None
    for s, w_ref in enumerate(w_refs):
        at = 2 * s * span
        right = jnp.concatenate(
            [jnp.concatenate([x[at:at + span], x[at + span:at + 2 * span]], axis=1) for x in summed], axis=0)
        rows = right.shape[0]
        w = w_ref[...].reshape(rows, w_ref.shape[2])[:, :rows]
        part = dot(w, right)
        total = part if total is None else total + part
    return total


def doubled(x, orb, atoms):
    pairs = x.reshape(orb * orb * atoms // 8, 8, x.shape[1])
    turned = pltpu.roll(pairs, atoms, 1)
    upper = iota(pairs.shape, 1) < atoms
    first = jnp.where(upper, pairs, turned)
    second = jnp.where(upper, turned, pairs)
    return jnp.stack([first, second], axis=1).reshape(orb, orb, 8, x.shape[1])


def final_kernel(orb, atoms, near_ref, rim_ref, ff_ref, fj_ref, wn_ref, wf_ref, s_ref, table_ref, gn_ref, gd_ref,
                 out_ref, sn_ref, ld_ref):
    energies = table_ref.shape[2]
    span = orb * atoms
    groups = span // 8
    slabs = [whole(near_ref, orb), joined(ff_ref, fj_ref, orb, span)]
    rims = [rim_ref[...], rim_of(fj_ref, span)]
    total = s_ref[...] + slab_products([wn_ref, wf_ref], slabs, rims, table_ref)
    re, im = total[:, :energies], total[:, energies:]
    for c, x in enumerate((re, im, re + im)):
        sn_ref[c] = x.reshape(orb, groups, 8, energies)

    def product(left, right_ref, acc):
        for k in range(orb):
            for c in range(3):
                right = right_ref[c, k]
                for d in range(2):
                    term = left(c, d, k)[None] * right
                    acc[c][d] = term if acc[c][d] is None else acc[c][d] + term
        return acc

    def pair(p, carry):
        m = product(lambda c, d, k: gd_ref[c, 2 * p + d, k], sn_ref, [[None, None] for _ in range(3)])
        upper = iota((groups, 8, energies), 1) < atoms
        for d in range(2):
            lr = m[0][d] - m[1][d]
            li = m[2][d] - (m[0][d] + m[1][d])
            for c, x in enumerate((lr, li, lr + li)):
                turned = pltpu.roll(x, atoms, 1)
                first = jnp.where(upper, x, turned)
                second = jnp.where(upper, turned, x)
                ld_ref[c, d] = jnp.stack([first, second], axis=1).reshape(orb, 8, energies)
        m = product(lambda c, d, k: ld_ref[c, d, k], gn_ref, [[None, None] for _ in range(3)])
        for d in range(2):
            i = 2 * p + d
            ur = gn_ref[0, i] + (m[0][d] - m[1][d])
            ui = gn_ref[1, i] + (m[2][d] - (m[0][d] + m[1][d]))
            out_ref[0, i] = ur.reshape(orb * atoms, energies).astype(BF16)
            out_ref[1, i] = ui.reshape(orb * atoms, energies).astype(BF16)
        return carry

    lax.fori_loop(0, orb // 2, pair, 0)


def move(value, axis, target):
    count = lax.axis_size(axis)
    return lax.ppermute(value, axis, [(i, target(i) % count) for i in range(count)])


def ring(value, axis, step):
    return move(value, axis, lambda i: i + step)


def pair(i):
    return i ^ 1


def relay(i, count):
    if i & 1:
        return i - 2 if i > 1 else 0
    return i + 2 if i + 2 < count else count - 1


def move_far(value):
    atoms, energies = lax.axis_size("atom"), lax.axis_size("energy")
    moves = []
    for a in range(atoms):
        b = a + 1 if a & 1 else a - 1
        for e in range(energies):
            target = (b, e) if 0 <= b < atoms else (a, (e ^ 1) % energies)
            moves.append((a * energies + e, target[0] * energies + target[1]))
    return lax.ppermute(value, ("atom", "energy"), moves)


def per_device(bare_green, coupling_grad, neighbours, shifts, strength, occupation):
    _, orb, _, atoms, energies = bare_green.shape
    bonds = coupling_grad.shape[0]
    rows = orb * orb * atoms
    span = orb * atoms
    cols = -(-rows // LANES) * LANES
    period = span * LANES // math.gcd(span, LANES)
    early = orb // 3
    late = 2 * (orb - early) * span + 2 * span
    vmem = pl.BlockSpec(memory_space=pltpu.VMEM)
    smem = pl.BlockSpec(memory_space=pltpu.SMEM)
    small = pltpu.CompilerParams(vmem_limit_bytes=20 * 1024 * 1024)

    def shape(*dims, kind=BF16):
        return jax.ShapeDtypeStruct(dims, kind)

    def call(kernel, name, out_shape, *operands, scratch=(), scalars=()):
        return pl.pallas_call(
            kernel, out_shape=out_shape, name=name,
            in_specs=[smem if i in scalars else vmem for i in range(len(operands))],
            out_specs=jax.tree.map(lambda _: vmem, out_shape),
            scratch_shapes=scratch, compiler_params=small,
        )(*operands)

    green = bare_green.reshape(2, rows, energies)
    near = move(green, "atom", pair)
    grads = jnp.transpose(coupling_grad, (0, 1, 3, 2)).reshape(bonds * orb * atoms, orb)
    phonons = [x[None] for x in (shifts, strength, occupation)]
    fetched = [pltpu.with_memory_space_constraint(x, pltpu.HBM) for x in (green, grads, neighbours, *phonons)]
    edge, held, grads, near_atoms, *phonons = pl.pallas_call(
        functools.partial(pack_kernel, orb), name="pack",
        out_shape=[shape(2 * span, LANES), shape(2, rows, energies), shape(*grads.shape),
                   shape(bonds, 16, LANES, kind=jnp.int32)] + [shape(*x.shape, kind=x.dtype) for x in phonons],
        in_specs=[pl.BlockSpec(memory_space=pltpu.HBM)] * 6, out_specs=[vmem] * 7,
        scratch_shapes=[pltpu.SMEM(neighbours.shape, jnp.int32), pltpu.SemaphoreType.DMA((6,))],
        compiler_params=small,
    )(*fetched)
    left, right, table = call(
        functools.partial(factors_kernel, orb, atoms), "factors",
        [shape(bonds, orb, 16, cols), shape(3, bonds, span // 16, 16, period), shape(orb, energies + LANES, energies)],
        grads, near_atoms, *phonons)
    join, rim = call(
        join_kernel, "join", [shape(late, energies), shape(2 * span, LANES)],
        ring(edge, "energy", 1), ring(edge, "energy", -1), held, table)
    far_join = move_far(join)
    rim_near = move(rim, "atom", pair)
    passed = call(pass_kernel, "pass", shape(2, early * span, energies), near, join)
    far_first = move(passed, "atom", lambda i: relay(i, lax.axis_size("atom")))
    weight = shape(orb, span, cols)
    plain = shape(3, orb, span // 8, 8, energies, kind=F32)
    w_near, w_own, w_far, own, gn, gd = call(
        functools.partial(weights_kernel, orb, atoms), "weights",
        [weight, weight, weight, shape(rows, 2 * energies, kind=F32),
         plain, shape(3, orb, orb, 8, energies, kind=F32)],
        left, right, table, held, rim)

    result = call(
        functools.partial(final_kernel, orb, atoms), "green_update", shape(2, orb, span, energies),
        near, rim_near, far_first, far_join, w_near, w_far, own, table, gn, gd,
        scratch=[pltpu.VMEM(plain.shape, F32), pltpu.VMEM((3, 2, orb, 8, energies), F32)])
    return result.reshape(bare_green.shape)


def solution(mesh):
    placed = (
        P(None, None, None, "atom", "energy"),
        P(None, None, None, "atom"),
        P("atom", None),
        P(),
        P(),
        P(),
    )
    return jax.shard_map(
        per_device,
        mesh=mesh,
        in_specs=placed,
        out_specs=P(None, None, None, "atom", "energy"),
        check_vma=False,
    )
```

time: 20.6 us -> 19.6 us (0.951)
  waiting for transfers between devices: 4.13 us -> 1.56 us
  starting transfers between devices: 6.91 us -> 8.79 us
  local copies, waits for them, and re-layouts: 1.01 us -> 0 us
  Pallas kernels: 8.34 us -> 9.03 us
    ppermute x4 -> x5, waiting for transfers between devices: 4.13 us -> 1.56 us  [move(): lax.ppermute(value, axis, [(i, target(i) % count) for i in range(count)])]
    ppermute x2 -> x1, starting transfers between devices: 0.67 us -> 1.98 us  [move_far(): return lax.ppermute(value, ('atom', 'energy'), moves)]
    unnamed x14 -> x0, local copies, waits for them, and re-layouts: 1.01 us -> none
    pallas_call x4 -> x6, Pallas kernels: 8.34 us -> 9.03 us  [the longest x5 7.81 us: call(): pl.pallas_call(kernel, out_shape=out_shape, name=name, in_specs=[smem if...]
    ppermute x4 -> x5, starting transfers between devices: 6.24 us -> 6.81 us  [move(): lax.ppermute(value, axis, [(i, target(i) % count) for i in range(count)])]
  transfers between devices with their start and end apart: 6 -> 6, of which waited for: 1 -> 2; matrix products, arithmetic and copies ran while one was open for 0% -> 0% of each run, Pallas kernels for 22% -> 29%
where the time goes in v3:
time: 19.6 us; the launch traced here: 19.4 us
  Pallas kernels  9.03 us (46%)
  starting transfers between devices  8.79 us (45%)
  waiting for transfers between devices  1.56 us (8%)
    pallas_call x5, Pallas kernels, call(): pl.pallas_call(kernel, out_shape=out_shape, name=name, in_specs=[smem if...  7.81 us
    ppermute x5, starting transfers between devices, move(): lax.ppermute(value, axis, [(i, target(i) % count) for i in range(count)])  6.81 us
    ppermute x1, starting transfers between devices, move_far(): return lax.ppermute(value, ('atom', 'energy'), moves)  1.98 us
    ppermute x5, waiting for transfers between devices, move(): lax.ppermute(value, axis, [(i, target(i) % count) for i in range(count)])  1.56 us
    pallas_call x1, Pallas kernels, per_device(): pl.pallas_call(functools.partial(pack_kernel, orb), name='pack', out_shap...  1.23 us
  transfers between devices with their start and end apart: 6, of which 2 were waited for; matrix products, arithmetic and copies ran while one was open for 0% of the time, Pallas kernels for 29%

profile of v3, /device:TPU:0, one launch (start us, length us, event | category | flops | bytes accessed | tf_op | source)
XLA Modules:
  0.0 19.4 jit_solution(6385038647355374497)
XLA Ops:
  0.0 2.9 %collective-permute-start = (bf16[2,576,128]{2,1,0:T(8,128)(2,1)}, bf16[2,576,128]{2,1,0:T(8,128)(2,1)S(1)}, u32[]{:S(2)}, u32[]{:S(2)}) collective-permute-start(bf16[2,576,128]{2,1,0:T(8,128)(2,1)} %bitcast.8), channel_id=1, source_target_pairs={{0,4},{4,0},{8,12},{12,8},{16,20},{20,16},{24,28},{28,24},{1,5},{5... | collective-permute-start | bytes 884744 | tf_op jit(solution)/shard_map/ppermute | solution.py:264
  2.9 1.2 %pack.1 = (bf16[96,128]{1,0:T(8,128)(2,1)S(1)}, bf16[2,576,128]{2,1,0:T(8,128)(2,1)S(1)}, bf16[384,12]{1,0:T(8,128)(2,1)S(1)}, s32[8,16,128]{2,1,0:T(8,128)S(1)}...) custom-call(bf16[2,576,128]{2,1,0:T(8,128)(2,1)} %bitcast.9, bf16[384,12]{1,0:T(8,128)(2,1)} %bitcast.10, ...), custom_call_target="tpu_custom_call" | custom-call | tf_op jit(solution)/shard_map/pack/pallas_call | solution.py:321
  4.2 0.1 collective-permute-start.1
  4.2 1.7 %collective-permute-start.2 = (bf16[96,128]{1,0:T(8,128)(2,1)S(1)}, bf16[96,128]{1,0:T(8,128)(2,1)S(1)}, u32[]{:S(2)}, u32[]{:S(2)}) collective-permute-start(bf16[96,128]{1,0:T(8,128)(2,1)S(1)} %get-tuple-element.22), channel_id=1, source_target_pairs={{0,3},{1,0},{2,1},{3,2},{4,7},{5,4},{6,5},{7,6},{8,11},{9,8},{10,9... | collective-permute-start | bytes 73736 | tf_op jit(solution)/shard_map/ppermute | solution.py:264
  6.0 0.6 %factors.1 = (bf16[8,12,16,640]{3,2,1,0:T(8,128)(2,1)S(1)}, bf16[3,8,3,16,384]{4,3,2,1,0:T(8,128)(2,1)S(1)}, bf16[12,256,128]{2,1,0:T(8,128)(2,1)S(1)}) custom-call(bf16[384,12]{1,0:T(8,128)(2,1)S(1)} %get-tuple-element.24.c_ref, s32[8,16,128]{2,1,0:T(8,128)S(1)} %get-tuple-element.25.near_ref, s32[1,32]{1,0:T(1,128)S(1)} %get-tuple-element.26.sh_ref, ...), custom_call_target="tpu_custom_call" | custom-call | tf_op jit(solution)/shard_map/factors/pallas_call | solution.py:309
  6.6 0.9 %collective-permute-done.1.low_ref = bf16[96,128]{1,0:T(8,128)(2,1)S(1)} collective-permute-done((bf16[96,128]{1,0:T(8,128)(2,1)S(1)}, bf16[96,128]{1,0:T(8,128)(2,1)S(1)}, u32[]{:S(2)}, u32[]{:S(2)}) %collective-permute-start.1) | collective-permute-done | bytes 24608 | tf_op jit(solution)/shard_map/ppermute | solution.py:264
  7.5 0.0 collective-permute-done.2.high_ref
  7.5 2.0 %collective-permute-start.5 = (bf16[864,128]{1,0:T(8,128)(2,1)S(1)}, bf16[864,128]{1,0:T(8,128)(2,1)S(1)}, u32[]{:S(2)}, u32[]{:S(2)}) collective-permute-start(bf16[864,128]{1,0:T(8,128)(2,1)S(1)} %get-tuple-element.31.after_ref), channel_id=1, source_target_pairs={{0,1},{1,0},{2,3},{3,2},{4,8},{5,9},{6,10},{7,11},{8,4},{9,5},{10,... | collective-permute-start | bytes 663560 | tf_op jit(solution)/shard_map/ppermute | solution.py:289
  9.5 0.7 %collective-permute-done.x_ref.near_ref = bf16[2,576,128]{2,1,0:T(8,128)(2,1)S(1)} collective-permute-done((bf16[2,576,128]{2,1,0:T(8,128)(2,1)}, bf16[2,576,128]{2,1,0:T(8,128)(2,1)S(1)}, u32[]{:S(2)}, u32[]{:S(2)}) %collective-permute-start) | collective-permute-done | bytes 294944 | tf_op jit(solution)/shard_map/ppermute | solution.py:264
  10.2 1.9 %collective-permute-start.4 = (bf16[2,192,128]{2,1,0:T(8,128)(2,1)S(1)}, bf16[2,192,128]{2,1,0:T(8,128)(2,1)S(1)}, u32[]{:S(2)}, u32[]{:S(2)}) collective-permute-start(bf16[2,192,128]{2,1,0:T(8,128)(2,1)S(1)} %pass.1), channel_id=1, source_target_pairs={{0,8},{4,0},{8,16},{12,4},{16,24},{20,12},{24,28},{28,20},{1,9},{5... | collective-permute-start | bytes 294920 | tf_op jit(solution)/shard_map/ppermute | solution.py:264
  12.0 0.2 %collective-permute-start.3 = (bf16[96,128]{1,0:T(8,128)(2,1)S(1)}, bf16[96,128]{1,0:T(8,128)(2,1)S(1)}, u32[]{:S(2)}, u32[]{:S(2)}) collective-permute-start(bf16[96,128]{1,0:T(8,128)(2,1)S(1)} %get-tuple-element.30.rim_ref), channel_id=1, source_target_pairs={{0,4},{4,0},{8,12},{12,8},{16,20},{20,16},{24,28},{28,24},{1,5},{5... | collective-permute-start | bytes 73736 | tf_op jit(solution)/shard_map/ppermute | solution.py:264
  12.2 3.8 %weights.1 = (bf16[12,48,640]{2,1,0:T(8,128)(2,1)S(1)}, bf16[12,48,640]{2,1,0:T(8,128)(2,1)}, bf16[12,48,640]{2,1,0:T(8,128)(2,1)S(1)}, f32[576,256]{1,0:T(8,128...) custom-call(bf16[8,12,16,640]{3,2,1,0:T(8,128)(2,1)S(1)} %get-tuple-element.32.t1_ref, ...), custom_call_target="tpu_custom_call" | custom-call | tf_op jit(solution)/shard_map/weights/pallas_call | solution.py:309
  16.0 0.0 collective-permute-done.3.rim_ref
  16.0 0.0 collective-permute-done.5.fj_ref
  16.0 0.0 collective-permute-done.4.ff_ref
  16.1 3.4 %green_update.1 = bf16[2,12,48,128]{3,2,1,0:T(8,128)(2,1)} custom-call(bf16[2,576,128]{2,1,0:T(8,128)(2,1)S(1)} %collective-permute-done.x_ref.near_ref, bf16[96,128]{1,0:T(8,128)(2,1)S(1)} %collective-permute-done.3.rim_ref, bf16[2,192,128]{2,1,0:T(8,128)(2,1)S(1)} %collective-permute-done.4.ff_ref, bf16[864,128]{1,0:T(8,128)(2,1)S(1)} %collective-permute-done.5.fj_ref, ...), custom_call_target="tpu_custom_call" | custom-call | tf_op jit(solution)/shard_map/green_update/pallas_call | solution.py:309
  (2 shorter events, 0.0 us)
Async XLA Ops:
  0.0 10.2 %collective-permute-start = (bf16[2,576,128]{2,1,0:T(8,128)(2,1)}, bf16[2,576,128]{2,1,0:T(8,128)(2,1)S(1)}, u32[]{:S(2)}, u32[]{:S(2)}) collective-permute-start(bf16[2,576,128]{2,1,0:T(8,128)(2,1)} %bitcast.8), channel_id=1, source_target_pairs={{0,4},{4,0},{8,12},{12,8},{16,20},{20,16},{24,28},{28,24},{1,5},{5... | collective-permute-start | bytes 884744 | tf_op jit(solution)/shard_map/ppermute | solution.py:264
  4.2 3.3 %collective-permute-start.1 = (bf16[96,128]{1,0:T(8,128)(2,1)S(1)}, bf16[96,128]{1,0:T(8,128)(2,1)S(1)}, u32[]{:S(2)}, u32[]{:S(2)}) collective-permute-start(bf16[96,128]{1,0:T(8,128)(2,1)S(1)} %get-tuple-element.22), channel_id=1, source_target_pairs={{0,1},{1,2},{2,3},{3,0},{4,5},{5,6},{6,7},{7,4},{8,9},{9,10},{10,1... | collective-permute-start | bytes 73736 | tf_op jit(solution)/shard_map/ppermute | solution.py:264
  4.2 3.3 %collective-permute-start.2 = (bf16[96,128]{1,0:T(8,128)(2,1)S(1)}, bf16[96,128]{1,0:T(8,128)(2,1)S(1)}, u32[]{:S(2)}, u32[]{:S(2)}) collective-permute-start(bf16[96,128]{1,0:T(8,128)(2,1)S(1)} %get-tuple-element.22), channel_id=1, source_target_pairs={{0,3},{1,0},{2,1},{3,2},{4,7},{5,4},{6,5},{7,6},{8,11},{9,8},{10,9... | collective-permute-start | bytes 73736 | tf_op jit(solution)/shard_map/ppermute | solution.py:264
  7.5 8.5 %collective-permute-start.5 = (bf16[864,128]{1,0:T(8,128)(2,1)S(1)}, bf16[864,128]{1,0:T(8,128)(2,1)S(1)}, u32[]{:S(2)}, u32[]{:S(2)}) collective-permute-start(bf16[864,128]{1,0:T(8,128)(2,1)S(1)} %get-tuple-element.31.after_ref), channel_id=1, source_target_pairs={{0,1},{1,0},{2,3},{3,2},{4,8},{5,9},{6,10},{7,11},{8,4},{9,5},{10,... | collective-permute-start | bytes 663560 | tf_op jit(solution)/shard_map/ppermute | solution.py:289
  10.2 5.9 %collective-permute-start.4 = (bf16[2,192,128]{2,1,0:T(8,128)(2,1)S(1)}, bf16[2,192,128]{2,1,0:T(8,128)(2,1)S(1)}, u32[]{:S(2)}, u32[]{:S(2)}) collective-permute-start(bf16[2,192,128]{2,1,0:T(8,128)(2,1)S(1)} %pass.1), channel_id=1, source_target_pairs={{0,8},{4,0},{8,16},{12,4},{16,24},{20,12},{24,28},{28,20},{1,9},{5... | collective-permute-start | bytes 294920 | tf_op jit(solution)/shard_map/ppermute | solution.py:264
  12.0 4.0 %collective-permute-start.3 = (bf16[96,128]{1,0:T(8,128)(2,1)S(1)}, bf16[96,128]{1,0:T(8,128)(2,1)S(1)}, u32[]{:S(2)}, u32[]{:S(2)}) collective-permute-start(bf16[96,128]{1,0:T(8,128)(2,1)S(1)} %get-tuple-element.30.rim_ref), channel_id=1, source_target_pairs={{0,4},{4,0},{8,12},{12,8},{16,20},{20,16},{24,28},{28,24},{1,5},{5... | collective-permute-start | bytes 73736 | tf_op jit(solution)/shard_map/ppermute | solution.py:264

commit v4 on v3

--- a/solution.py
+++ b/solution.py
@@ -140,35 +140,40 @@
             t2_ref[s, n] = jnp.where(mask[None], right[n], 0.0).astype(BF16)
 
 
-def weights_kernel(orb, atoms, t1_ref, t2_ref, table_ref, g_ref, rim_ref, wl_ref, wo_ref, wh_ref, s_ref, gn_ref, gd_ref):
-    bonds = t1_ref.shape[0]
-    span = orb * atoms
-    tiles = t1_ref.shape[3] // LANES
-    period = t2_ref.shape[4]
+def weights_kernel(orb, atoms, t1_ref, t2_ref, g_ref, wn_ref, wo_ref, gn_ref, gd_ref):
     gr = g_ref[0].astype(F32)
     gi = g_ref[1].astype(F32)
     for c, x in enumerate((gr, gi, gr + gi)):
         gn_ref[c] = x.reshape(gn_ref.shape[1:])
         gd_ref[c] = doubled(x, orb, atoms)
-
-    for t in range(tiles):
+    fill(t1_ref, t2_ref, (wn_ref, wo_ref), 0)
+
+
+def others_kernel(orb, t1_ref, t2_ref, table_ref, g_ref, rim_ref, wo_ref, wf_ref, s_ref):
+    fill(t1_ref, t2_ref, (wf_ref,), 2)
+    s_ref[...] = slab_products([wo_ref], [whole(g_ref, orb)], [rim_ref[...]], table_ref)
+
+
+def fill(t1_ref, t2_ref, outs, first):
+    bonds, orb = t1_ref.shape[:2]
+    groups, period = t2_ref.shape[2], t2_ref.shape[4]
+    for t in range(t1_ref.shape[3] // LANES):
         at = slice(t * LANES, (t + 1) * LANES)
         start = (t * LANES) % period
         cut = slice(start, start + LANES)
-
-        def body(i, carry):
-            x = t1_ref[:, i, :, at]
-            for s, out in enumerate((wl_ref, wo_ref, wh_ref)):
-                for q in range(span // 16):
-                    total = x[0] * t2_ref[s, 0, q, :, cut]
+        for s, out in enumerate(outs):
+            held = [[t2_ref[s + first, n, q, :, cut] for n in range(bonds)] for q in range(groups)]
+
+            def body(i, carry):
+                x = [t1_ref[n, i, :, at] for n in range(bonds)]
+                for q in range(groups):
+                    total = x[0] * held[q][0]
                     for n in range(1, bonds):
-                        total = total + x[n] * t2_ref[s, n, q, :, cut]
+                        total = total + x[n] * held[q][n]
                     out[i, q * 16:(q + 1) * 16, at] = total
-            return carry
-
-        lax.fori_loop(0, orb, body, 0)
-
-    s_ref[...] = slab_products([wo_ref], [whole(g_ref, orb)], [rim_ref[...]], table_ref)
+                return carry
+
+            lax.fori_loop(0, orb, body, 0, unroll=orb)
 
 
 def rim_of(join_ref, span):
@@ -179,10 +184,11 @@
     return [[(ref.at[0], k), (ref.at[1], k)] for k in range(orb)]
 
 
-def joined(first_ref, join_ref, orb, span):
-    early = first_ref.shape[1] // span
-    late = orb - early
-    blocks = [[(first_ref.at[0], k), (first_ref.at[1], k)] for k in range(early)]
+def joined(parts, join_ref, orb, span):
+    blocks = []
+    for ref in parts:
+        blocks += [[(ref.at[0], k), (ref.at[1], k)] for k in range(ref.shape[1] // span)]
+    late = orb - len(blocks)
     return blocks + [[(join_ref, k), (join_ref, late + k)] for k in range(late)]
 
 
@@ -216,11 +222,11 @@
 
 
 def final_kernel(orb, atoms, near_ref, rim_ref, ff_ref, fj_ref, wn_ref, wf_ref, s_ref, table_ref, gn_ref, gd_ref,
-                 out_ref, sn_ref, ld_ref):
+                 out_hbm, sn_ref, ld_ref, out_ref, sems):
     energies = table_ref.shape[2]
     span = orb * atoms
     groups = span // 8
-    slabs = [whole(near_ref, orb), joined(ff_ref, fj_ref, orb, span)]
+    slabs = [whole(near_ref, orb), joined((ff_ref,), fj_ref, orb, span)]
     rims = [rim_ref[...], rim_of(fj_ref, span)]
     total = s_ref[...] + slab_products([wn_ref, wf_ref], slabs, rims, table_ref)
     re, im = total[:, :energies], total[:, energies:]
@@ -235,6 +241,10 @@
                     term = left(c, d, k)[None] * right
                     acc[c][d] = term if acc[c][d] is None else acc[c][d] + term
         return acc
+
+    def sent(p):
+        at = pl.ds(2 * p, 2)
+        return pltpu.make_async_copy(out_ref.at[:, at], out_hbm.at[:, at], sems.at[p])
 
     def pair(p, carry):
         m = product(lambda c, d, k: gd_ref[c, 2 * p + d, k], sn_ref, [[None, None] for _ in range(3)])
@@ -254,9 +264,12 @@
             ui = gn_ref[1, i] + (m[2][d] - (m[0][d] + m[1][d]))
             out_ref[0, i] = ur.reshape(orb * atoms, energies).astype(BF16)
             out_ref[1, i] = ui.reshape(orb * atoms, energies).astype(BF16)
+        sent(p).start()
         return carry
 
-    lax.fori_loop(0, orb // 2, pair, 0)
+    lax.fori_loop(0, orb // 2, pair, 0, unroll=1)
+    for p in range(orb // 2):
+        sent(p).wait()
 
 
 def move(value, axis, target):
@@ -328,8 +341,14 @@
     )(*fetched)
     left, right, table = call(
         functools.partial(factors_kernel, orb, atoms), "factors",
-        [shape(bonds, orb, 16, cols), shape(3, bonds, span // 16, 16, period), shape(orb, energies + LANES, energies)],
+        [shape(bonds, orb, 16, cols), shape(3, bonds, span // 16, 16, period),
+         shape(orb, energies + LANES, energies)],
         grads, near_atoms, *phonons)
+    weight = shape(orb, span, cols)
+    plain = shape(3, orb, span // 8, 8, energies, kind=F32)
+    w_near, w_own, gn, gd = call(
+        functools.partial(weights_kernel, orb, atoms), "weights",
+        [weight, weight, plain, shape(3, orb, orb, 8, energies, kind=F32)], left, right, held)
     join, rim = call(
         join_kernel, "join", [shape(late, energies), shape(2 * span, LANES)],
         ring(edge, "energy", 1), ring(edge, "energy", -1), held, table)
@@ -337,18 +356,19 @@
     rim_near = move(rim, "atom", pair)
     passed = call(pass_kernel, "pass", shape(2, early * span, energies), near, join)
     far_first = move(passed, "atom", lambda i: relay(i, lax.axis_size("atom")))
-    weight = shape(orb, span, cols)
-    plain = shape(3, orb, span // 8, 8, energies, kind=F32)
-    w_near, w_own, w_far, own, gn, gd = call(
-        functools.partial(weights_kernel, orb, atoms), "weights",
-        [weight, weight, weight, shape(rows, 2 * energies, kind=F32),
-         plain, shape(3, orb, orb, 8, energies, kind=F32)],
-        left, right, table, held, rim)
-
-    result = call(
-        functools.partial(final_kernel, orb, atoms), "green_update", shape(2, orb, span, energies),
-        near, rim_near, far_first, far_join, w_near, w_far, own, table, gn, gd,
-        scratch=[pltpu.VMEM(plain.shape, F32), pltpu.VMEM((3, 2, orb, 8, energies), F32)])
+    w_far, own = call(
+        functools.partial(others_kernel, orb), "others", [weight, shape(rows, 2 * energies, kind=F32)],
+        left, right, table, held, rim, w_own)
+
+    result = pl.pallas_call(
+        functools.partial(final_kernel, orb, atoms), name="green_update",
+        out_shape=shape(2, orb, span, energies),
+        in_specs=[vmem] * 10, out_specs=pl.BlockSpec(memory_space=pltpu.HBM),
+        scratch_shapes=[
+            pltpu.VMEM(plain.shape, F32), pltpu.VMEM((3, 2, orb, 8, energies), F32),
+            pltpu.VMEM((2, orb, span, energies), BF16), pltpu.SemaphoreType.DMA((orb // 2,))],
+        compiler_params=small,
+    )(near, rim_near, far_first, far_join, w_near, w_far, own, table, gn, gd)
     return result.reshape(bare_green.shape)
 
 

time: 19.6 us -> 19.3 us (0.985)
  Pallas kernels: 9.03 us -> 7.99 us
  waiting for transfers between devices: 1.56 us -> 2.21 us
    pallas_call x5, Pallas kernels: 7.81 us -> 3.62 us  [call(): pl.pallas_call(kernel, out_shape=out_shape, name=name, in_specs=[smem if...]
    pallas_call x0 -> x1, Pallas kernels: none -> 3.15 us  [per_device(): pl.pallas_call(functools.partial(final_kernel, orb, atoms), name='green_u...]
    ppermute x5, waiting for transfers between devices: 1.56 us -> 2.2 us  [move(): lax.ppermute(value, axis, [(i, target(i) % count) for i in range(count)])]
  transfers between devices with their start and end apart: 6 -> 6, of which waited for: 2 -> 3; matrix products, arithmetic and copies ran while one was open for 0% -> 0% of each run, Pallas kernels for 29% -> 25%
where the time goes in v4:
time: 19.3 us; the launch traced here: 19 us
  starting transfers between devices  8.79 us (46%)
  Pallas kernels  7.99 us (41%)
  waiting for transfers between devices  2.21 us (11%)
    ppermute x5, starting transfers between devices, move(): lax.ppermute(value, axis, [(i, target(i) % count) for i in range(count)])  6.81 us
    pallas_call x5, Pallas kernels, call(): pl.pallas_call(kernel, out_shape=out_shape, name=name, in_specs=[smem if...  3.62 us
    pallas_call x1, Pallas kernels, per_device(): pl.pallas_call(functools.partial(final_kernel, orb, atoms), name='green_u...  3.15 us
    ppermute x5, waiting for transfers between devices, move(): lax.ppermute(value, axis, [(i, target(i) % count) for i in range(count)])  2.2 us
    ppermute x1, starting transfers between devices, move_far(): return lax.ppermute(value, ('atom', 'energy'), moves)  1.98 us
    pallas_call x1, Pallas kernels, per_device(): pl.pallas_call(functools.partial(pack_kernel, orb), name='pack', out_shap...  1.23 us
  transfers between devices with their start and end apart: 6, of which 3 were waited for; matrix products, arithmetic and copies ran while one was open for 0% of the time, Pallas kernels for 25%

profile of v4, /device:TPU:0, one launch (start us, length us, event | category | flops | bytes accessed | tf_op | source)
XLA Modules:
  0.0 19.0 jit_solution(13293505372439902944)
XLA Ops:
  0.0 2.9 %collective-permute-start = (bf16[2,576,128]{2,1,0:T(8,128)(2,1)}, bf16[2,576,128]{2,1,0:T(8,128)(2,1)S(1)}, u32[]{:S(2)}, u32[]{:S(2)}) collective-permute-start(bf16[2,576,128]{2,1,0:T(8,128)(2,1)} %bitcast.8), channel_id=1, source_target_pairs={{0,4},{4,0},{8,12},{12,8},{16,20},{20,16},{24,28},{28,24},{1,5},{5... | collective-permute-start | bytes 884744 | tf_op jit(solution)/shard_map/ppermute | solution.py:277
  2.9 1.2 %pack.1 = (bf16[96,128]{1,0:T(8,128)(2,1)S(1)}, bf16[2,576,128]{2,1,0:T(8,128)(2,1)S(1)}, bf16[384,12]{1,0:T(8,128)(2,1)S(1)}, s32[8,16,128]{2,1,0:T(8,128)S(1)}...) custom-call(bf16[2,576,128]{2,1,0:T(8,128)(2,1)} %bitcast.9, bf16[384,12]{1,0:T(8,128)(2,1)} %bitcast.10, ...), custom_call_target="tpu_custom_call" | custom-call | tf_op jit(solution)/shard_map/pack/pallas_call | solution.py:334
  4.2 0.1 collective-permute-start.1
  4.2 1.7 %collective-permute-start.2 = (bf16[96,128]{1,0:T(8,128)(2,1)S(1)}, bf16[96,128]{1,0:T(8,128)(2,1)S(1)}, u32[]{:S(2)}, u32[]{:S(2)}) collective-permute-start(bf16[96,128]{1,0:T(8,128)(2,1)S(1)} %get-tuple-element.23), channel_id=1, source_target_pairs={{0,3},{1,0},{2,1},{3,2},{4,7},{5,4},{6,5},{7,6},{8,11},{9,8},{10,9... | collective-permute-start | bytes 73736 | tf_op jit(solution)/shard_map/ppermute | solution.py:277
  6.0 0.6 %factors.1 = (bf16[8,12,16,640]{3,2,1,0:T(8,128)(2,1)S(1)}, bf16[3,8,3,16,384]{4,3,2,1,0:T(8,128)(2,1)S(1)}, bf16[12,256,128]{2,1,0:T(8,128)(2,1)S(1)}) custom-call(bf16[384,12]{1,0:T(8,128)(2,1)S(1)} %get-tuple-element.25.c_ref, s32[8,16,128]{2,1,0:T(8,128)S(1)} %get-tuple-element.26.near_ref, s32[1,32]{1,0:T(1,128)S(1)} %get-tuple-element.27.sh_ref, ...), custom_call_target="tpu_custom_call" | custom-call | tf_op jit(solution)/shard_map/factors/pallas_call | solution.py:322
  6.6 0.9 %collective-permute-done.1.low_ref = bf16[96,128]{1,0:T(8,128)(2,1)S(1)} collective-permute-done((bf16[96,128]{1,0:T(8,128)(2,1)S(1)}, bf16[96,128]{1,0:T(8,128)(2,1)S(1)}, u32[]{:S(2)}, u32[]{:S(2)}) %collective-permute-start.1) | collective-permute-done | bytes 24608 | tf_op jit(solution)/shard_map/ppermute | solution.py:277
  7.5 0.0 collective-permute-done.2.high_ref
  7.5 2.0 %collective-permute-start.5 = (bf16[864,128]{1,0:T(8,128)(2,1)S(1)}, bf16[864,128]{1,0:T(8,128)(2,1)S(1)}, u32[]{:S(2)}, u32[]{:S(2)}) collective-permute-start(bf16[864,128]{1,0:T(8,128)(2,1)S(1)} %get-tuple-element.32.after_ref), channel_id=1, source_target_pairs={{0,1},{1,0},{2,3},{3,2},{4,8},{5,9},{6,10},{7,11},{8,4},{9,5},{10,... | collective-permute-start | bytes 663560 | tf_op jit(solution)/shard_map/ppermute | solution.py:302
  9.5 0.7 %collective-permute-done.x_ref.near_ref = bf16[2,576,128]{2,1,0:T(8,128)(2,1)S(1)} collective-permute-done((bf16[2,576,128]{2,1,0:T(8,128)(2,1)}, bf16[2,576,128]{2,1,0:T(8,128)(2,1)S(1)}, u32[]{:S(2)}, u32[]{:S(2)}) %collective-permute-start) | collective-permute-done | bytes 294944 | tf_op jit(solution)/shard_map/ppermute | solution.py:277
  10.2 1.9 %collective-permute-start.4 = (bf16[2,192,128]{2,1,0:T(8,128)(2,1)S(1)}, bf16[2,192,128]{2,1,0:T(8,128)(2,1)S(1)}, u32[]{:S(2)}, u32[]{:S(2)}) collective-permute-start(bf16[2,192,128]{2,1,0:T(8,128)(2,1)S(1)} %pass.1), channel_id=1, source_target_pairs={{0,8},{4,0},{8,16},{12,4},{16,24},{20,12},{24,28},{28,20},{1,9},{5... | collective-permute-start | bytes 294920 | tf_op jit(solution)/shard_map/ppermute | solution.py:277
  12.0 0.2 %collective-permute-start.3 = (bf16[96,128]{1,0:T(8,128)(2,1)S(1)}, bf16[96,128]{1,0:T(8,128)(2,1)S(1)}, u32[]{:S(2)}, u32[]{:S(2)}) collective-permute-start(bf16[96,128]{1,0:T(8,128)(2,1)S(1)} %get-tuple-element.31.rim_ref), channel_id=1, source_target_pairs={{0,4},{4,0},{8,12},{12,8},{16,20},{20,16},{24,28},{28,24},{1,5},{5... | collective-permute-start | bytes 73736 | tf_op jit(solution)/shard_map/ppermute | solution.py:277
  12.2 1.7 %weights.1 = (bf16[12,48,640]{2,1,0:T(8,128)(2,1)S(1)}, bf16[12,48,640]{2,1,0:T(8,128)(2,1)S(1)}, f32[3,12,6,8,128]{4,3,2,1,0:T(8,128)S(1)}, f32[3,12,12,8,128]{4,3,2,1,0:T(8,128)S(1)}) custom-call(bf16[8,12,16,640]{3,2,1,0:T(8,128)(2,1)S(1)} %get-tuple-element.33.t1_ref, bf16[3,8,3,16,384]{4,3,2,1,0:T(8,128)(2,1)S(1)} %get-tuple-element.34.t2_ref, ...), custom_call_target="tpu_custom_call" | custom-call | tf_op jit(solution)/shard_map/weights/pallas_call | solution.py:322
  13.9 1.3 %others.1 = (bf16[12,48,640]{2,1,0:T(8,128)(2,1)S(1)}, f32[576,256]{1,0:T(8,128)S(1)}) custom-call(bf16[8,12,16,640]{3,2,1,0:T(8,128)(2,1)S(1)} %get-tuple-element.33.t1_ref, bf16[3,8,3,16,384]{4,3,2,1,0:T(8,128)(2,1)S(1)} %get-tuple-element.34.t2_ref, bf16[12,256,128]{2,1,0:T(8,128)(2,1)S(1)} %get-tuple-element.30.after_ref.table_ref, ...), custom_call_target="tpu_custom_call" | custom-call | tf_op jit(solution)/shard_map/others/pallas_call | solution.py:322
  15.2 0.6 %collective-permute-done.3.rim_ref = bf16[96,128]{1,0:T(8,128)(2,1)S(1)} collective-permute-done((bf16[96,128]{1,0:T(8,128)(2,1)S(1)}, bf16[96,128]{1,0:T(8,128)(2,1)S(1)}, u32[]{:S(2)}, u32[]{:S(2)}) %collective-permute-start.3) | collective-permute-done | bytes 24608 | tf_op jit(solution)/shard_map/ppermute | solution.py:277
  15.9 0.0 collective-permute-done.5.fj_ref
  15.9 0.0 collective-permute-done.4.ff_ref
  15.9 3.1 %green_update.1 = bf16[2,12,48,128]{3,2,1,0:T(8,128)(2,1)} custom-call(bf16[2,576,128]{2,1,0:T(8,128)(2,1)S(1)} %collective-permute-done.x_ref.near_ref, bf16[96,128]{1,0:T(8,128)(2,1)S(1)} %collective-permute-done.3.rim_ref, bf16[2,192,128]{2,1,0:T(8,128)(2,1)S(1)} %collective-permute-done.4.ff_ref, bf16[864,128]{1,0:T(8,128)(2,1)S(1)} %collective-permute-done.5.fj_ref, ...), custom_call_target="tpu_custom_call" | custom-call | tf_op jit(solution)/shard_map/green_update/pallas_call | solution.py:363
  (2 shorter events, 0.0 us)
Async XLA Ops:
  0.0 10.2 %collective-permute-start = (bf16[2,576,128]{2,1,0:T(8,128)(2,1)}, bf16[2,576,128]{2,1,0:T(8,128)(2,1)S(1)}, u32[]{:S(2)}, u32[]{:S(2)}) collective-permute-start(bf16[2,576,128]{2,1,0:T(8,128)(2,1)} %bitcast.8), channel_id=1, source_target_pairs={{0,4},{4,0},{8,12},{12,8},{16,20},{20,16},{24,28},{28,24},{1,5},{5... | collective-permute-start | bytes 884744 | tf_op jit(solution)/shard_map/ppermute | solution.py:277
  4.2 3.3 %collective-permute-start.1 = (bf16[96,128]{1,0:T(8,128)(2,1)S(1)}, bf16[96,128]{1,0:T(8,128)(2,1)S(1)}, u32[]{:S(2)}, u32[]{:S(2)}) collective-permute-start(bf16[96,128]{1,0:T(8,128)(2,1)S(1)} %get-tuple-element.23), channel_id=1, source_target_pairs={{0,1},{1,2},{2,3},{3,0},{4,5},{5,6},{6,7},{7,4},{8,9},{9,10},{10,1... | collective-permute-start | bytes 73736 | tf_op jit(solution)/shard_map/ppermute | solution.py:277
  4.2 3.3 %collective-permute-start.2 = (bf16[96,128]{1,0:T(8,128)(2,1)S(1)}, bf16[96,128]{1,0:T(8,128)(2,1)S(1)}, u32[]{:S(2)}, u32[]{:S(2)}) collective-permute-start(bf16[96,128]{1,0:T(8,128)(2,1)S(1)} %get-tuple-element.23), channel_id=1, source_target_pairs={{0,3},{1,0},{2,1},{3,2},{4,7},{5,4},{6,5},{7,6},{8,11},{9,8},{10,9... | collective-permute-start | bytes 73736 | tf_op jit(solution)/shard_map/ppermute | solution.py:277
  7.5 8.4 %collective-permute-start.5 = (bf16[864,128]{1,0:T(8,128)(2,1)S(1)}, bf16[864,128]{1,0:T(8,128)(2,1)S(1)}, u32[]{:S(2)}, u32[]{:S(2)}) collective-permute-start(bf16[864,128]{1,0:T(8,128)(2,1)S(1)} %get-tuple-element.32.after_ref), channel_id=1, source_target_pairs={{0,1},{1,0},{2,3},{3,2},{4,8},{5,9},{6,10},{7,11},{8,4},{9,5},{10,... | collective-permute-start | bytes 663560 | tf_op jit(solution)/shard_map/ppermute | solution.py:302
  10.2 5.7 %collective-permute-start.4 = (bf16[2,192,128]{2,1,0:T(8,128)(2,1)S(1)}, bf16[2,192,128]{2,1,0:T(8,128)(2,1)S(1)}, u32[]{:S(2)}, u32[]{:S(2)}) collective-permute-start(bf16[2,192,128]{2,1,0:T(8,128)(2,1)S(1)} %pass.1), channel_id=1, source_target_pairs={{0,8},{4,0},{8,16},{12,4},{16,24},{20,12},{24,28},{28,20},{1,9},{5... | collective-permute-start | bytes 294920 | tf_op jit(solution)/shard_map/ppermute | solution.py:277
  12.0 3.8 %collective-permute-start.3 = (bf16[96,128]{1,0:T(8,128)(2,1)S(1)}, bf16[96,128]{1,0:T(8,128)(2,1)S(1)}, u32[]{:S(2)}, u32[]{:S(2)}) collective-permute-start(bf16[96,128]{1,0:T(8,128)(2,1)S(1)} %get-tuple-element.31.rim_ref), channel_id=1, source_target_pairs={{0,4},{4,0},{8,12},{12,8},{16,20},{20,16},{24,28},{28,24},{1,5},{5... | collective-permute-start | bytes 73736 | tf_op jit(solution)/shard_map/ppermute | solution.py:277

commit v5 on v4

--- a/solution.py
+++ b/solution.py
@@ -60,7 +60,7 @@
     rest = (out_ref.shape[0] - rim) // 2
     for r in range(2):
         out_ref[r * rest:(r + 1) * rest] = g_ref[r, rows - rest:]
-    below = (iota(low_ref.shape, 1) & WIDTH) == 0
+    below = ((iota(low_ref.shape, 1) & WIDTH) == 0) ^ ((lax.axis_index("energy") & 1) == 0)
     low, high = low_ref[...].astype(F32), high_ref[...].astype(F32)
     halo = jnp.where(below, low, high).astype(BF16)
     out_ref[2 * rest:] = halo
@@ -285,6 +285,10 @@
     return i ^ 1
 
 
+def cross(i):
+    return i + 1 if i & 1 else i - 1
+
+
 def relay(i, count):
     if i & 1:
         return i - 2 if i > 1 else 0
@@ -309,7 +313,7 @@
     span = orb * atoms
     cols = -(-rows // LANES) * LANES
     period = span * LANES // math.gcd(span, LANES)
-    early = orb // 3
+    early = orb // 2
     late = 2 * (orb - early) * span + 2 * span
     vmem = pl.BlockSpec(memory_space=pltpu.VMEM)
     smem = pl.BlockSpec(memory_space=pltpu.SMEM)
@@ -351,7 +355,7 @@
         [weight, weight, plain, shape(3, orb, orb, 8, energies, kind=F32)], left, right, held)
     join, rim = call(
         join_kernel, "join", [shape(late, energies), shape(2 * span, LANES)],
-        ring(edge, "energy", 1), ring(edge, "energy", -1), held, table)
+        move(edge, "energy", pair), move(edge, "energy", cross), held, table)
     far_join = move_far(join)
     rim_near = move(rim, "atom", pair)
     passed = call(pass_kernel, "pass", shape(2, early * span, energies), near, join)

time: 19.3 us -> 19.2 us (level)
  starting transfers between devices: 8.79 us -> 7.53 us
  waiting for transfers between devices: 2.21 us -> 3.46 us
    ppermute x5, waiting for transfers between devices: 2.2 us -> 3.45 us  [move(): lax.ppermute(value, axis, [(i, target(i) % count) for i in range(count)])]
    ppermute x1, starting transfers between devices: 1.98 us -> 0.81 us  [move_far(): return lax.ppermute(value, ('atom', 'energy'), moves)]
  transfers between devices with their start and end apart: 6 -> 6, of which waited for: 3 -> 3; matrix products, arithmetic and copies ran while one was open for 0% -> 0% of each run, Pallas kernels for 25% -> 26%
where the time goes in v5:
time: 19.2 us; the launch traced here: 19 us
  Pallas kernels  7.99 us (42%)
  starting transfers between devices  7.53 us (39%)
  waiting for transfers between devices  3.46 us (18%)
    ppermute x5, starting transfers between devices, move(): lax.ppermute(value, axis, [(i, target(i) % count) for i in range(count)])  6.72 us
    pallas_call x5, Pallas kernels, call(): pl.pallas_call(kernel, out_shape=out_shape, name=name, in_specs=[smem if...  3.62 us
    ppermute x5, waiting for transfers between devices, move(): lax.ppermute(value, axis, [(i, target(i) % count) for i in range(count)])  3.45 us
    pallas_call x1, Pallas kernels, per_device(): pl.pallas_call(functools.partial(final_kernel, orb, atoms), name='green_u...  3.15 us
    pallas_call x1, Pallas kernels, per_device(): pl.pallas_call(functools.partial(pack_kernel, orb), name='pack', out_shap...  1.23 us
    ppermute x1, starting transfers between devices, move_far(): return lax.ppermute(value, ('atom', 'energy'), moves)  0.81 us
  transfers between devices with their start and end apart: 6, of which 3 were waited for; matrix products, arithmetic and copies ran while one was open for 0% of the time, Pallas kernels for 26%

profile of v5, /device:TPU:0, one launch (start us, length us, event | category | flops | bytes accessed | tf_op | source)
XLA Modules:
  0.0 19.0 jit_solution(8742897294433610864)
XLA Ops:
  0.0 2.9 %collective-permute-start = (bf16[2,576,128]{2,1,0:T(8,128)(2,1)}, bf16[2,576,128]{2,1,0:T(8,128)(2,1)S(1)}, u32[]{:S(2)}, u32[]{:S(2)}) collective-permute-start(bf16[2,576,128]{2,1,0:T(8,128)(2,1)} %bitcast.8), channel_id=1, source_target_pairs={{0,4},{4,0},{8,12},{12,8},{16,20},{20,16},{24,28},{28,24},{1,5},{5... | collective-permute-start | bytes 884744 | tf_op jit(solution)/shard_map/ppermute | solution.py:277
  2.9 1.2 %pack.1 = (bf16[96,128]{1,0:T(8,128)(2,1)S(1)}, bf16[2,576,128]{2,1,0:T(8,128)(2,1)S(1)}, bf16[384,12]{1,0:T(8,128)(2,1)S(1)}, s32[8,16,128]{2,1,0:T(8,128)S(1)}...) custom-call(bf16[2,576,128]{2,1,0:T(8,128)(2,1)} %bitcast.9, bf16[384,12]{1,0:T(8,128)(2,1)} %bitcast.10, ...), custom_call_target="tpu_custom_call" | custom-call | tf_op jit(solution)/shard_map/pack/pallas_call | solution.py:338
  4.2 0.1 collective-permute-start.1
  4.3 1.6 %collective-permute-start.2 = (bf16[96,128]{1,0:T(8,128)(2,1)S(1)}, bf16[96,128]{1,0:T(8,128)(2,1)S(1)}, u32[]{:S(2)}, u32[]{:S(2)}) collective-permute-start(bf16[96,128]{1,0:T(8,128)(2,1)S(1)} %get-tuple-element.23), channel_id=1, source_target_pairs={{0,3},{1,2},{2,1},{3,0},{4,7},{5,6},{6,5},{7,4},{8,11},{9,10},{10,... | collective-permute-start | bytes 73736 | tf_op jit(solution)/shard_map/ppermute | solution.py:277
  5.9 0.6 %factors.1 = (bf16[8,12,16,640]{3,2,1,0:T(8,128)(2,1)S(1)}, bf16[3,8,3,16,384]{4,3,2,1,0:T(8,128)(2,1)S(1)}, bf16[12,256,128]{2,1,0:T(8,128)(2,1)S(1)}) custom-call(bf16[384,12]{1,0:T(8,128)(2,1)S(1)} %get-tuple-element.25.c_ref, s32[8,16,128]{2,1,0:T(8,128)S(1)} %get-tuple-element.26.near_ref, s32[1,32]{1,0:T(1,128)S(1)} %get-tuple-element.27.sh_ref, ...), custom_call_target="tpu_custom_call" | custom-call | tf_op jit(solution)/shard_map/factors/pallas_call | solution.py:326
  6.5 0.0 collective-permute-done.1.low_ref
  6.5 1.0 %collective-permute-done.2.high_ref = bf16[96,128]{1,0:T(8,128)(2,1)S(1)} collective-permute-done((bf16[96,128]{1,0:T(8,128)(2,1)S(1)}, bf16[96,128]{1,0:T(8,128)(2,1)S(1)}, u32[]{:S(2)}, u32[]{:S(2)}) %collective-permute-start.2) | collective-permute-done | bytes 24608 | tf_op jit(solution)/shard_map/ppermute | solution.py:277
  7.6 0.8 %collective-permute-start.5 = (bf16[672,128]{1,0:T(8,128)(2,1)S(1)}, bf16[672,128]{1,0:T(8,128)(2,1)S(1)}, u32[]{:S(2)}, u32[]{:S(2)}) collective-permute-start(bf16[672,128]{1,0:T(8,128)(2,1)S(1)} %get-tuple-element.32.after_ref), channel_id=1, source_target_pairs={{0,1},{1,0},{2,3},{3,2},{4,8},{5,9},{6,10},{7,11},{8,4},{9,5},{10,... | collective-permute-start | bytes 516104 | tf_op jit(solution)/shard_map/ppermute | solution.py:306
  8.4 1.8 %collective-permute-done.x_ref.near_ref = bf16[2,576,128]{2,1,0:T(8,128)(2,1)S(1)} collective-permute-done((bf16[2,576,128]{2,1,0:T(8,128)(2,1)}, bf16[2,576,128]{2,1,0:T(8,128)(2,1)S(1)}, u32[]{:S(2)}, u32[]{:S(2)}) %collective-permute-start) | collective-permute-done | bytes 294944 | tf_op jit(solution)/shard_map/ppermute | solution.py:277
  10.2 1.9 %collective-permute-start.4 = (bf16[2,288,128]{2,1,0:T(8,128)(2,1)S(1)}, bf16[2,288,128]{2,1,0:T(8,128)(2,1)S(1)}, u32[]{:S(2)}, u32[]{:S(2)}) collective-permute-start(bf16[2,288,128]{2,1,0:T(8,128)(2,1)S(1)} %pass.1), channel_id=1, source_target_pairs={{0,8},{4,0},{8,16},{12,4},{16,24},{20,12},{24,28},{28,20},{1,9},{5... | collective-permute-start | bytes 442376 | tf_op jit(solution)/shard_map/ppermute | solution.py:277
  12.1 0.2 %collective-permute-start.3 = (bf16[96,128]{1,0:T(8,128)(2,1)S(1)}, bf16[96,128]{1,0:T(8,128)(2,1)S(1)}, u32[]{:S(2)}, u32[]{:S(2)}) collective-permute-start(bf16[96,128]{1,0:T(8,128)(2,1)S(1)} %get-tuple-element.31.rim_ref), channel_id=1, source_target_pairs={{0,4},{4,0},{8,12},{12,8},{16,20},{20,16},{24,28},{28,24},{1,5},{5... | collective-permute-start | bytes 73736 | tf_op jit(solution)/shard_map/ppermute | solution.py:277
  12.2 1.7 %weights.1 = (bf16[12,48,640]{2,1,0:T(8,128)(2,1)S(1)}, bf16[12,48,640]{2,1,0:T(8,128)(2,1)S(1)}, f32[3,12,6,8,128]{4,3,2,1,0:T(8,128)S(1)}, f32[3,12,12,8,128]{4,3,2,1,0:T(8,128)S(1)}) custom-call(bf16[8,12,16,640]{3,2,1,0:T(8,128)(2,1)S(1)} %get-tuple-element.33.t1_ref, bf16[3,8,3,16,384]{4,3,2,1,0:T(8,128)(2,1)S(1)} %get-tuple-element.34.t2_ref, ...), custom_call_target="tpu_custom_call" | custom-call | tf_op jit(solution)/shard_map/weights/pallas_call | solution.py:326
  13.9 1.3 %others.1 = (bf16[12,48,640]{2,1,0:T(8,128)(2,1)S(1)}, f32[576,256]{1,0:T(8,128)S(1)}) custom-call(bf16[8,12,16,640]{3,2,1,0:T(8,128)(2,1)S(1)} %get-tuple-element.33.t1_ref, bf16[3,8,3,16,384]{4,3,2,1,0:T(8,128)(2,1)S(1)} %get-tuple-element.34.t2_ref, bf16[12,256,128]{2,1,0:T(8,128)(2,1)S(1)} %get-tuple-element.30.after_ref.table_ref, ...), custom_call_target="tpu_custom_call" | custom-call | tf_op jit(solution)/shard_map/others/pallas_call | solution.py:326
  15.2 0.6 %collective-permute-done.3.rim_ref = bf16[96,128]{1,0:T(8,128)(2,1)S(1)} collective-permute-done((bf16[96,128]{1,0:T(8,128)(2,1)S(1)}, bf16[96,128]{1,0:T(8,128)(2,1)S(1)}, u32[]{:S(2)}, u32[]{:S(2)}) %collective-permute-start.3) | collective-permute-done | bytes 24608 | tf_op jit(solution)/shard_map/ppermute | solution.py:277
  15.9 0.0 collective-permute-done.5.fj_ref
  15.9 0.0 collective-permute-done.4.ff_ref
  15.9 3.1 %green_update.1 = bf16[2,12,48,128]{3,2,1,0:T(8,128)(2,1)} custom-call(bf16[2,576,128]{2,1,0:T(8,128)(2,1)S(1)} %collective-permute-done.x_ref.near_ref, bf16[96,128]{1,0:T(8,128)(2,1)S(1)} %collective-permute-done.3.rim_ref, bf16[2,288,128]{2,1,0:T(8,128)(2,1)S(1)} %collective-permute-done.4.ff_ref, bf16[672,128]{1,0:T(8,128)(2,1)S(1)} %collective-permute-done.5.fj_ref, ...), custom_call_target="tpu_custom_call" | custom-call | tf_op jit(solution)/shard_map/green_update/pallas_call | solution.py:367
  (2 shorter events, 0.0 us)
Async XLA Ops:
  0.0 10.2 %collective-permute-start = (bf16[2,576,128]{2,1,0:T(8,128)(2,1)}, bf16[2,576,128]{2,1,0:T(8,128)(2,1)S(1)}, u32[]{:S(2)}, u32[]{:S(2)}) collective-permute-start(bf16[2,576,128]{2,1,0:T(8,128)(2,1)} %bitcast.8), channel_id=1, source_target_pairs={{0,4},{4,0},{8,12},{12,8},{16,20},{20,16},{24,28},{28,24},{1,5},{5... | collective-permute-start | bytes 884744 | tf_op jit(solution)/shard_map/ppermute | solution.py:277
  4.2 2.3 %collective-permute-start.1 = (bf16[96,128]{1,0:T(8,128)(2,1)S(1)}, bf16[96,128]{1,0:T(8,128)(2,1)S(1)}, u32[]{:S(2)}, u32[]{:S(2)}) collective-permute-start(bf16[96,128]{1,0:T(8,128)(2,1)S(1)} %get-tuple-element.23), channel_id=1, source_target_pairs={{0,1},{1,0},{2,3},{3,2},{4,5},{5,4},{6,7},{7,6},{8,9},{9,8},{10,11... | collective-permute-start | bytes 73736 | tf_op jit(solution)/shard_map/ppermute | solution.py:277
  4.3 3.3 %collective-permute-start.2 = (bf16[96,128]{1,0:T(8,128)(2,1)S(1)}, bf16[96,128]{1,0:T(8,128)(2,1)S(1)}, u32[]{:S(2)}, u32[]{:S(2)}) collective-permute-start(bf16[96,128]{1,0:T(8,128)(2,1)S(1)} %get-tuple-element.23), channel_id=1, source_target_pairs={{0,3},{1,2},{2,1},{3,0},{4,7},{5,6},{6,5},{7,4},{8,11},{9,10},{10,... | collective-permute-start | bytes 73736 | tf_op jit(solution)/shard_map/ppermute | solution.py:277
  7.6 8.3 %collective-permute-start.5 = (bf16[672,128]{1,0:T(8,128)(2,1)S(1)}, bf16[672,128]{1,0:T(8,128)(2,1)S(1)}, u32[]{:S(2)}, u32[]{:S(2)}) collective-permute-start(bf16[672,128]{1,0:T(8,128)(2,1)S(1)} %get-tuple-element.32.after_ref), channel_id=1, source_target_pairs={{0,1},{1,0},{2,3},{3,2},{4,8},{5,9},{6,10},{7,11},{8,4},{9,5},{10,... | collective-permute-start | bytes 516104 | tf_op jit(solution)/shard_map/ppermute | solution.py:306
  10.2 5.7 %collective-permute-start.4 = (bf16[2,288,128]{2,1,0:T(8,128)(2,1)S(1)}, bf16[2,288,128]{2,1,0:T(8,128)(2,1)S(1)}, u32[]{:S(2)}, u32[]{:S(2)}) collective-permute-start(bf16[2,288,128]{2,1,0:T(8,128)(2,1)S(1)} %pass.1), channel_id=1, source_target_pairs={{0,8},{4,0},{8,16},{12,4},{16,24},{20,12},{24,28},{28,20},{1,9},{5... | collective-permute-start | bytes 442376 | tf_op jit(solution)/shard_map/ppermute | solution.py:277
  12.1 3.8 %collective-permute-start.3 = (bf16[96,128]{1,0:T(8,128)(2,1)S(1)}, bf16[96,128]{1,0:T(8,128)(2,1)S(1)}, u32[]{:S(2)}, u32[]{:S(2)}) collective-permute-start(bf16[96,128]{1,0:T(8,128)(2,1)S(1)} %get-tuple-element.31.rim_ref), channel_id=1, source_target_pairs={{0,4},{4,0},{8,12},{12,8},{16,20},{20,16},{24,28},{28,24},{1,5},{5... | collective-permute-start | bytes 73736 | tf_op jit(solution)/shard_map/ppermute | solution.py:277

commit v6 on v5

--- a/solution.py
+++ b/solution.py
@@ -26,13 +26,7 @@
     return sum((x >= step * m).astype(jnp.int32) for m in range(1, most))
 
 
-def pack_kernel(orb, g_hbm, c_hbm, nbr_hbm, sh_hbm, st_hbm, oc_hbm,
-                edge_ref, g_ref, c_ref, near_ref, sh_ref, st_ref, oc_ref, nbr_ref, sems):
-    ends = ((g_hbm, g_ref), (nbr_hbm, nbr_ref), (c_hbm, c_ref), (sh_hbm, sh_ref), (st_hbm, st_ref), (oc_hbm, oc_ref))
-    copies = [pltpu.make_async_copy(source, target, sems.at[i]) for i, (source, target) in enumerate(ends)]
-    for copy in copies:
-        copy.start()
-    copies[0].wait()
+def pack_edges(orb, g_ref, edge_ref):
     span = g_ref.shape[1] // orb
     lane = iota((span, LANES), 1)
     for r in range(2):
@@ -42,6 +36,21 @@
             turned = pltpu.roll(x, EDGE * k + WIDTH, 1)
             total = jnp.where((lane >= EDGE * k) & (lane < EDGE * (k + 1)), turned, total)
         edge_ref[r * span:(r + 1) * span] = total.astype(BF16)
+
+
+def from_sides(pair_ref, cross_ref):
+    below = ((iota(pair_ref.shape, 1) & WIDTH) == 0) ^ ((lax.axis_index("energy") & 1) == 0)
+    return jnp.where(below, pair_ref[...].astype(F32), cross_ref[...].astype(F32)).astype(BF16)
+
+
+def pack_kernel(orb, g_hbm, c_hbm, nbr_hbm, sh_hbm, st_hbm, oc_hbm,
+                edge_ref, g_ref, c_ref, near_ref, sh_ref, st_ref, oc_ref, nbr_ref, sems):
+    ends = ((g_hbm, g_ref), (nbr_hbm, nbr_ref), (c_hbm, c_ref), (sh_hbm, sh_ref), (st_hbm, st_ref), (oc_hbm, oc_ref))
+    copies = [pltpu.make_async_copy(source, target, sems.at[i]) for i, (source, target) in enumerate(ends)]
+    for copy in copies:
+        copy.start()
+    copies[0].wait()
+    pack_edges(orb, g_ref, edge_ref)
     copies[1].wait()
     atoms, bonds = nbr_ref.shape
     own = iota(near_ref.shape[1:], 0) & (atoms - 1)
@@ -54,21 +63,20 @@
         copy.wait()
 
 
-def join_kernel(low_ref, high_ref, g_ref, after_ref, out_ref, rim_ref):
+def join_kernel(pair_ref, cross_ref, g_ref, after_ref, out_ref, rim_ref):
     rows = g_ref.shape[1]
-    rim = low_ref.shape[0]
+    rim = pair_ref.shape[0]
     rest = (out_ref.shape[0] - rim) // 2
     for r in range(2):
         out_ref[r * rest:(r + 1) * rest] = g_ref[r, rows - rest:]
-    below = ((iota(low_ref.shape, 1) & WIDTH) == 0) ^ ((lax.axis_index("energy") & 1) == 0)
-    low, high = low_ref[...].astype(F32), high_ref[...].astype(F32)
-    halo = jnp.where(below, low, high).astype(BF16)
+    halo = from_sides(pair_ref, cross_ref)
     out_ref[2 * rest:] = halo
     rim_ref[...] = halo
 
 
-def pass_kernel(x_ref, after_ref, out_ref):
+def pass_kernel(orb, x_ref, after_ref, out_ref, edge_ref):
     out_ref[...] = x_ref[:, :out_ref.shape[1]]
+    pack_edges(orb, x_ref, edge_ref)
 
 
 def band_weights(sh_ref, st_ref, oc_ref):
@@ -221,13 +229,13 @@
     return jnp.stack([first, second], axis=1).reshape(orb, orb, 8, x.shape[1])
 
 
-def final_kernel(orb, atoms, near_ref, rim_ref, ff_ref, fj_ref, wn_ref, wf_ref, s_ref, table_ref, gn_ref, gd_ref,
+def final_kernel(orb, atoms, near_ref, pair_ref, cross_ref, ff_ref, fj_ref, wn_ref, wf_ref, s_ref, table_ref, gn_ref, gd_ref,
                  out_hbm, sn_ref, ld_ref, out_ref, sems):
     energies = table_ref.shape[2]
     span = orb * atoms
     groups = span // 8
     slabs = [whole(near_ref, orb), joined((ff_ref,), fj_ref, orb, span)]
-    rims = [rim_ref[...], rim_of(fj_ref, span)]
+    rims = [from_sides(pair_ref, cross_ref), rim_of(fj_ref, span)]
     total = s_ref[...] + slab_products([wn_ref, wf_ref], slabs, rims, table_ref)
     re, im = total[:, :energies], total[:, energies:]
     for c, x in enumerate((re, im, re + im)):
@@ -355,10 +363,11 @@
         [weight, weight, plain, shape(3, orb, orb, 8, energies, kind=F32)], left, right, held)
     join, rim = call(
         join_kernel, "join", [shape(late, energies), shape(2 * span, LANES)],
-        move(edge, "energy", pair), move(edge, "energy", cross), held, table)
+        move(edge, "energy", pair), move(edge, "energy", cross), held, w_near)
     far_join = move_far(join)
-    rim_near = move(rim, "atom", pair)
-    passed = call(pass_kernel, "pass", shape(2, early * span, energies), near, join)
+    passed, near_edge = call(
+        functools.partial(pass_kernel, orb), "pack_near",
+        [shape(2, early * span, energies), shape(2 * span, LANES)], near, join)
     far_first = move(passed, "atom", lambda i: relay(i, lax.axis_size("atom")))
     w_far, own = call(
         functools.partial(others_kernel, orb), "others", [weight, shape(rows, 2 * energies, kind=F32)],
@@ -367,12 +376,12 @@
     result = pl.pallas_call(
         functools.partial(final_kernel, orb, atoms), name="green_update",
         out_shape=shape(2, orb, span, energies),
-        in_specs=[vmem] * 10, out_specs=pl.BlockSpec(memory_space=pltpu.HBM),
+        in_specs=[vmem] * 11, out_specs=pl.BlockSpec(memory_space=pltpu.HBM),
         scratch_shapes=[
             pltpu.VMEM(plain.shape, F32), pltpu.VMEM((3, 2, orb, 8, energies), F32),
             pltpu.VMEM((2, orb, span, energies), BF16), pltpu.SemaphoreType.DMA((orb // 2,))],
         compiler_params=small,
-    )(near, rim_near, far_first, far_join, w_near, w_far, own, table, gn, gd)
+    )(near, move(near_edge, "energy", pair), move(near_edge, "energy", cross), far_first, far_join, w_near, w_far, own, table, gn, gd)
     return result.reshape(bare_green.shape)
 
 

time: 19.2 us -> 18.8 us (0.979)
  waiting for transfers between devices: 3.46 us -> 2.13 us
  starting transfers between devices: 7.53 us -> 8.31 us
    ppermute x5 -> x6, starting transfers between devices: 6.72 us -> 8.16 us  [move(): lax.ppermute(value, axis, [(i, target(i) % count) for i in range(count)])]
    ppermute x5 -> x6, waiting for transfers between devices: 3.45 us -> 2.12 us  [move(): lax.ppermute(value, axis, [(i, target(i) % count) for i in range(count)])]
    ppermute x1, starting transfers between devices: 0.81 us -> 0.15 us  [move_far(): return lax.ppermute(value, ('atom', 'energy'), moves)]
  transfers between devices with their start and end apart: 6 -> 7, of which waited for: 3 -> 3; matrix products, arithmetic and copies ran while one was open for 0% -> 0% of each run, Pallas kernels for 26% -> 27%
where the time goes in v6:
time: 18.8 us; the launch traced here: 18.6 us
  starting transfers between devices  8.31 us (44%)
  Pallas kernels  8.13 us (43%)
  waiting for transfers between devices  2.13 us (11%)
    ppermute x6, starting transfers between devices, move(): lax.ppermute(value, axis, [(i, target(i) % count) for i in range(count)])  8.16 us
    pallas_call x5, Pallas kernels, call(): pl.pallas_call(kernel, out_shape=out_shape, name=name, in_specs=[smem if...  3.75 us
    pallas_call x1, Pallas kernels, per_device(): pl.pallas_call(functools.partial(final_kernel, orb, atoms), name='green_u...  3.15 us
    ppermute x6, waiting for transfers between devices, move(): lax.ppermute(value, axis, [(i, target(i) % count) for i in range(count)])  2.12 us
    pallas_call x1, Pallas kernels, per_device(): pl.pallas_call(functools.partial(pack_kernel, orb), name='pack', out_shap...  1.23 us
  transfers between devices with their start and end apart: 7, of which 3 were waited for; matrix products, arithmetic and copies ran while one was open for 0% of the time, Pallas kernels for 27%

profile of v6, /device:TPU:0, one launch (start us, length us, event | category | flops | bytes accessed | tf_op | source)
XLA Modules:
  0.0 18.6 jit_solution(18012843749412506546)
XLA Ops:
  0.0 2.9 %collective-permute-start = (bf16[2,576,128]{2,1,0:T(8,128)(2,1)}, bf16[2,576,128]{2,1,0:T(8,128)(2,1)S(1)}, u32[]{:S(2)}, u32[]{:S(2)}) collective-permute-start(bf16[2,576,128]{2,1,0:T(8,128)(2,1)} %bitcast.8), channel_id=1, source_target_pairs={{0,4},{4,0},{8,12},{12,8},{16,20},{20,16},{24,28},{28,24},{1,5},{5... | collective-permute-start | bytes 884744 | tf_op jit(solution)/shard_map/ppermute | solution.py:285
  2.9 1.2 %pack.1 = (bf16[96,128]{1,0:T(8,128)(2,1)S(1)}, bf16[2,576,128]{2,1,0:T(8,128)(2,1)S(1)}, bf16[384,12]{1,0:T(8,128)(2,1)S(1)}, s32[8,16,128]{2,1,0:T(8,128)S(1)}...) custom-call(bf16[2,576,128]{2,1,0:T(8,128)(2,1)} %bitcast.9, bf16[384,12]{1,0:T(8,128)(2,1)} %bitcast.10, ...), custom_call_target="tpu_custom_call" | custom-call | tf_op jit(solution)/shard_map/pack/pallas_call | solution.py:346
  4.2 0.1 collective-permute-start.1
  4.3 1.6 %collective-permute-start.2 = (bf16[96,128]{1,0:T(8,128)(2,1)S(1)}, bf16[96,128]{1,0:T(8,128)(2,1)S(1)}, u32[]{:S(2)}, u32[]{:S(2)}) collective-permute-start(bf16[96,128]{1,0:T(8,128)(2,1)S(1)} %get-tuple-element.25), channel_id=1, source_target_pairs={{0,3},{1,2},{2,1},{3,0},{4,7},{5,6},{6,5},{7,4},{8,11},{9,10},{10,... | collective-permute-start | bytes 73736 | tf_op jit(solution)/shard_map/ppermute | solution.py:285
  5.9 0.6 %factors.1 = (bf16[8,12,16,640]{3,2,1,0:T(8,128)(2,1)S(1)}, bf16[3,8,3,16,384]{4,3,2,1,0:T(8,128)(2,1)S(1)}, bf16[12,256,128]{2,1,0:T(8,128)(2,1)S(1)}) custom-call(bf16[384,12]{1,0:T(8,128)(2,1)S(1)} %get-tuple-element.27.c_ref, s32[8,16,128]{2,1,0:T(8,128)S(1)} %get-tuple-element.28.near_ref, s32[1,32]{1,0:T(1,128)S(1)} %get-tuple-element.29.sh_ref, ...), custom_call_target="tpu_custom_call" | custom-call | tf_op jit(solution)/shard_map/factors/pallas_call | solution.py:334
  6.5 1.7 %weights.1 = (bf16[12,48,640]{2,1,0:T(8,128)(2,1)S(1)}, bf16[12,48,640]{2,1,0:T(8,128)(2,1)S(1)}, f32[3,12,6,8,128]{4,3,2,1,0:T(8,128)S(1)}, f32[3,12,12,8,128]{4,3,2,1,0:T(8,128)S(1)}) custom-call(bf16[8,12,16,640]{3,2,1,0:T(8,128)(2,1)S(1)} %get-tuple-element.32.t1_ref, bf16[3,8,3,16,384]{4,3,2,1,0:T(8,128)(2,1)S(1)} %get-tuple-element.33.t2_ref, ...), custom_call_target="tpu_custom_call" | custom-call | tf_op jit(solution)/shard_map/weights/pallas_call | solution.py:334
  8.2 0.0 collective-permute-done.1.pair_ref
  8.2 0.0 collective-permute-done.2.cross_ref
  8.2 0.2 collective-permute-start.6
  8.4 1.8 %collective-permute-done.x_ref.near_ref = bf16[2,576,128]{2,1,0:T(8,128)(2,1)S(1)} collective-permute-done((bf16[2,576,128]{2,1,0:T(8,128)(2,1)}, bf16[2,576,128]{2,1,0:T(8,128)(2,1)S(1)}, u32[]{:S(2)}, u32[]{:S(2)}) %collective-permute-start) | collective-permute-done | bytes 294944 | tf_op jit(solution)/shard_map/ppermute | solution.py:285
  10.2 0.1 pack_near.1
  10.3 1.9 %collective-permute-start.5 = (bf16[2,288,128]{2,1,0:T(8,128)(2,1)S(1)}, bf16[2,288,128]{2,1,0:T(8,128)(2,1)S(1)}, u32[]{:S(2)}, u32[]{:S(2)}) collective-permute-start(bf16[2,288,128]{2,1,0:T(8,128)(2,1)S(1)} %get-tuple-element.37), channel_id=1, source_target_pairs={{0,8},{4,0},{8,16},{12,4},{16,24},{20,12},{24,28},{28,20},{1,9},{5... | collective-permute-start | bytes 442376 | tf_op jit(solution)/shard_map/ppermute | solution.py:285
  12.2 0.0 collective-permute-start.3
  12.2 1.6 %collective-permute-start.4 = (bf16[96,128]{1,0:T(8,128)(2,1)S(1)}, bf16[96,128]{1,0:T(8,128)(2,1)S(1)}, u32[]{:S(2)}, u32[]{:S(2)}) collective-permute-start(bf16[96,128]{1,0:T(8,128)(2,1)S(1)} %get-tuple-element.36), channel_id=1, source_target_pairs={{0,3},{1,2},{2,1},{3,0},{4,7},{5,6},{6,5},{7,4},{8,11},{9,10},{10,... | collective-permute-start | bytes 73736 | tf_op jit(solution)/shard_map/ppermute | solution.py:285
  13.8 1.3 %others.1 = (bf16[12,48,640]{2,1,0:T(8,128)(2,1)S(1)}, f32[576,256]{1,0:T(8,128)S(1)}) custom-call(bf16[8,12,16,640]{3,2,1,0:T(8,128)(2,1)S(1)} %get-tuple-element.32.t1_ref, bf16[3,8,3,16,384]{4,3,2,1,0:T(8,128)(2,1)S(1)} %get-tuple-element.33.t2_ref, bf16[12,256,128]{2,1,0:T(8,128)(2,1)S(1)} %get-tuple-element.38.table_ref, ...), custom_call_target="tpu_custom_call" | custom-call | tf_op jit(solution)/shard_map/others/pallas_call | solution.py:334
  15.1 0.0 collective-permute-done.6.fj_ref
  15.1 0.0 collective-permute-done.3.pair_ref
  15.1 0.3 %collective-permute-done.4.cross_ref = bf16[96,128]{1,0:T(8,128)(2,1)S(1)} collective-permute-done((bf16[96,128]{1,0:T(8,128)(2,1)S(1)}, bf16[96,128]{1,0:T(8,128)(2,1)S(1)}, u32[]{:S(2)}, u32[]{:S(2)}) %collective-permute-start.4) | collective-permute-done | bytes 24608 | tf_op jit(solution)/shard_map/ppermute | solution.py:285
  15.4 0.1 collective-permute-done.5.ff_ref
  15.5 3.1 %green_update.1 = bf16[2,12,48,128]{3,2,1,0:T(8,128)(2,1)} custom-call(bf16[2,576,128]{2,1,0:T(8,128)(2,1)S(1)} %collective-permute-done.x_ref.near_ref, bf16[96,128]{1,0:T(8,128)(2,1)S(1)} %collective-permute-done.3.pair_ref, bf16[96,128]{1,0:T(8,128)(2,1)S(1)} %collective-permute-done.4.cross_ref, bf16[2,288,128]{2,1,0:T(8,128)(2,1)S(1)} %collective-permute-done.5.ff_ref, ...), custom_call_target="tpu_custom_call" | custom-call | tf_op jit(solution)/shard_map/green_update/pallas_call | solution.py:376
  (1 shorter events, 0.0 us)
Async XLA Ops:
  0.0 10.2 %collective-permute-start = (bf16[2,576,128]{2,1,0:T(8,128)(2,1)}, bf16[2,576,128]{2,1,0:T(8,128)(2,1)S(1)}, u32[]{:S(2)}, u32[]{:S(2)}) collective-permute-start(bf16[2,576,128]{2,1,0:T(8,128)(2,1)} %bitcast.8), channel_id=1, source_target_pairs={{0,4},{4,0},{8,12},{12,8},{16,20},{20,16},{24,28},{28,24},{1,5},{5... | collective-permute-start | bytes 884744 | tf_op jit(solution)/shard_map/ppermute | solution.py:285
  4.2 4.0 %collective-permute-start.1 = (bf16[96,128]{1,0:T(8,128)(2,1)S(1)}, bf16[96,128]{1,0:T(8,128)(2,1)S(1)}, u32[]{:S(2)}, u32[]{:S(2)}) collective-permute-start(bf16[96,128]{1,0:T(8,128)(2,1)S(1)} %get-tuple-element.25), channel_id=1, source_target_pairs={{0,1},{1,0},{2,3},{3,2},{4,5},{5,4},{6,7},{7,6},{8,9},{9,8},{10,11... | collective-permute-start | bytes 73736 | tf_op jit(solution)/shard_map/ppermute | solution.py:285
  4.3 4.0 %collective-permute-start.2 = (bf16[96,128]{1,0:T(8,128)(2,1)S(1)}, bf16[96,128]{1,0:T(8,128)(2,1)S(1)}, u32[]{:S(2)}, u32[]{:S(2)}) collective-permute-start(bf16[96,128]{1,0:T(8,128)(2,1)S(1)} %get-tuple-element.25), channel_id=1, source_target_pairs={{0,3},{1,2},{2,1},{3,0},{4,7},{5,6},{6,5},{7,4},{8,11},{9,10},{10,... | collective-permute-start | bytes 73736 | tf_op jit(solution)/shard_map/ppermute | solution.py:285
  8.2 6.9 %collective-permute-start.6 = (bf16[672,128]{1,0:T(8,128)(2,1)S(1)}, bf16[672,128]{1,0:T(8,128)(2,1)S(1)}, u32[]{:S(2)}, u32[]{:S(2)}) collective-permute-start(bf16[672,128]{1,0:T(8,128)(2,1)S(1)} %get-tuple-element.35.after_ref), channel_id=1, source_target_pairs={{0,1},{1,0},{2,3},{3,2},{4,8},{5,9},{6,10},{7,11},{8,4},{9,5},{10,... | collective-permute-start | bytes 516104 | tf_op jit(solution)/shard_map/ppermute | solution.py:314
  10.3 5.2 %collective-permute-start.5 = (bf16[2,288,128]{2,1,0:T(8,128)(2,1)S(1)}, bf16[2,288,128]{2,1,0:T(8,128)(2,1)S(1)}, u32[]{:S(2)}, u32[]{:S(2)}) collective-permute-start(bf16[2,288,128]{2,1,0:T(8,128)(2,1)S(1)} %get-tuple-element.37), channel_id=1, source_target_pairs={{0,8},{4,0},{8,16},{12,4},{16,24},{20,12},{24,28},{28,20},{1,9},{5... | collective-permute-start | bytes 442376 | tf_op jit(solution)/shard_map/ppermute | solution.py:285
  12.2 2.9 %collective-permute-start.3 = (bf16[96,128]{1,0:T(8,128)(2,1)S(1)}, bf16[96,128]{1,0:T(8,128)(2,1)S(1)}, u32[]{:S(2)}, u32[]{:S(2)}) collective-permute-start(bf16[96,128]{1,0:T(8,128)(2,1)S(1)} %get-tuple-element.36), channel_id=1, source_target_pairs={{0,1},{1,0},{2,3},{3,2},{4,5},{5,4},{6,7},{7,6},{8,9},{9,8},{10,11... | collective-permute-start | bytes 73736 | tf_op jit(solution)/shard_map/ppermute | solution.py:285
  12.2 3.3 %collective-permute-start.4 = (bf16[96,128]{1,0:T(8,128)(2,1)S(1)}, bf16[96,128]{1,0:T(8,128)(2,1)S(1)}, u32[]{:S(2)}, u32[]{:S(2)}) collective-permute-start(bf16[96,128]{1,0:T(8,128)(2,1)S(1)} %get-tuple-element.36), channel_id=1, source_target_pairs={{0,3},{1,2},{2,1},{3,0},{4,7},{5,6},{6,5},{7,4},{8,11},{9,10},{10,... | collective-permute-start | bytes 73736 | tf_op jit(solution)/shard_map/ppermute | solution.py:285

commit v7 on v6

--- a/solution.py
+++ b/solution.py
@@ -175,10 +175,11 @@
             def body(i, carry):
                 x = [t1_ref[n, i, :, at] for n in range(bonds)]
                 for q in range(groups):
-                    total = x[0] * held[q][0]
-                    for n in range(1, bonds):
-                        total = total + x[n] * held[q][n]
-                    out[i, q * 16:(q + 1) * 16, at] = total
+                    terms = [x[n] * held[q][n] for n in range(bonds)]
+                    while len(terms) > 1:
+                        pairs = [terms[n] + terms[n + 1] for n in range(0, len(terms) - 1, 2)]
+                        terms = pairs + terms[2 * len(pairs):]
+                    out[i, q * 16:(q + 1) * 16, at] = terms[0]
                 return carry
 
             lax.fori_loop(0, orb, body, 0, unroll=orb)
@@ -283,10 +284,6 @@
 def move(value, axis, target):
     count = lax.axis_size(axis)
     return lax.ppermute(value, axis, [(i, target(i) % count) for i in range(count)])
-
-
-def ring(value, axis, step):
-    return move(value, axis, lambda i: i + step)
 
 
 def pair(i):

time: 18.8 us -> 18.8 us (level)
  no operation moved by 1% of the time
where the time goes in v7:
time: 18.8 us; the launch traced here: 18.6 us
  starting transfers between devices  8.29 us (44%)
  Pallas kernels  8.15 us (43%)
  waiting for transfers between devices  2.12 us (11%)
    ppermute x6, starting transfers between devices, move(): lax.ppermute(value, axis, [(i, target(i) % count) for i in range(count)])  8.16 us
    pallas_call x5, Pallas kernels, call(): pl.pallas_call(kernel, out_shape=out_shape, name=name, in_specs=[smem if...  3.77 us
    pallas_call x1, Pallas kernels, per_device(): pl.pallas_call(functools.partial(final_kernel, orb, atoms), name='green_u...  3.15 us
    ppermute x6, waiting for transfers between devices, move(): lax.ppermute(value, axis, [(i, target(i) % count) for i in range(count)])  2.12 us
    pallas_call x1, Pallas kernels, per_device(): pl.pallas_call(functools.partial(pack_kernel, orb), name='pack', out_shap...  1.23 us
  transfers between devices with their start and end apart: 7, of which 3 were waited for; matrix products, arithmetic and copies ran while one was open for 0% of the time, Pallas kernels for 27%

profile of v7, /device:TPU:0, one launch (start us, length us, event | category | flops | bytes accessed | tf_op | source)
XLA Modules:
  0.0 18.6 jit_solution(7733441055276420925)
XLA Ops:
  0.0 2.9 %collective-permute-start = (bf16[2,576,128]{2,1,0:T(8,128)(2,1)}, bf16[2,576,128]{2,1,0:T(8,128)(2,1)S(1)}, u32[]{:S(2)}, u32[]{:S(2)}) collective-permute-start(bf16[2,576,128]{2,1,0:T(8,128)(2,1)} %bitcast.8), channel_id=1, source_target_pairs={{0,4},{4,0},{8,12},{12,8},{16,20},{20,16},{24,28},{28,24},{1,5},{5... | collective-permute-start | bytes 884744 | tf_op jit(solution)/shard_map/ppermute | solution.py:286
  2.9 1.2 %pack.1 = (bf16[96,128]{1,0:T(8,128)(2,1)S(1)}, bf16[2,576,128]{2,1,0:T(8,128)(2,1)S(1)}, bf16[384,12]{1,0:T(8,128)(2,1)S(1)}, s32[8,16,128]{2,1,0:T(8,128)S(1)}...) custom-call(bf16[2,576,128]{2,1,0:T(8,128)(2,1)} %bitcast.9, bf16[384,12]{1,0:T(8,128)(2,1)} %bitcast.10, ...), custom_call_target="tpu_custom_call" | custom-call | tf_op jit(solution)/shard_map/pack/pallas_call | solution.py:343
  4.2 0.1 collective-permute-start.1
  4.3 1.6 %collective-permute-start.2 = (bf16[96,128]{1,0:T(8,128)(2,1)S(1)}, bf16[96,128]{1,0:T(8,128)(2,1)S(1)}, u32[]{:S(2)}, u32[]{:S(2)}) collective-permute-start(bf16[96,128]{1,0:T(8,128)(2,1)S(1)} %get-tuple-element.25), channel_id=1, source_target_pairs={{0,3},{1,2},{2,1},{3,0},{4,7},{5,6},{6,5},{7,4},{8,11},{9,10},{10,... | collective-permute-start | bytes 73736 | tf_op jit(solution)/shard_map/ppermute | solution.py:286
  5.9 0.6 %factors.1 = (bf16[8,12,16,640]{3,2,1,0:T(8,128)(2,1)S(1)}, bf16[3,8,3,16,384]{4,3,2,1,0:T(8,128)(2,1)S(1)}, bf16[12,256,128]{2,1,0:T(8,128)(2,1)S(1)}) custom-call(bf16[384,12]{1,0:T(8,128)(2,1)S(1)} %get-tuple-element.27.c_ref, s32[8,16,128]{2,1,0:T(8,128)S(1)} %get-tuple-element.28.near_ref, s32[1,32]{1,0:T(1,128)S(1)} %get-tuple-element.29.sh_ref, ...), custom_call_target="tpu_custom_call" | custom-call | tf_op jit(solution)/shard_map/factors/pallas_call | solution.py:331
  6.5 1.7 %weights.1 = (bf16[12,48,640]{2,1,0:T(8,128)(2,1)S(1)}, bf16[12,48,640]{2,1,0:T(8,128)(2,1)S(1)}, f32[3,12,6,8,128]{4,3,2,1,0:T(8,128)S(1)}, f32[3,12,12,8,128]{4,3,2,1,0:T(8,128)S(1)}) custom-call(bf16[8,12,16,640]{3,2,1,0:T(8,128)(2,1)S(1)} %get-tuple-element.32.t1_ref, bf16[3,8,3,16,384]{4,3,2,1,0:T(8,128)(2,1)S(1)} %get-tuple-element.33.t2_ref, ...), custom_call_target="tpu_custom_call" | custom-call | tf_op jit(solution)/shard_map/weights/pallas_call | solution.py:331
  8.2 0.0 collective-permute-done.1.pair_ref
  8.2 0.0 collective-permute-done.2.cross_ref
  8.3 0.1 collective-permute-start.6
  8.4 1.7 %collective-permute-done.x_ref.near_ref = bf16[2,576,128]{2,1,0:T(8,128)(2,1)S(1)} collective-permute-done((bf16[2,576,128]{2,1,0:T(8,128)(2,1)}, bf16[2,576,128]{2,1,0:T(8,128)(2,1)S(1)}, u32[]{:S(2)}, u32[]{:S(2)}) %collective-permute-start) | collective-permute-done | bytes 294944 | tf_op jit(solution)/shard_map/ppermute | solution.py:286
  10.2 0.1 pack_near.1
  10.3 1.9 %collective-permute-start.5 = (bf16[2,288,128]{2,1,0:T(8,128)(2,1)S(1)}, bf16[2,288,128]{2,1,0:T(8,128)(2,1)S(1)}, u32[]{:S(2)}, u32[]{:S(2)}) collective-permute-start(bf16[2,288,128]{2,1,0:T(8,128)(2,1)S(1)} %get-tuple-element.37), channel_id=1, source_target_pairs={{0,8},{4,0},{8,16},{12,4},{16,24},{20,12},{24,28},{28,20},{1,9},{5... | collective-permute-start | bytes 442376 | tf_op jit(solution)/shard_map/ppermute | solution.py:286
  12.2 0.0 collective-permute-start.3
  12.2 1.6 %collective-permute-start.4 = (bf16[96,128]{1,0:T(8,128)(2,1)S(1)}, bf16[96,128]{1,0:T(8,128)(2,1)S(1)}, u32[]{:S(2)}, u32[]{:S(2)}) collective-permute-start(bf16[96,128]{1,0:T(8,128)(2,1)S(1)} %get-tuple-element.36), channel_id=1, source_target_pairs={{0,3},{1,2},{2,1},{3,0},{4,7},{5,6},{6,5},{7,4},{8,11},{9,10},{10,... | collective-permute-start | bytes 73736 | tf_op jit(solution)/shard_map/ppermute | solution.py:286
  13.8 1.3 %others.1 = (bf16[12,48,640]{2,1,0:T(8,128)(2,1)S(1)}, f32[576,256]{1,0:T(8,128)S(1)}) custom-call(bf16[8,12,16,640]{3,2,1,0:T(8,128)(2,1)S(1)} %get-tuple-element.32.t1_ref, bf16[3,8,3,16,384]{4,3,2,1,0:T(8,128)(2,1)S(1)} %get-tuple-element.33.t2_ref, bf16[12,256,128]{2,1,0:T(8,128)(2,1)S(1)} %get-tuple-element.38.table_ref, ...), custom_call_target="tpu_custom_call" | custom-call | tf_op jit(solution)/shard_map/others/pallas_call | solution.py:331
  15.1 0.0 collective-permute-done.6.fj_ref
  15.1 0.0 collective-permute-done.3.pair_ref
  15.1 0.3 %collective-permute-done.4.cross_ref = bf16[96,128]{1,0:T(8,128)(2,1)S(1)} collective-permute-done((bf16[96,128]{1,0:T(8,128)(2,1)S(1)}, bf16[96,128]{1,0:T(8,128)(2,1)S(1)}, u32[]{:S(2)}, u32[]{:S(2)}) %collective-permute-start.4) | collective-permute-done | bytes 24608 | tf_op jit(solution)/shard_map/ppermute | solution.py:286
  15.4 0.1 collective-permute-done.5.ff_ref
  15.5 3.1 %green_update.1 = bf16[2,12,48,128]{3,2,1,0:T(8,128)(2,1)} custom-call(bf16[2,576,128]{2,1,0:T(8,128)(2,1)S(1)} %collective-permute-done.x_ref.near_ref, bf16[96,128]{1,0:T(8,128)(2,1)S(1)} %collective-permute-done.3.pair_ref, bf16[96,128]{1,0:T(8,128)(2,1)S(1)} %collective-permute-done.4.cross_ref, bf16[2,288,128]{2,1,0:T(8,128)(2,1)S(1)} %collective-permute-done.5.ff_ref, ...), custom_call_target="tpu_custom_call" | custom-call | tf_op jit(solution)/shard_map/green_update/pallas_call | solution.py:373
  (1 shorter events, 0.0 us)
Async XLA Ops:
  0.0 10.2 %collective-permute-start = (bf16[2,576,128]{2,1,0:T(8,128)(2,1)}, bf16[2,576,128]{2,1,0:T(8,128)(2,1)S(1)}, u32[]{:S(2)}, u32[]{:S(2)}) collective-permute-start(bf16[2,576,128]{2,1,0:T(8,128)(2,1)} %bitcast.8), channel_id=1, source_target_pairs={{0,4},{4,0},{8,12},{12,8},{16,20},{20,16},{24,28},{28,24},{1,5},{5... | collective-permute-start | bytes 884744 | tf_op jit(solution)/shard_map/ppermute | solution.py:286
  4.2 4.1 %collective-permute-start.1 = (bf16[96,128]{1,0:T(8,128)(2,1)S(1)}, bf16[96,128]{1,0:T(8,128)(2,1)S(1)}, u32[]{:S(2)}, u32[]{:S(2)}) collective-permute-start(bf16[96,128]{1,0:T(8,128)(2,1)S(1)} %get-tuple-element.25), channel_id=1, source_target_pairs={{0,1},{1,0},{2,3},{3,2},{4,5},{5,4},{6,7},{7,6},{8,9},{9,8},{10,11... | collective-permute-start | bytes 73736 | tf_op jit(solution)/shard_map/ppermute | solution.py:286
  4.3 4.0 %collective-permute-start.2 = (bf16[96,128]{1,0:T(8,128)(2,1)S(1)}, bf16[96,128]{1,0:T(8,128)(2,1)S(1)}, u32[]{:S(2)}, u32[]{:S(2)}) collective-permute-start(bf16[96,128]{1,0:T(8,128)(2,1)S(1)} %get-tuple-element.25), channel_id=1, source_target_pairs={{0,3},{1,2},{2,1},{3,0},{4,7},{5,6},{6,5},{7,4},{8,11},{9,10},{10,... | collective-permute-start | bytes 73736 | tf_op jit(solution)/shard_map/ppermute | solution.py:286
  8.3 6.8 %collective-permute-start.6 = (bf16[672,128]{1,0:T(8,128)(2,1)S(1)}, bf16[672,128]{1,0:T(8,128)(2,1)S(1)}, u32[]{:S(2)}, u32[]{:S(2)}) collective-permute-start(bf16[672,128]{1,0:T(8,128)(2,1)S(1)} %get-tuple-element.35.after_ref), channel_id=1, source_target_pairs={{0,1},{1,0},{2,3},{3,2},{4,8},{5,9},{6,10},{7,11},{8,4},{9,5},{10,... | collective-permute-start | bytes 516104 | tf_op jit(solution)/shard_map/ppermute | solution.py:311
  10.3 5.2 %collective-permute-start.5 = (bf16[2,288,128]{2,1,0:T(8,128)(2,1)S(1)}, bf16[2,288,128]{2,1,0:T(8,128)(2,1)S(1)}, u32[]{:S(2)}, u32[]{:S(2)}) collective-permute-start(bf16[2,288,128]{2,1,0:T(8,128)(2,1)S(1)} %get-tuple-element.37), channel_id=1, source_target_pairs={{0,8},{4,0},{8,16},{12,4},{16,24},{20,12},{24,28},{28,20},{1,9},{5... | collective-permute-start | bytes 442376 | tf_op jit(solution)/shard_map/ppermute | solution.py:286
  12.2 2.9 %collective-permute-start.3 = (bf16[96,128]{1,0:T(8,128)(2,1)S(1)}, bf16[96,128]{1,0:T(8,128)(2,1)S(1)}, u32[]{:S(2)}, u32[]{:S(2)}) collective-permute-start(bf16[96,128]{1,0:T(8,128)(2,1)S(1)} %get-tuple-element.36), channel_id=1, source_target_pairs={{0,1},{1,0},{2,3},{3,2},{4,5},{5,4},{6,7},{7,6},{8,9},{9,8},{10,11... | collective-permute-start | bytes 73736 | tf_op jit(solution)/shard_map/ppermute | solution.py:286
  12.2 3.3 %collective-permute-start.4 = (bf16[96,128]{1,0:T(8,128)(2,1)S(1)}, bf16[96,128]{1,0:T(8,128)(2,1)S(1)}, u32[]{:S(2)}, u32[]{:S(2)}) collective-permute-start(bf16[96,128]{1,0:T(8,128)(2,1)S(1)} %get-tuple-element.36), channel_id=1, source_target_pairs={{0,3},{1,2},{2,1},{3,0},{4,7},{5,6},{6,5},{7,4},{8,11},{9,10},{10,... | collective-permute-start | bytes 73736 | tf_op jit(solution)/shard_map/ppermute | solution.py:286

commit v8 on v7

--- a/solution.py
+++ b/solution.py
@@ -157,8 +157,11 @@
     fill(t1_ref, t2_ref, (wn_ref, wo_ref), 0)
 
 
-def others_kernel(orb, t1_ref, t2_ref, table_ref, g_ref, rim_ref, wo_ref, wf_ref, s_ref):
+def far_kernel(t1_ref, t2_ref, after_ref, wf_ref):
     fill(t1_ref, t2_ref, (wf_ref,), 2)
+
+
+def own_kernel(orb, table_ref, g_ref, rim_ref, wo_ref, s_ref):
     s_ref[...] = slab_products([wo_ref], [whole(g_ref, orb)], [rim_ref[...]], table_ref)
 
 
@@ -318,7 +321,7 @@
     span = orb * atoms
     cols = -(-rows // LANES) * LANES
     period = span * LANES // math.gcd(span, LANES)
-    early = orb // 2
+    early = orb // 3
     late = 2 * (orb - early) * span + 2 * span
     vmem = pl.BlockSpec(memory_space=pltpu.VMEM)
     smem = pl.BlockSpec(memory_space=pltpu.SMEM)
@@ -362,13 +365,13 @@
         join_kernel, "join", [shape(late, energies), shape(2 * span, LANES)],
         move(edge, "energy", pair), move(edge, "energy", cross), held, w_near)
     far_join = move_far(join)
+    w_far = call(far_kernel, "far_weights", weight, left, right, join)
     passed, near_edge = call(
         functools.partial(pass_kernel, orb), "pack_near",
-        [shape(2, early * span, energies), shape(2 * span, LANES)], near, join)
+        [shape(2, early * span, energies), shape(2 * span, LANES)], near, w_far)
     far_first = move(passed, "atom", lambda i: relay(i, lax.axis_size("atom")))
-    w_far, own = call(
-        functools.partial(others_kernel, orb), "others", [weight, shape(rows, 2 * energies, kind=F32)],
-        left, right, table, held, rim, w_own)
+    own = call(
+        functools.partial(own_kernel, orb), "own", shape(rows, 2 * energies, kind=F32), table, held, rim, w_own)
 
     result = pl.pallas_call(
         functools.partial(final_kernel, orb, atoms), name="green_update",

time: 18.8 us -> 18.8 us (level)
  waiting for transfers between devices: 2.12 us -> 1.92 us
    ppermute x6, waiting for transfers between devices: 2.12 us -> 1.91 us  [move(): lax.ppermute(value, axis, [(i, target(i) % count) for i in range(count)])]
    pallas_call x5 -> x6, Pallas kernels: 3.77 us -> 3.92 us  [call(): pl.pallas_call(kernel, out_shape=out_shape, name=name, in_specs=[smem if...]
  transfers between devices with their start and end apart: 7 -> 7, of which waited for: 3 -> 2; matrix products, arithmetic and copies ran while one was open for 0% -> 0% of each run, Pallas kernels for 27% -> 28%
where the time goes in v8:
time: 18.8 us; the launch traced here: 18.6 us
  Pallas kernels  8.31 us (44%)
  starting transfers between devices  8.29 us (44%)
  waiting for transfers between devices  1.92 us (10%)
    ppermute x6, starting transfers between devices, move(): lax.ppermute(value, axis, [(i, target(i) % count) for i in range(count)])  8.16 us
    pallas_call x6, Pallas kernels, call(): pl.pallas_call(kernel, out_shape=out_shape, name=name, in_specs=[smem if...  3.92 us
    pallas_call x1, Pallas kernels, per_device(): pl.pallas_call(functools.partial(final_kernel, orb, atoms), name='green_u...  3.16 us
    ppermute x6, waiting for transfers between devices, move(): lax.ppermute(value, axis, [(i, target(i) % count) for i in range(count)])  1.91 us
    pallas_call x1, Pallas kernels, per_device(): pl.pallas_call(functools.partial(pack_kernel, orb), name='pack', out_shap...  1.23 us
  transfers between devices with their start and end apart: 7, of which 2 were waited for; matrix products, arithmetic and copies ran while one was open for 0% of the time, Pallas kernels for 28%

profile of v8, /device:TPU:0, one launch (start us, length us, event | category | flops | bytes accessed | tf_op | source)
XLA Modules:
  0.0 18.6 jit_solution(9900948948698331271)
XLA Ops:
  0.0 2.9 %collective-permute-start = (bf16[2,576,128]{2,1,0:T(8,128)(2,1)}, bf16[2,576,128]{2,1,0:T(8,128)(2,1)S(1)}, u32[]{:S(2)}, u32[]{:S(2)}) collective-permute-start(bf16[2,576,128]{2,1,0:T(8,128)(2,1)} %bitcast.8), channel_id=1, source_target_pairs={{0,4},{4,0},{8,12},{12,8},{16,20},{20,16},{24,28},{28,24},{1,5},{5... | collective-permute-start | bytes 884744 | tf_op jit(solution)/shard_map/ppermute | solution.py:289
  2.9 1.2 %pack.1 = (bf16[96,128]{1,0:T(8,128)(2,1)S(1)}, bf16[2,576,128]{2,1,0:T(8,128)(2,1)S(1)}, bf16[384,12]{1,0:T(8,128)(2,1)S(1)}, s32[8,16,128]{2,1,0:T(8,128)S(1)}...) custom-call(bf16[2,576,128]{2,1,0:T(8,128)(2,1)} %bitcast.9, bf16[384,12]{1,0:T(8,128)(2,1)} %bitcast.10, ...), custom_call_target="tpu_custom_call" | custom-call | tf_op jit(solution)/shard_map/pack/pallas_call | solution.py:346
  4.2 0.1 collective-permute-start.1
  4.3 1.6 %collective-permute-start.2 = (bf16[96,128]{1,0:T(8,128)(2,1)S(1)}, bf16[96,128]{1,0:T(8,128)(2,1)S(1)}, u32[]{:S(2)}, u32[]{:S(2)}) collective-permute-start(bf16[96,128]{1,0:T(8,128)(2,1)S(1)} %get-tuple-element.30), channel_id=1, source_target_pairs={{0,3},{1,2},{2,1},{3,0},{4,7},{5,6},{6,5},{7,4},{8,11},{9,10},{10,... | collective-permute-start | bytes 73736 | tf_op jit(solution)/shard_map/ppermute | solution.py:289
  5.9 0.6 %factors.1 = (bf16[8,12,16,640]{3,2,1,0:T(8,128)(2,1)S(1)}, bf16[3,8,3,16,384]{4,3,2,1,0:T(8,128)(2,1)S(1)}, bf16[12,256,128]{2,1,0:T(8,128)(2,1)S(1)}) custom-call(bf16[384,12]{1,0:T(8,128)(2,1)S(1)} %get-tuple-element.23.c_ref, s32[8,16,128]{2,1,0:T(8,128)S(1)} %get-tuple-element.24.near_ref, s32[1,32]{1,0:T(1,128)S(1)} %get-tuple-element.25.sh_ref, ...), custom_call_target="tpu_custom_call" | custom-call | tf_op jit(solution)/shard_map/factors/pallas_call | solution.py:334
  6.5 1.7 %weights.1 = (bf16[12,48,640]{2,1,0:T(8,128)(2,1)S(1)}, bf16[12,48,640]{2,1,0:T(8,128)(2,1)S(1)}, f32[3,12,6,8,128]{4,3,2,1,0:T(8,128)S(1)}, f32[3,12,12,8,128]{4,3,2,1,0:T(8,128)S(1)}) custom-call(bf16[8,12,16,640]{3,2,1,0:T(8,128)(2,1)S(1)} %get-tuple-element.28.t1_ref, bf16[3,8,3,16,384]{4,3,2,1,0:T(8,128)(2,1)S(1)} %get-tuple-element.29.t2_ref, ...), custom_call_target="tpu_custom_call" | custom-call | tf_op jit(solution)/shard_map/weights/pallas_call | solution.py:334
  8.2 0.0 collective-permute-done.1.pair_ref
  8.2 0.0 collective-permute-done.2.cross_ref
  8.3 0.1 collective-permute-start.6
  8.4 0.8 %far_weights.1.after_ref.wf_ref = bf16[12,48,640]{2,1,0:T(8,128)(2,1)S(1)} custom-call(bf16[8,12,16,640]{3,2,1,0:T(8,128)(2,1)S(1)} %get-tuple-element.28.t1_ref, bf16[3,8,3,16,384]{4,3,2,1,0:T(8,128)(2,1)S(1)} %get-tuple-element.29.t2_ref, bf16[864,128]{1,0:T(8,128)(2,1)S(1)} %get-tuple-element.33.after_ref), custom_call_target="tpu_custom_call" | custom-call | tf_op jit(solution)/shard_map/far_weights/pallas_call | solution.py:334
  9.2 1.0 %collective-permute-done.x_ref.near_ref = bf16[2,576,128]{2,1,0:T(8,128)(2,1)S(1)} collective-permute-done((bf16[2,576,128]{2,1,0:T(8,128)(2,1)}, bf16[2,576,128]{2,1,0:T(8,128)(2,1)S(1)}, u32[]{:S(2)}, u32[]{:S(2)}) %collective-permute-start) | collective-permute-done | bytes 294944 | tf_op jit(solution)/shard_map/ppermute | solution.py:289
  10.2 0.1 pack_near.1
  10.3 1.9 %collective-permute-start.5 = (bf16[2,192,128]{2,1,0:T(8,128)(2,1)S(1)}, bf16[2,192,128]{2,1,0:T(8,128)(2,1)S(1)}, u32[]{:S(2)}, u32[]{:S(2)}) collective-permute-start(bf16[2,192,128]{2,1,0:T(8,128)(2,1)S(1)} %get-tuple-element.35), channel_id=1, source_target_pairs={{0,8},{4,0},{8,16},{12,4},{16,24},{20,12},{24,28},{28,20},{1,9},{5... | collective-permute-start | bytes 294920 | tf_op jit(solution)/shard_map/ppermute | solution.py:289
  12.2 0.0 collective-permute-start.3
  12.2 1.6 %collective-permute-start.4 = (bf16[96,128]{1,0:T(8,128)(2,1)S(1)}, bf16[96,128]{1,0:T(8,128)(2,1)S(1)}, u32[]{:S(2)}, u32[]{:S(2)}) collective-permute-start(bf16[96,128]{1,0:T(8,128)(2,1)S(1)} %get-tuple-element.34), channel_id=1, source_target_pairs={{0,3},{1,2},{2,1},{3,0},{4,7},{5,6},{6,5},{7,4},{8,11},{9,10},{10,... | collective-permute-start | bytes 73736 | tf_op jit(solution)/shard_map/ppermute | solution.py:289
  13.8 0.7 %own.1.s_ref = f32[576,256]{1,0:T(8,128)S(1)} custom-call(bf16[12,256,128]{2,1,0:T(8,128)(2,1)S(1)} %get-tuple-element.36.table_ref, bf16[2,576,128]{2,1,0:T(8,128)(2,1)S(1)} %get-tuple-element.31.g_ref, bf16[96,128]{1,0:T(8,128)(2,1)S(1)} %get-tuple-element.37.rim_ref, bf16[12,48,640]{2,1,0:T(8,128)(2,1)S(1)} %get-tuple-element.38.wo_ref), custom_call_target="tpu_custom_call" | custom-call | tf_op jit(solution)/shard_map/own/pallas_call | solution.py:334
  14.5 0.0 collective-permute-done.6.fj_ref
  14.5 0.0 collective-permute-done.3.pair_ref
  14.5 0.9 %collective-permute-done.4.cross_ref = bf16[96,128]{1,0:T(8,128)(2,1)S(1)} collective-permute-done((bf16[96,128]{1,0:T(8,128)(2,1)S(1)}, bf16[96,128]{1,0:T(8,128)(2,1)S(1)}, u32[]{:S(2)}, u32[]{:S(2)}) %collective-permute-start.4) | collective-permute-done | bytes 24608 | tf_op jit(solution)/shard_map/ppermute | solution.py:289
  15.4 0.0 collective-permute-done.5.ff_ref
  15.4 3.2 %green_update.1 = bf16[2,12,48,128]{3,2,1,0:T(8,128)(2,1)} custom-call(bf16[2,576,128]{2,1,0:T(8,128)(2,1)S(1)} %collective-permute-done.x_ref.near_ref, bf16[96,128]{1,0:T(8,128)(2,1)S(1)} %collective-permute-done.3.pair_ref, bf16[96,128]{1,0:T(8,128)(2,1)S(1)} %collective-permute-done.4.cross_ref, bf16[2,192,128]{2,1,0:T(8,128)(2,1)S(1)} %collective-permute-done.5.ff_ref, ...), custom_call_target="tpu_custom_call" | custom-call | tf_op jit(solution)/shard_map/green_update/pallas_call | solution.py:376
  (1 shorter events, 0.0 us)
Async XLA Ops:
  0.0 10.2 %collective-permute-start = (bf16[2,576,128]{2,1,0:T(8,128)(2,1)}, bf16[2,576,128]{2,1,0:T(8,128)(2,1)S(1)}, u32[]{:S(2)}, u32[]{:S(2)}) collective-permute-start(bf16[2,576,128]{2,1,0:T(8,128)(2,1)} %bitcast.8), channel_id=1, source_target_pairs={{0,4},{4,0},{8,12},{12,8},{16,20},{20,16},{24,28},{28,24},{1,5},{5... | collective-permute-start | bytes 884744 | tf_op jit(solution)/shard_map/ppermute | solution.py:289
  4.2 4.1 %collective-permute-start.1 = (bf16[96,128]{1,0:T(8,128)(2,1)S(1)}, bf16[96,128]{1,0:T(8,128)(2,1)S(1)}, u32[]{:S(2)}, u32[]{:S(2)}) collective-permute-start(bf16[96,128]{1,0:T(8,128)(2,1)S(1)} %get-tuple-element.30), channel_id=1, source_target_pairs={{0,1},{1,0},{2,3},{3,2},{4,5},{5,4},{6,7},{7,6},{8,9},{9,8},{10,11... | collective-permute-start | bytes 73736 | tf_op jit(solution)/shard_map/ppermute | solution.py:289
  4.3 4.0 %collective-permute-start.2 = (bf16[96,128]{1,0:T(8,128)(2,1)S(1)}, bf16[96,128]{1,0:T(8,128)(2,1)S(1)}, u32[]{:S(2)}, u32[]{:S(2)}) collective-permute-start(bf16[96,128]{1,0:T(8,128)(2,1)S(1)} %get-tuple-element.30), channel_id=1, source_target_pairs={{0,3},{1,2},{2,1},{3,0},{4,7},{5,6},{6,5},{7,4},{8,11},{9,10},{10,... | collective-permute-start | bytes 73736 | tf_op jit(solution)/shard_map/ppermute | solution.py:289
  8.3 6.2 %collective-permute-start.6 = (bf16[864,128]{1,0:T(8,128)(2,1)S(1)}, bf16[864,128]{1,0:T(8,128)(2,1)S(1)}, u32[]{:S(2)}, u32[]{:S(2)}) collective-permute-start(bf16[864,128]{1,0:T(8,128)(2,1)S(1)} %get-tuple-element.33.after_ref), channel_id=1, source_target_pairs={{0,1},{1,0},{2,3},{3,2},{4,8},{5,9},{6,10},{7,11},{8,4},{9,5},{10,... | collective-permute-start | bytes 663560 | tf_op jit(solution)/shard_map/ppermute | solution.py:314
  10.3 5.1 %collective-permute-start.5 = (bf16[2,192,128]{2,1,0:T(8,128)(2,1)S(1)}, bf16[2,192,128]{2,1,0:T(8,128)(2,1)S(1)}, u32[]{:S(2)}, u32[]{:S(2)}) collective-permute-start(bf16[2,192,128]{2,1,0:T(8,128)(2,1)S(1)} %get-tuple-element.35), channel_id=1, source_target_pairs={{0,8},{4,0},{8,16},{12,4},{16,24},{20,12},{24,28},{28,20},{1,9},{5... | collective-permute-start | bytes 294920 | tf_op jit(solution)/shard_map/ppermute | solution.py:289
  12.2 2.3 %collective-permute-start.3 = (bf16[96,128]{1,0:T(8,128)(2,1)S(1)}, bf16[96,128]{1,0:T(8,128)(2,1)S(1)}, u32[]{:S(2)}, u32[]{:S(2)}) collective-permute-start(bf16[96,128]{1,0:T(8,128)(2,1)S(1)} %get-tuple-element.34), channel_id=1, source_target_pairs={{0,1},{1,0},{2,3},{3,2},{4,5},{5,4},{6,7},{7,6},{8,9},{9,8},{10,11... | collective-permute-start | bytes 73736 | tf_op jit(solution)/shard_map/ppermute | solution.py:289
  12.2 3.3 %collective-permute-start.4 = (bf16[96,128]{1,0:T(8,128)(2,1)S(1)}, bf16[96,128]{1,0:T(8,128)(2,1)S(1)}, u32[]{:S(2)}, u32[]{:S(2)}) collective-permute-start(bf16[96,128]{1,0:T(8,128)(2,1)S(1)} %get-tuple-element.34), channel_id=1, source_target_pairs={{0,3},{1,2},{2,1},{3,0},{4,7},{5,6},{6,5},{7,4},{8,11},{9,10},{10,... | collective-permute-start | bytes 73736 | tf_op jit(solution)/shard_map/ppermute | solution.py:289

commit v9 on v8

--- a/solution.py
+++ b/solution.py
@@ -264,11 +264,14 @@
         for d in range(2):
             lr = m[0][d] - m[1][d]
             li = m[2][d] - (m[0][d] + m[1][d])
-            for c, x in enumerate((lr, li, lr + li)):
+            rows = []
+            for x in (lr, li):
                 turned = pltpu.roll(x, atoms, 1)
                 first = jnp.where(upper, x, turned)
                 second = jnp.where(upper, turned, x)
-                ld_ref[c, d] = jnp.stack([first, second], axis=1).reshape(orb, 8, energies)
+                rows.append(jnp.stack([first, second], axis=1).reshape(orb, 8, energies))
+            for c, x in enumerate((rows[0], rows[1], rows[0] + rows[1])):
+                ld_ref[c, d] = x
         m = product(lambda c, d, k: ld_ref[c, d, k], gn_ref, [[None, None] for _ in range(3)])
         for d in range(2):
             i = 2 * p + d

time: 18.8 us -> 18.8 us (level)
  no operation moved by 1% of the time
where the time goes in v9:
time: 18.8 us; the launch traced here: 18.6 us
  starting transfers between devices  8.29 us (44%)
  Pallas kernels  8.29 us (44%)
  waiting for transfers between devices  1.92 us (10%)
    ppermute x6, starting transfers between devices, move(): lax.ppermute(value, axis, [(i, target(i) % count) for i in range(count)])  8.16 us
    pallas_call x6, Pallas kernels, call(): pl.pallas_call(kernel, out_shape=out_shape, name=name, in_specs=[smem if...  3.92 us
    pallas_call x1, Pallas kernels, per_device(): pl.pallas_call(functools.partial(final_kernel, orb, atoms), name='green_u...  3.14 us
    ppermute x6, waiting for transfers between devices, move(): lax.ppermute(value, axis, [(i, target(i) % count) for i in range(count)])  1.91 us
    pallas_call x1, Pallas kernels, per_device(): pl.pallas_call(functools.partial(pack_kernel, orb), name='pack', out_shap...  1.23 us
  transfers between devices with their start and end apart: 7, of which 2 were waited for; matrix products, arithmetic and copies ran while one was open for 0% of the time, Pallas kernels for 28%

profile of v9, /device:TPU:0, one launch (start us, length us, event | category | flops | bytes accessed | tf_op | source)
XLA Modules:
  0.0 18.6 jit_solution(6348247400453856907)
XLA Ops:
  0.0 2.9 %collective-permute-start = (bf16[2,576,128]{2,1,0:T(8,128)(2,1)}, bf16[2,576,128]{2,1,0:T(8,128)(2,1)S(1)}, u32[]{:S(2)}, u32[]{:S(2)}) collective-permute-start(bf16[2,576,128]{2,1,0:T(8,128)(2,1)} %bitcast.8), channel_id=1, source_target_pairs={{0,4},{4,0},{8,12},{12,8},{16,20},{20,16},{24,28},{28,24},{1,5},{5... | collective-permute-start | bytes 884744 | tf_op jit(solution)/shard_map/ppermute | solution.py:292
  2.9 1.2 %pack.1 = (bf16[96,128]{1,0:T(8,128)(2,1)S(1)}, bf16[2,576,128]{2,1,0:T(8,128)(2,1)S(1)}, bf16[384,12]{1,0:T(8,128)(2,1)S(1)}, s32[8,16,128]{2,1,0:T(8,128)S(1)}...) custom-call(bf16[2,576,128]{2,1,0:T(8,128)(2,1)} %bitcast.9, bf16[384,12]{1,0:T(8,128)(2,1)} %bitcast.10, ...), custom_call_target="tpu_custom_call" | custom-call | tf_op jit(solution)/shard_map/pack/pallas_call | solution.py:349
  4.2 0.1 collective-permute-start.1
  4.3 1.6 %collective-permute-start.2 = (bf16[96,128]{1,0:T(8,128)(2,1)S(1)}, bf16[96,128]{1,0:T(8,128)(2,1)S(1)}, u32[]{:S(2)}, u32[]{:S(2)}) collective-permute-start(bf16[96,128]{1,0:T(8,128)(2,1)S(1)} %get-tuple-element.30), channel_id=1, source_target_pairs={{0,3},{1,2},{2,1},{3,0},{4,7},{5,6},{6,5},{7,4},{8,11},{9,10},{10,... | collective-permute-start | bytes 73736 | tf_op jit(solution)/shard_map/ppermute | solution.py:292
  5.9 0.6 %factors.1 = (bf16[8,12,16,640]{3,2,1,0:T(8,128)(2,1)S(1)}, bf16[3,8,3,16,384]{4,3,2,1,0:T(8,128)(2,1)S(1)}, bf16[12,256,128]{2,1,0:T(8,128)(2,1)S(1)}) custom-call(bf16[384,12]{1,0:T(8,128)(2,1)S(1)} %get-tuple-element.23.c_ref, s32[8,16,128]{2,1,0:T(8,128)S(1)} %get-tuple-element.24.near_ref, s32[1,32]{1,0:T(1,128)S(1)} %get-tuple-element.25.sh_ref, ...), custom_call_target="tpu_custom_call" | custom-call | tf_op jit(solution)/shard_map/factors/pallas_call | solution.py:337
  6.5 1.7 %weights.1 = (bf16[12,48,640]{2,1,0:T(8,128)(2,1)S(1)}, bf16[12,48,640]{2,1,0:T(8,128)(2,1)S(1)}, f32[3,12,6,8,128]{4,3,2,1,0:T(8,128)S(1)}, f32[3,12,12,8,128]{4,3,2,1,0:T(8,128)S(1)}) custom-call(bf16[8,12,16,640]{3,2,1,0:T(8,128)(2,1)S(1)} %get-tuple-element.28.t1_ref, bf16[3,8,3,16,384]{4,3,2,1,0:T(8,128)(2,1)S(1)} %get-tuple-element.29.t2_ref, ...), custom_call_target="tpu_custom_call" | custom-call | tf_op jit(solution)/shard_map/weights/pallas_call | solution.py:337
  8.2 0.0 collective-permute-done.1.pair_ref
  8.2 0.0 collective-permute-done.2.cross_ref
  8.3 0.1 collective-permute-start.6
  8.4 0.8 %far_weights.1.after_ref.wf_ref = bf16[12,48,640]{2,1,0:T(8,128)(2,1)S(1)} custom-call(bf16[8,12,16,640]{3,2,1,0:T(8,128)(2,1)S(1)} %get-tuple-element.28.t1_ref, bf16[3,8,3,16,384]{4,3,2,1,0:T(8,128)(2,1)S(1)} %get-tuple-element.29.t2_ref, bf16[864,128]{1,0:T(8,128)(2,1)S(1)} %get-tuple-element.33.after_ref), custom_call_target="tpu_custom_call" | custom-call | tf_op jit(solution)/shard_map/far_weights/pallas_call | solution.py:337
  9.2 1.0 %collective-permute-done.x_ref.near_ref = bf16[2,576,128]{2,1,0:T(8,128)(2,1)S(1)} collective-permute-done((bf16[2,576,128]{2,1,0:T(8,128)(2,1)}, bf16[2,576,128]{2,1,0:T(8,128)(2,1)S(1)}, u32[]{:S(2)}, u32[]{:S(2)}) %collective-permute-start) | collective-permute-done | bytes 294944 | tf_op jit(solution)/shard_map/ppermute | solution.py:292
  10.2 0.1 pack_near.1
  10.3 1.9 %collective-permute-start.5 = (bf16[2,192,128]{2,1,0:T(8,128)(2,1)S(1)}, bf16[2,192,128]{2,1,0:T(8,128)(2,1)S(1)}, u32[]{:S(2)}, u32[]{:S(2)}) collective-permute-start(bf16[2,192,128]{2,1,0:T(8,128)(2,1)S(1)} %get-tuple-element.35), channel_id=1, source_target_pairs={{0,8},{4,0},{8,16},{12,4},{16,24},{20,12},{24,28},{28,20},{1,9},{5... | collective-permute-start | bytes 294920 | tf_op jit(solution)/shard_map/ppermute | solution.py:292
  12.2 0.0 collective-permute-start.3
  12.2 1.6 %collective-permute-start.4 = (bf16[96,128]{1,0:T(8,128)(2,1)S(1)}, bf16[96,128]{1,0:T(8,128)(2,1)S(1)}, u32[]{:S(2)}, u32[]{:S(2)}) collective-permute-start(bf16[96,128]{1,0:T(8,128)(2,1)S(1)} %get-tuple-element.34), channel_id=1, source_target_pairs={{0,3},{1,2},{2,1},{3,0},{4,7},{5,6},{6,5},{7,4},{8,11},{9,10},{10,... | collective-permute-start | bytes 73736 | tf_op jit(solution)/shard_map/ppermute | solution.py:292
  13.8 0.7 %own.1.s_ref = f32[576,256]{1,0:T(8,128)S(1)} custom-call(bf16[12,256,128]{2,1,0:T(8,128)(2,1)S(1)} %get-tuple-element.36.table_ref, bf16[2,576,128]{2,1,0:T(8,128)(2,1)S(1)} %get-tuple-element.31.g_ref, bf16[96,128]{1,0:T(8,128)(2,1)S(1)} %get-tuple-element.37.rim_ref, bf16[12,48,640]{2,1,0:T(8,128)(2,1)S(1)} %get-tuple-element.38.wo_ref), custom_call_target="tpu_custom_call" | custom-call | tf_op jit(solution)/shard_map/own/pallas_call | solution.py:337
  14.5 0.0 collective-permute-done.6.fj_ref
  14.5 0.0 collective-permute-done.3.pair_ref
  14.5 0.9 %collective-permute-done.4.cross_ref = bf16[96,128]{1,0:T(8,128)(2,1)S(1)} collective-permute-done((bf16[96,128]{1,0:T(8,128)(2,1)S(1)}, bf16[96,128]{1,0:T(8,128)(2,1)S(1)}, u32[]{:S(2)}, u32[]{:S(2)}) %collective-permute-start.4) | collective-permute-done | bytes 24608 | tf_op jit(solution)/shard_map/ppermute | solution.py:292
  15.4 0.0 collective-permute-done.5.ff_ref
  15.4 3.1 %green_update.1 = bf16[2,12,48,128]{3,2,1,0:T(8,128)(2,1)} custom-call(bf16[2,576,128]{2,1,0:T(8,128)(2,1)S(1)} %collective-permute-done.x_ref.near_ref, bf16[96,128]{1,0:T(8,128)(2,1)S(1)} %collective-permute-done.3.pair_ref, bf16[96,128]{1,0:T(8,128)(2,1)S(1)} %collective-permute-done.4.cross_ref, bf16[2,192,128]{2,1,0:T(8,128)(2,1)S(1)} %collective-permute-done.5.ff_ref, ...), custom_call_target="tpu_custom_call" | custom-call | tf_op jit(solution)/shard_map/green_update/pallas_call | solution.py:379
  (1 shorter events, 0.0 us)
Async XLA Ops:
  0.0 10.2 %collective-permute-start = (bf16[2,576,128]{2,1,0:T(8,128)(2,1)}, bf16[2,576,128]{2,1,0:T(8,128)(2,1)S(1)}, u32[]{:S(2)}, u32[]{:S(2)}) collective-permute-start(bf16[2,576,128]{2,1,0:T(8,128)(2,1)} %bitcast.8), channel_id=1, source_target_pairs={{0,4},{4,0},{8,12},{12,8},{16,20},{20,16},{24,28},{28,24},{1,5},{5... | collective-permute-start | bytes 884744 | tf_op jit(solution)/shard_map/ppermute | solution.py:292
  4.2 4.1 %collective-permute-start.1 = (bf16[96,128]{1,0:T(8,128)(2,1)S(1)}, bf16[96,128]{1,0:T(8,128)(2,1)S(1)}, u32[]{:S(2)}, u32[]{:S(2)}) collective-permute-start(bf16[96,128]{1,0:T(8,128)(2,1)S(1)} %get-tuple-element.30), channel_id=1, source_target_pairs={{0,1},{1,0},{2,3},{3,2},{4,5},{5,4},{6,7},{7,6},{8,9},{9,8},{10,11... | collective-permute-start | bytes 73736 | tf_op jit(solution)/shard_map/ppermute | solution.py:292
  4.3 4.0 %collective-permute-start.2 = (bf16[96,128]{1,0:T(8,128)(2,1)S(1)}, bf16[96,128]{1,0:T(8,128)(2,1)S(1)}, u32[]{:S(2)}, u32[]{:S(2)}) collective-permute-start(bf16[96,128]{1,0:T(8,128)(2,1)S(1)} %get-tuple-element.30), channel_id=1, source_target_pairs={{0,3},{1,2},{2,1},{3,0},{4,7},{5,6},{6,5},{7,4},{8,11},{9,10},{10,... | collective-permute-start | bytes 73736 | tf_op jit(solution)/shard_map/ppermute | solution.py:292
  8.3 6.2 %collective-permute-start.6 = (bf16[864,128]{1,0:T(8,128)(2,1)S(1)}, bf16[864,128]{1,0:T(8,128)(2,1)S(1)}, u32[]{:S(2)}, u32[]{:S(2)}) collective-permute-start(bf16[864,128]{1,0:T(8,128)(2,1)S(1)} %get-tuple-element.33.after_ref), channel_id=1, source_target_pairs={{0,1},{1,0},{2,3},{3,2},{4,8},{5,9},{6,10},{7,11},{8,4},{9,5},{10,... | collective-permute-start | bytes 663560 | tf_op jit(solution)/shard_map/ppermute | solution.py:317
  10.3 5.1 %collective-permute-start.5 = (bf16[2,192,128]{2,1,0:T(8,128)(2,1)S(1)}, bf16[2,192,128]{2,1,0:T(8,128)(2,1)S(1)}, u32[]{:S(2)}, u32[]{:S(2)}) collective-permute-start(bf16[2,192,128]{2,1,0:T(8,128)(2,1)S(1)} %get-tuple-element.35), channel_id=1, source_target_pairs={{0,8},{4,0},{8,16},{12,4},{16,24},{20,12},{24,28},{28,20},{1,9},{5... | collective-permute-start | bytes 294920 | tf_op jit(solution)/shard_map/ppermute | solution.py:292
  12.2 2.3 %collective-permute-start.3 = (bf16[96,128]{1,0:T(8,128)(2,1)S(1)}, bf16[96,128]{1,0:T(8,128)(2,1)S(1)}, u32[]{:S(2)}, u32[]{:S(2)}) collective-permute-start(bf16[96,128]{1,0:T(8,128)(2,1)S(1)} %get-tuple-element.34), channel_id=1, source_target_pairs={{0,1},{1,0},{2,3},{3,2},{4,5},{5,4},{6,7},{7,6},{8,9},{9,8},{10,11... | collective-permute-start | bytes 73736 | tf_op jit(solution)/shard_map/ppermute | solution.py:292
  12.2 3.3 %collective-permute-start.4 = (bf16[96,128]{1,0:T(8,128)(2,1)S(1)}, bf16[96,128]{1,0:T(8,128)(2,1)S(1)}, u32[]{:S(2)}, u32[]{:S(2)}) collective-permute-start(bf16[96,128]{1,0:T(8,128)(2,1)S(1)} %get-tuple-element.34), channel_id=1, source_target_pairs={{0,3},{1,2},{2,1},{3,0},{4,7},{5,6},{6,5},{7,4},{8,11},{9,10},{10,... | collective-permute-start | bytes 73736 | tf_op jit(solution)/shard_map/ppermute | solution.py:292

commit v10 on v9

--- a/solution.py
+++ b/solution.py
@@ -74,9 +74,8 @@
     rim_ref[...] = halo
 
 
-def pass_kernel(orb, x_ref, after_ref, out_ref, edge_ref):
+def pass_kernel(x_ref, after_ref, out_ref):
     out_ref[...] = x_ref[:, :out_ref.shape[1]]
-    pack_edges(orb, x_ref, edge_ref)
 
 
 def band_weights(sh_ref, st_ref, oc_ref):
@@ -369,9 +368,8 @@
         move(edge, "energy", pair), move(edge, "energy", cross), held, w_near)
     far_join = move_far(join)
     w_far = call(far_kernel, "far_weights", weight, left, right, join)
-    passed, near_edge = call(
-        functools.partial(pass_kernel, orb), "pack_near",
-        [shape(2, early * span, energies), shape(2 * span, LANES)], near, w_far)
+    passed = call(pass_kernel, "pass", shape(2, early * span, energies), near, w_far)
+    near_edge = call(functools.partial(pack_edges, orb), "pack_near", shape(2 * span, LANES), near)
     far_first = move(passed, "atom", lambda i: relay(i, lax.axis_size("atom")))
     own = call(
         functools.partial(own_kernel, orb), "own", shape(rows, 2 * energies, kind=F32), table, held, rim, w_own)

time: 18.8 us -> 18.9 us (level)
    pallas_call x6 -> x7, Pallas kernels: 3.92 us -> 3.93 us  [call(): pl.pallas_call(kernel, out_shape=out_shape, name=name, in_specs=[smem if...]
where the time goes in v10:
time: 18.9 us; the launch traced here: 18.7 us
  starting transfers between devices  8.36 us (44%)
  Pallas kernels  8.29 us (44%)
  waiting for transfers between devices  1.98 us (10%)
    ppermute x6, starting transfers between devices, move(): lax.ppermute(value, axis, [(i, target(i) % count) for i in range(count)])  8.23 us
    pallas_call x7, Pallas kernels, call(): pl.pallas_call(kernel, out_shape=out_shape, name=name, in_specs=[smem if...  3.93 us
    pallas_call x1, Pallas kernels, per_device(): pl.pallas_call(functools.partial(final_kernel, orb, atoms), name='green_u...  3.14 us
    ppermute x6, waiting for transfers between devices, move(): lax.ppermute(value, axis, [(i, target(i) % count) for i in range(count)])  1.97 us
    pallas_call x1, Pallas kernels, per_device(): pl.pallas_call(functools.partial(pack_kernel, orb), name='pack', out_shap...  1.23 us
  transfers between devices with their start and end apart: 7, of which 2 were waited for; matrix products, arithmetic and copies ran while one was open for 0% of the time, Pallas kernels for 28%

profile of v10, /device:TPU:0, one launch (start us, length us, event | category | flops | bytes accessed | tf_op | source)
XLA Modules:
  0.0 18.7 jit_solution(9231530484397228818)
XLA Ops:
  0.0 2.9 %collective-permute-start = (bf16[2,576,128]{2,1,0:T(8,128)(2,1)}, bf16[2,576,128]{2,1,0:T(8,128)(2,1)S(1)}, u32[]{:S(2)}, u32[]{:S(2)}) collective-permute-start(bf16[2,576,128]{2,1,0:T(8,128)(2,1)} %bitcast.8), channel_id=1, source_target_pairs={{0,4},{4,0},{8,12},{12,8},{16,20},{20,16},{24,28},{28,24},{1,5},{5... | collective-permute-start | bytes 884744 | tf_op jit(solution)/shard_map/ppermute | solution.py:291
  2.9 1.2 %pack.1 = (bf16[96,128]{1,0:T(8,128)(2,1)S(1)}, bf16[2,576,128]{2,1,0:T(8,128)(2,1)S(1)}, bf16[384,12]{1,0:T(8,128)(2,1)S(1)}, s32[8,16,128]{2,1,0:T(8,128)S(1)}...) custom-call(bf16[2,576,128]{2,1,0:T(8,128)(2,1)} %bitcast.9, bf16[384,12]{1,0:T(8,128)(2,1)} %bitcast.10, ...), custom_call_target="tpu_custom_call" | custom-call | tf_op jit(solution)/shard_map/pack/pallas_call | solution.py:348
  4.2 0.1 collective-permute-start.3
  4.3 1.6 %collective-permute-start.4 = (bf16[96,128]{1,0:T(8,128)(2,1)S(1)}, bf16[96,128]{1,0:T(8,128)(2,1)S(1)}, u32[]{:S(2)}, u32[]{:S(2)}) collective-permute-start(bf16[96,128]{1,0:T(8,128)(2,1)S(1)} %get-tuple-element.28), channel_id=1, source_target_pairs={{0,3},{1,2},{2,1},{3,0},{4,7},{5,6},{6,5},{7,4},{8,11},{9,10},{10,... | collective-permute-start | bytes 73736 | tf_op jit(solution)/shard_map/ppermute | solution.py:291
  5.9 0.6 %factors.1 = (bf16[8,12,16,640]{3,2,1,0:T(8,128)(2,1)S(1)}, bf16[3,8,3,16,384]{4,3,2,1,0:T(8,128)(2,1)S(1)}, bf16[12,256,128]{2,1,0:T(8,128)(2,1)S(1)}) custom-call(bf16[384,12]{1,0:T(8,128)(2,1)S(1)} %get-tuple-element.21.c_ref, s32[8,16,128]{2,1,0:T(8,128)S(1)} %get-tuple-element.22.near_ref, s32[1,32]{1,0:T(1,128)S(1)} %get-tuple-element.23.sh_ref, ...), custom_call_target="tpu_custom_call" | custom-call | tf_op jit(solution)/shard_map/factors/pallas_call | solution.py:336
  6.5 1.7 %weights.1 = (bf16[12,48,640]{2,1,0:T(8,128)(2,1)S(1)}, bf16[12,48,640]{2,1,0:T(8,128)(2,1)S(1)}, f32[3,12,6,8,128]{4,3,2,1,0:T(8,128)S(1)}, f32[3,12,12,8,128]{4,3,2,1,0:T(8,128)S(1)}) custom-call(bf16[8,12,16,640]{3,2,1,0:T(8,128)(2,1)S(1)} %get-tuple-element.26.t1_ref, bf16[3,8,3,16,384]{4,3,2,1,0:T(8,128)(2,1)S(1)} %get-tuple-element.27.t2_ref, ...), custom_call_target="tpu_custom_call" | custom-call | tf_op jit(solution)/shard_map/weights/pallas_call | solution.py:336
  8.2 0.0 collective-permute-done.3.pair_ref
  8.2 0.0 collective-permute-done.4.cross_ref
  8.3 0.1 collective-permute-start.6
  8.4 0.8 %far_weights.1.after_ref.wf_ref = bf16[12,48,640]{2,1,0:T(8,128)(2,1)S(1)} custom-call(bf16[8,12,16,640]{3,2,1,0:T(8,128)(2,1)S(1)} %get-tuple-element.26.t1_ref, bf16[3,8,3,16,384]{4,3,2,1,0:T(8,128)(2,1)S(1)} %get-tuple-element.27.t2_ref, bf16[864,128]{1,0:T(8,128)(2,1)S(1)} %get-tuple-element.31.after_ref), custom_call_target="tpu_custom_call" | custom-call | tf_op jit(solution)/shard_map/far_weights/pallas_call | solution.py:336
  9.2 1.0 %collective-permute-done.g_ref.x_ref.near_ref = bf16[2,576,128]{2,1,0:T(8,128)(2,1)S(1)} collective-permute-done((bf16[2,576,128]{2,1,0:T(8,128)(2,1)}, bf16[2,576,128]{2,1,0:T(8,128)(2,1)S(1)}, u32[]{:S(2)}, u32[]{:S(2)}) %collective-permute-start) | collective-permute-done | bytes 294944 | tf_op jit(solution)/shard_map/ppermute | solution.py:291
  10.2 1.9 %collective-permute-start.5 = (bf16[2,192,128]{2,1,0:T(8,128)(2,1)S(1)}, bf16[2,192,128]{2,1,0:T(8,128)(2,1)S(1)}, u32[]{:S(2)}, u32[]{:S(2)}) collective-permute-start(bf16[2,192,128]{2,1,0:T(8,128)(2,1)S(1)} %pass.1), channel_id=1, source_target_pairs={{0,8},{4,0},{8,16},{12,4},{16,24},{20,12},{24,28},{28,20},{1,9},{5... | collective-permute-start | bytes 294920 | tf_op jit(solution)/shard_map/ppermute | solution.py:291
  12.0 0.1 pack_near.1
  12.2 0.1 collective-permute-start.1
  12.3 1.6 %collective-permute-start.2 = (bf16[96,128]{1,0:T(8,128)(2,1)S(1)}, bf16[96,128]{1,0:T(8,128)(2,1)S(1)}, u32[]{:S(2)}, u32[]{:S(2)}) collective-permute-start(bf16[96,128]{1,0:T(8,128)(2,1)S(1)} %pack_near.1), channel_id=1, source_target_pairs={{0,3},{1,2},{2,1},{3,0},{4,7},{5,6},{6,5},{7,4},{8,11},{9,10},{10,... | collective-permute-start | bytes 73736 | tf_op jit(solution)/shard_map/ppermute | solution.py:291
  13.9 0.7 %own.1.s_ref = f32[576,256]{1,0:T(8,128)S(1)} custom-call(bf16[12,256,128]{2,1,0:T(8,128)(2,1)S(1)} %get-tuple-element.32.table_ref, bf16[2,576,128]{2,1,0:T(8,128)(2,1)S(1)} %get-tuple-element.29.g_ref, bf16[96,128]{1,0:T(8,128)(2,1)S(1)} %get-tuple-element.33.rim_ref, bf16[12,48,640]{2,1,0:T(8,128)(2,1)S(1)} %get-tuple-element.34.wo_ref), custom_call_target="tpu_custom_call" | custom-call | tf_op jit(solution)/shard_map/own/pallas_call | solution.py:336
  14.6 0.0 collective-permute-done.6.fj_ref
  14.6 0.0 collective-permute-done.1.pair_ref
  14.6 1.0 %collective-permute-done.2.cross_ref = bf16[96,128]{1,0:T(8,128)(2,1)S(1)} collective-permute-done((bf16[96,128]{1,0:T(8,128)(2,1)S(1)}, bf16[96,128]{1,0:T(8,128)(2,1)S(1)}, u32[]{:S(2)}, u32[]{:S(2)}) %collective-permute-start.2) | collective-permute-done | bytes 24608 | tf_op jit(solution)/shard_map/ppermute | solution.py:291
  15.6 0.0 collective-permute-done.5.ff_ref
  15.6 3.1 %green_update.1 = bf16[2,12,48,128]{3,2,1,0:T(8,128)(2,1)} custom-call(bf16[2,576,128]{2,1,0:T(8,128)(2,1)S(1)} %collective-permute-done.g_ref.x_ref.near_ref, bf16[96,128]{1,0:T(8,128)(2,1)S(1)} %collective-permute-done.1.pair_ref, bf16[96,128]{1,0:T(8,128)(2,1)S(1)} %collective-permute-done.2.cross_ref, ...), custom_call_target="tpu_custom_call" | custom-call | tf_op jit(solution)/shard_map/green_update/pallas_call | solution.py:377
  (2 shorter events, 0.0 us)
Async XLA Ops:
  0.0 10.2 %collective-permute-start = (bf16[2,576,128]{2,1,0:T(8,128)(2,1)}, bf16[2,576,128]{2,1,0:T(8,128)(2,1)S(1)}, u32[]{:S(2)}, u32[]{:S(2)}) collective-permute-start(bf16[2,576,128]{2,1,0:T(8,128)(2,1)} %bitcast.8), channel_id=1, source_target_pairs={{0,4},{4,0},{8,12},{12,8},{16,20},{20,16},{24,28},{28,24},{1,5},{5... | collective-permute-start | bytes 884744 | tf_op jit(solution)/shard_map/ppermute | solution.py:291
  4.2 4.1 %collective-permute-start.3 = (bf16[96,128]{1,0:T(8,128)(2,1)S(1)}, bf16[96,128]{1,0:T(8,128)(2,1)S(1)}, u32[]{:S(2)}, u32[]{:S(2)}) collective-permute-start(bf16[96,128]{1,0:T(8,128)(2,1)S(1)} %get-tuple-element.28), channel_id=1, source_target_pairs={{0,1},{1,0},{2,3},{3,2},{4,5},{5,4},{6,7},{7,6},{8,9},{9,8},{10,11... | collective-permute-start | bytes 73736 | tf_op jit(solution)/shard_map/ppermute | solution.py:291
  4.3 4.0 %collective-permute-start.4 = (bf16[96,128]{1,0:T(8,128)(2,1)S(1)}, bf16[96,128]{1,0:T(8,128)(2,1)S(1)}, u32[]{:S(2)}, u32[]{:S(2)}) collective-permute-start(bf16[96,128]{1,0:T(8,128)(2,1)S(1)} %get-tuple-element.28), channel_id=1, source_target_pairs={{0,3},{1,2},{2,1},{3,0},{4,7},{5,6},{6,5},{7,4},{8,11},{9,10},{10,... | collective-permute-start | bytes 73736 | tf_op jit(solution)/shard_map/ppermute | solution.py:291
  8.3 6.3 %collective-permute-start.6 = (bf16[864,128]{1,0:T(8,128)(2,1)S(1)}, bf16[864,128]{1,0:T(8,128)(2,1)S(1)}, u32[]{:S(2)}, u32[]{:S(2)}) collective-permute-start(bf16[864,128]{1,0:T(8,128)(2,1)S(1)} %get-tuple-element.31.after_ref), channel_id=1, source_target_pairs={{0,1},{1,0},{2,3},{3,2},{4,8},{5,9},{6,10},{7,11},{8,4},{9,5},{10,... | collective-permute-start | bytes 663560 | tf_op jit(solution)/shard_map/ppermute | solution.py:316
  10.2 5.4 %collective-permute-start.5 = (bf16[2,192,128]{2,1,0:T(8,128)(2,1)S(1)}, bf16[2,192,128]{2,1,0:T(8,128)(2,1)S(1)}, u32[]{:S(2)}, u32[]{:S(2)}) collective-permute-start(bf16[2,192,128]{2,1,0:T(8,128)(2,1)S(1)} %pass.1), channel_id=1, source_target_pairs={{0,8},{4,0},{8,16},{12,4},{16,24},{20,12},{24,28},{28,20},{1,9},{5... | collective-permute-start | bytes 294920 | tf_op jit(solution)/shard_map/ppermute | solution.py:291
  12.2 2.4 %collective-permute-start.1 = (bf16[96,128]{1,0:T(8,128)(2,1)S(1)}, bf16[96,128]{1,0:T(8,128)(2,1)S(1)}, u32[]{:S(2)}, u32[]{:S(2)}) collective-permute-start(bf16[96,128]{1,0:T(8,128)(2,1)S(1)} %pack_near.1), channel_id=1, source_target_pairs={{0,1},{1,0},{2,3},{3,2},{4,5},{5,4},{6,7},{7,6},{8,9},{9,8},{10,11... | collective-permute-start | bytes 73736 | tf_op jit(solution)/shard_map/ppermute | solution.py:291
  12.3 3.3 %collective-permute-start.2 = (bf16[96,128]{1,0:T(8,128)(2,1)S(1)}, bf16[96,128]{1,0:T(8,128)(2,1)S(1)}, u32[]{:S(2)}, u32[]{:S(2)}) collective-permute-start(bf16[96,128]{1,0:T(8,128)(2,1)S(1)} %pack_near.1), channel_id=1, source_target_pairs={{0,3},{1,2},{2,1},{3,0},{4,7},{5,6},{6,5},{7,4},{8,11},{9,10},{10,... | collective-permute-start | bytes 73736 | tf_op jit(solution)/shard_map/ppermute | solution.py:291
